TPU v7x, 32 devices: a whole 2x2x4 slice. The times are simulated.
32 devices in a mesh: dp: 16 (over z, y, x), mp: 2 (over core).
Axes of the slice: x: 2, y: 2, z: 4, core: 2. Of those that a mesh axis runs over, the one named last changes fastest.
Arguments:
- tokens: bfloat16 [2, 16, 512, 768], P(None, 'dp'), may hold values from -6 to 6
- pair_lengths: int32 [2, 16], P(None, 'dp'), may hold values from 128 to 512, as said below
- query_ids: int32 [2, 16], replicated, may hold values from 0 to 3, as said below
- distance_bucket: int32 [1023], replicated, may hold values from 0 to 31, as said below
- step_count: int32 [], replicated, may hold values from 1 to 20
- heads_in: float32 [768, 3, 768], P('dp', None, 'mp'), may hold values from -0.21650635 to 0.21650635
- heads_out: float32 [768, 768], P('dp', 'mp'), may hold values from -0.875 to 0.875
- hidden_in: float32 [768, 3072], P('dp', 'mp'), may hold values from -0.21875 to 0.21875
- hidden_out: float32 [768, 3072], P('dp', 'mp'), may hold values from -0.15625 to 0.15625
- gains: float32 [768, 3], P('dp'), may hold values from 0.3 to 2.5
- tied_rows: float32 [768, 2], P('dp'), may hold values from -6 to 6
- bias_table: float32 [32, 12], P(None, 'mp'), may hold values from -6 to 6
- first_heads_in: float32 [768, 3, 768], P('dp', None, 'mp'), may hold values from -5.722046e-06 to 5.722046e-06
- first_heads_out: float32 [768, 768], P('dp', 'mp'), may hold values from -5.722046e-06 to 5.722046e-06
- first_hidden_in: float32 [768, 3072], P('dp', 'mp'), may hold values from -5.722046e-06 to 5.722046e-06
- first_hidden_out: float32 [768, 3072], P('dp', 'mp'), may hold values from -5.722046e-06 to 5.722046e-06
- first_gains: float32 [768, 3], P('dp'), may hold values from -5.722046e-06 to 5.722046e-06
- first_tied: float32 [768, 2], P('dp'), may hold values from -5.722046e-06 to 5.722046e-06
- first_table: float32 [32, 12], P(None, 'mp'), may hold values from -5.722046e-06 to 5.722046e-06
- second_heads_in: float32 [768, 3, 768], P('dp', None, 'mp'), may hold values from 7.060041e-15 to 5.6480326e-14
- second_heads_out: float32 [768, 768], P('dp', 'mp'), may hold values from 7.060041e-15 to 5.6480326e-14
- second_hidden_in: float32 [768, 3072], P('dp', 'mp'), may hold values from 7.060041e-15 to 5.6480326e-14
- second_hidden_out: float32 [768, 3072], P('dp', 'mp'), may hold values from 7.060041e-15 to 5.6480326e-14
- second_gains: float32 [768, 3], P('dp'), may hold values from 7.060041e-15 to 5.6480326e-14
- second_tied: float32 [768, 2], P('dp'), may hold values from 7.060041e-15 to 5.6480326e-14
- second_table: float32 [32, 12], P(None, 'mp'), may hold values from 7.060041e-15 to 5.6480326e-14
Outputs:
- gradient_norm: float32 [], replicated
- token_gradient: float32 [2, 16, 512, 768], P(None, 'dp')
- next_heads_in: float32 [768, 3, 768], P('dp', None, 'mp')
- next_heads_out: float32 [768, 768], P('dp', 'mp')
- next_hidden_in: float32 [768, 3072], P('dp', 'mp')
- next_hidden_out: float32 [768, 3072], P('dp', 'mp')
- next_gains: float32 [768, 3], P('dp')
- next_tied: float32 [768, 2], P('dp')
- next_table: float32 [32, 12], P(None, 'mp')
- next_first_heads_in: float32 [768, 3, 768], P('dp', None, 'mp')
- next_first_heads_out: float32 [768, 768], P('dp', 'mp')
- next_first_hidden_in: float32 [768, 3072], P('dp', 'mp')
- next_first_hidden_out: float32 [768, 3072], P('dp', 'mp')
- next_first_gains: float32 [768, 3], P('dp')
- next_first_tied: float32 [768, 2], P('dp')
- next_first_table: float32 [32, 12], P(None, 'mp')
- next_second_heads_in: float32 [768, 3, 768], P('dp', None, 'mp')
- next_second_heads_out: float32 [768, 768], P('dp', 'mp')
- next_second_hidden_in: float32 [768, 3072], P('dp', 'mp')
- next_second_hidden_out: float32 [768, 3072], P('dp', 'mp')
- next_second_gains: float32 [768, 3], P('dp')
- next_second_tied: float32 [768, 2], P('dp')
- next_second_table: float32 [32, 12], P(None, 'mp')
Inputs may be any that keep to these rules, and one draw needn't show every extreme that they name: `pair_lengths`: pair 0 of each micro-batch uses all 512 positions of its slot. `query_ids`: every id names at least one pair of each micro-batch. `distance_bucket`: entry r + 511 is the bucket of key minus query r: buckets 16 to 31 are for r > 0, 0 to 15 for r <= 0; a magnitude below 8 is its own bucket (plus 16 for r > 0); larger magnitudes take buckets 8 to 15 (plus 16) that never fall as the magnitude grows, and the largest magnitude takes 15 (plus 16).
All inputs are finite; a program needn't handle non-finite values.
Results may differ from a plain program's by a relative error of at most 0.014.
Values may be sent and summed in bfloat16 or wider, within the bound.
No kernel may reach another device: no remote copies, remote signals or barrier semaphores. Data moves between devices by JAX's collectives and lax.ppermute only.
A program may use at most 320 MiB of HBM per device.

v0:
```python
import functools

import jax
import jax.numpy as jnp
from jax import lax
from jax.experimental import pallas as pl
from jax.experimental.pallas import tpu as pltpu
from jax.sharding import PartitionSpec as P

BUCKETS = 32
LOSS_SCALE = 1024
LANES = 128
ROWS = 256
SPAN = 512

norm_eps = 1e-06
clip_limit = 0.01
beta_first = 0.9
beta_second = 0.999
adam_eps = 1e-08
rate_matrix = 0.03
rate_vector = 0.25
decay_matrix = 0.1
masked_score = -1e30
gelu_slope = 0.7978845608028654
gelu_cubic = 0.044715
low_type = jnp.bfloat16
full_type = jnp.float32
core_swap = [(0, 1), (1, 0)]


def rms_scale(rows_in):
    return lax.rsqrt(jnp.mean(rows_in * rows_in, axis=-1, keepdims=True) + norm_eps)


def norm_input_grad(d_normed, gain_row, rows_in, norm_scale):
    weighted = d_normed * gain_row
    return norm_scale * weighted - rows_in * norm_scale**3 * jnp.mean(
        weighted * rows_in, axis=-1, keepdims=True
    )


def dot_nt(left, right):
    return lax.dot_general(left, right, (((1,), (1,)), ((), ())), preferred_element_type=full_type)


def dot_tn(left, right):
    return lax.dot_general(left, right, (((0,), (0,)), ((), ())), preferred_element_type=full_type)


def dot_nn(left, right):
    return lax.dot_general(left, right, (((1,), (0,)), ((), ())), preferred_element_type=full_type)


def call(
    kernel, name, out_shape, cost=(0, 0), vmem=16, deps=(), passing=(), in_specs=None,
    out_specs=None, input_output_aliases=None, **options
):
    single = not isinstance(out_shape, (list, tuple))
    out_shapes = [out_shape] if single else list(out_shape)
    outputs, extra = len(out_shapes), len(deps) + len(passing)

    def apply(*operands):
        inputs = len(operands)
        if in_specs is None:
            options["grid"] = (1,)
        specs = [whole(operand.shape) for operand in operands] if in_specs is None else in_specs
        targets = out_specs or [whole(shape.shape) for shape in out_shapes]
        targets = targets if isinstance(targets, (list, tuple)) else [targets]
        aliases = dict(input_output_aliases or {})
        for i in range(len(passing)):
            aliases[inputs + len(deps) + i] = outputs + i

        def run(*refs):
            own = inputs + extra
            kernel(*refs[:inputs], *refs[own : own + outputs], *refs[own + outputs + len(passing) :])

        results = pl.pallas_call(
            run,
            out_shape=[*out_shapes, *(shape_of(a.shape, a.dtype) for a in passing)],
            in_specs=[*specs, *[in_place()] * extra],
            out_specs=[*targets, *[in_place()] * len(passing)],
            input_output_aliases=aliases,
            compiler_params=pltpu.CompilerParams(vmem_limit_bytes=vmem * 1024 * 1024),
            cost_estimate=pl.CostEstimate(
                flops=int(cost[0] * 2e6), bytes_accessed=int(cost[1] * 1e3), transcendentals=0
            ),
            name=name,
            **options,
        )(*operands, *deps, *passing)
        return results[0] if single and not passing else results

    return apply


def in_place():
    return pl.BlockSpec(memory_space=pl.ANY)


def shape_of(shape, dtype):
    return jax.ShapeDtypeStruct(tuple(shape), dtype)


def whole(shape):
    return pl.BlockSpec(tuple(shape), lambda *_: (0,) * len(shape))


def on_scalars():
    return pl.BlockSpec(memory_space=pltpu.SMEM)


def row_blocks(shape, step=0):
    return pl.BlockSpec(tuple(shape), lambda i: (i,) + (0,) * (len(shape) - 1))


def column_blocks(shape, offset=0):
    return pl.BlockSpec(tuple(shape), lambda i: (0,) * (len(shape) - 1) + (i + offset,))


def fill_rows(target, pieces, columns=slice(None)):
    start = 0
    for piece in pieces:
        rows = piece.shape[0]
        target[start : start + rows, :] = piece[:, columns]
        start += rows


def spill_rows(value, pieces, first=0):
    start = 0
    for piece in pieces:
        rows = piece.shape[0]
        low, high = max(start, first), min(start + rows, first + value.shape[0])
        if low < high:
            piece[low - start : high - start] = value[low - first : high - first].astype(piece.dtype)
        start += rows


def swap(array, mask, size, label="exchange"):
    with jax.named_scope(f"{label}_across_{mask}"):
        return lax.ppermute(array, "dp", [(i, i ^ mask) for i in range(size)])


def tie(arrays, deps):
    return call(lambda: None, "tie", [], deps=deps, passing=arrays, in_specs=[], grid=(1,))()


def other_core(array, label="other_core"):
    with jax.named_scope(label):
        return lax.ppermute(array, "mp", core_swap)


def stage_bits(size):
    if size == 16:
        return (8, 4, 2, 1)
    return tuple(1 << i for i in range(size.bit_length() - 1))


def device_of(place, me, size):
    mask = jnp.zeros_like(place)
    for i, bit in enumerate(stage_bits(size)):
        mask = mask + jnp.bitwise_and(place >> i, 1) * bit
    return jnp.bitwise_xor(mask, me)


def piece_rows(size, width):
    if size != 16:
        return [width]
    return [width // 4] * 3 + [width // 8] * 2


def join_kernel(*refs):
    *part_refs, out_ref = refs
    start = 0
    for part in part_refs:
        rows = part.shape[0]
        out_ref[start : start + rows] = part[...]
        start += rows


def join(parts, **options):
    rows = sum(part.shape[0] for part in parts)
    return call(
        join_kernel, "join", shape_of((rows, *parts[0].shape[1:]), parts[0].dtype), **options
    )(*parts)


def step_kernel(groups, y_ref, x_ref, *refs):
    part_refs, (low_ref, high_ref, *joined_refs) = refs[: sum(groups)], refs[sum(groups) :]
    low_ref[...] = y_ref[...]
    high_ref[...] = x_ref[...]
    for group, joined_ref in zip(groups, joined_refs):
        join_kernel(*part_refs[:group], joined_ref)
        part_refs = part_refs[group:]


def gather_step(across_y, across_x, *groups, **options):
    half = (across_y.shape[0] // 2, across_y.shape[1])
    shapes = [shape_of(half, across_y.dtype)] * 2
    for parts in groups:
        shapes.append(shape_of((sum(p.shape[0] for p in parts), parts[0].shape[1]), parts[0].dtype))
    flat = [part for parts in groups for part in parts]
    return call(
        functools.partial(step_kernel, tuple(len(parts) for parts in groups)),
        "gather_step",
        shapes,
        grid=(1,),
        in_specs=[
            pl.BlockSpec(half, lambda i: (0, 0)),
            pl.BlockSpec(half, lambda i: (1, 0)),
            *(whole(part.shape) for part in flat),
        ],
        out_specs=[whole(shape.shape) for shape in shapes],
        **options,
    )(across_y, across_x, *flat)


def line_parts(part, size, label):
    return [part] + [swap(part, mask, size, label) for mask in (8, 4, 12)]


def side_parts(quarter, size, label):
    return [swap(quarter, mask, size, label) for mask in (2, 1)]


def corner_parts(low, high, size, label):
    return [swap(low, 1, size, label), swap(high, 2, size, label)]


def gather_doubling(part, size):
    for bit in stage_bits(size):
        part = jnp.concatenate([part, swap(part, bit, size)], axis=0)
    return part


def small_line(part, size, label):
    if size != 16:
        return part[None]
    return join(line_parts(part[None], size, label))


def small_plane(quarter, size, label):
    if size != 16:
        return [gather_doubling(quarter, size)]
    return [quarter] + [swap(quarter, mask, size, label) for mask in (2, 1, 3)]


def stacked(refs):
    return jnp.concatenate([ref[...] for ref in refs], axis=0)


def stacked_row(refs, row):
    return jnp.concatenate([ref[:, row, :] for ref in refs], axis=0)


def gather_small(part, size, label):
    return small_plane(small_line(part, size, label), size, label)


def plane_sum_kernel(*refs):
    count = len(refs) // 6
    for i in range(count):
        y_ref, x_ref, low_ref, high_ref = refs[4 * i : 4 * i + 4]
        y_out, x_out = refs[4 * count + 2 * i : 4 * count + 2 * i + 2]
        half = low_ref.shape[0]
        y_out[:half] = (y_ref[:half].astype(full_type) + low_ref[...].astype(full_type)).astype(
            low_type
        )
        y_out[half:] = y_ref[half:]
        x_out[:half] = x_ref[:half]
        x_out[half:] = (x_ref[half:].astype(full_type) + high_ref[...].astype(full_type)).astype(
            low_type
        )


def line_sum_kernel(*refs):
    count = sum(ref.shape[0] == refs[0].shape[0] for ref in refs)
    add_refs, out_refs = refs[:count], refs[count:]
    rows = out_refs[0].shape[0]
    for i, out_ref in enumerate(out_refs):
        span = slice(i * rows, (i + 1) * rows)
        total = add_refs[0][span].astype(full_type)
        for ref in add_refs[1:]:
            total = total + ref[span].astype(full_type)
        out_ref[...] = total.astype(out_ref.dtype)


class Scatter:
    def __init__(self, pieces, size, label):
        self.pieces, self.size, self.label = pieces, size, label
        self.sources, self.came = (), ()
        if size == 16:
            *self.pieces, low, high = pieces
            self.came = [swap(low, 1, size, label), swap(high, 2, size, label)]

    def near(self, deps=(), passing=()):
        if self.size != 16:
            return passing
        keep = self.pieces[0]
        half = (keep.shape[0] // 2, keep.shape[1])
        kept, sent, *passed = call(
            line_sum_kernel,
            "line_sum",
            [shape_of(half, full_type), shape_of(half, low_type)],
            deps=deps,
            passing=passing,
        )(keep, *self.came)
        self.sources, self.came, self.pieces = (sent,), [swap(sent, 4, self.size, self.label)], [kept]
        return passed

    def far(self, deps=()):
        if self.size != 16:
            return self.line(deps)[0]
        kept = self.pieces[0]
        half = (kept.shape[0] // 2, kept.shape[1])
        own, sent = call(
            line_sum_kernel,
            "line_sum",
            [shape_of(half, full_type), shape_of(half, low_type)],
            deps=deps,
        )(kept, *self.came)
        self.sources = (sent,)
        return [own, swap(sent, 8, self.size, self.label)]

    def line(self, deps=(), passing=()):
        size, label = self.size, self.label
        if size != 16:
            grad = self.pieces[0]
            for bit in reversed(stage_bits(size)):
                half = grad.shape[0] // 2
                came = swap(grad[half:], bit, size, label)
                grad = (grad[:half].astype(full_type) + came.astype(full_type)).astype(low_type)
            return [grad.astype(full_type)], passing
        keep = self.pieces[0]
        part = (keep.shape[0] // 4, keep.shape[1])
        own, *others = call(
            line_sum_kernel,
            "line_sum",
            [shape_of(part, full_type)] + [shape_of(part, low_type)] * 3,
            deps=deps,
            passing=passing,
        )(keep, *self.came)
        came = [swap(other, mask, size, label) for other, mask in zip(others, (8, 4, 12))]
        return [own] + came, others[3:]


def scatter_sides(scatters, deps=()):
    if scatters[0].size != 16:
        return ()
    sides = [part for scatter in scatters for part in scatter.pieces[1:]]
    operands = [part for s in scatters for part in (*s.pieces[1:], *s.came)]
    sums = call(
        plane_sum_kernel, "plane_sum", [shape_of(part.shape, low_type) for part in sides], deps=deps
    )(*operands)
    for i, scatter in enumerate(scatters):
        to_y, to_x = sums[2 * i : 2 * i + 2]
        scatter.came = [
            swap(to_y, 2, scatter.size, scatter.label), swap(to_x, 1, scatter.size, scatter.label)
        ]
    return tuple(sums)


def pack_heads_kernel(in_ref, out_ref, gain_ref, tied_ref, a_ref):
    parts, rows, width = in_ref.shape
    for c in range(parts):
        a_ref[:, c * width : (c + 1) * width] = in_ref[c].astype(low_type)
    a_ref[:, parts * width : (parts + 1) * width] = out_ref[...].astype(low_type)
    gains, tied = gain_ref[...], tied_ref[...]
    vectors = few_rows([gains[i : i + 1] for i in range(3)] + [tied[i : i + 1] for i in range(2)], 16)
    pick = lax.broadcasted_iota(jnp.int32, (16, LANES), 0) == lax.broadcasted_iota(
        jnp.int32, (16, LANES), 1
    )
    extra = dot_tn(vectors.astype(low_type), jnp.where(pick, 1.0, 0.0).astype(low_type))
    a_ref[:, (parts + 1) * width :] = extra.astype(low_type)


def pack_hidden_kernel(up_ref, down_ref, b_ref, c_ref):
    b_ref[...] = up_ref[...].astype(low_type)
    c_ref[...] = down_ref[...].astype(low_type)


def prepare_kernel(
    size, me_ref, line_ref, table_ref, query_ref, order_ref, bias_ref, hot_ref, same_ref, positive_ref
):
    me = me_ref[0]
    lane = lambda shape: lax.broadcasted_iota(jnp.int32, shape, 1)
    row = lambda shape: lax.broadcasted_iota(jnp.int32, shape, 0)
    low = lambda hit: jnp.where(hit, 1.0, 0.0).astype(low_type)
    width = order_ref.shape[0]
    own = width // size
    feature = lane((1, width))
    place = device_of(feature // own, me, size) * own + feature % own
    for start in range(0, width, LANES):
        order_ref[start : start + LANES] = low(row((LANES, width)) + start == place)
    length = line_ref.shape[1]
    hot = low(row((LANES, length)) == line_ref[...])
    lines = dot_nn(table_ref[...].astype(low_type), hot[:BUCKETS])
    for head in range(table_ref.shape[0]):
        bias_ref[head // 2, head % 2 : head % 2 + 1] = lines[head : head + 1]
    step = 2 * LANES
    for start in range(0, hot_ref.shape[0], step):
        wanted = start // 2 + step - 2 - row((step, length))
        hot_ref[start : start + step] = dot_nt(low(wanted == lane((step, length))), hot).astype(
            low_type
        )
    shape = (size, LANES)
    pair = device_of(row(shape), me, size)
    other = device_of(lane(shape), me, size)
    for m in range(query_ref.shape[0]):
        queries = query_ref[m : m + 1]
        if size < LANES:
            blank = jnp.zeros((1, LANES - size), jnp.int32)
            queries = jnp.concatenate([queries, blank], axis=1)
        picked = jnp.where(lane(shape) == pair, queries, 0).astype(full_type)
        mine = jnp.sum(picked, axis=1, keepdims=True)
        theirs = jnp.sum(jnp.where(lane(shape) == row(shape), mine, 0.0), axis=0, keepdims=True)
        same = jnp.where((mine == theirs) & (lane(shape) < size), 1.0, 0.0)
        same_ref[m] = same
        earlier = jnp.max(jnp.where(other < pair, same, 0.0), axis=1, keepdims=True)
        positive_ref[m] = jnp.broadcast_to(1.0 - earlier, shape)


def order_kernel(x_ref, order_ref, out_ref):
    out_ref[...] = dot_nn(x_ref[...], order_ref[...]).astype(low_type)


def turn_kernel(x_ref, out_ref):
    out_ref[...] = x_ref[...].T


def head_lanes():
    lane = lax.broadcasted_iota(jnp.int32, (1, LANES), 1)
    return [lane < LANES // 2, lane >= LANES // 2]


def project_kernel(pieces, pairs, x_ref, *refs):
    weight_refs, (qkv_ref, normed_ref, vector_ref, w_ref) = refs[:pieces], refs[pieces:]
    parts = qkv_ref.shape[1]
    in_width = pairs * parts * LANES

    @pl.when(pl.program_id(0) == 0)
    def assemble():
        fill_rows(w_ref, weight_refs)
        pick = lax.broadcasted_iota(jnp.int32, (16, LANES), 0) == lax.broadcasted_iota(
            jnp.int32, (16, LANES), 1
        )
        vectors = dot_nt(jnp.where(pick, 1.0, 0.0).astype(low_type), w_ref[:, -LANES:])
        vector_ref[...] = vectors[:8]

    x = x_ref[...].astype(full_type)
    normed = (x * rms_scale(x) * vector_ref[0:1]).astype(low_type)
    normed_ref[...] = normed
    projected = dot_nn(normed, w_ref[:, :in_width]).astype(low_type)
    for c in range(parts):
        for p in range(pairs):
            start = (c * pairs + p) * LANES
            qkv_ref[p, c] = projected[:, start : start + LANES]


def project(rows_low, weights, pairs, deps):
    count, width = rows_low.shape
    parts = 3
    return call(
        functools.partial(project_kernel, len(weights), pairs),
        "projection",
        [
            shape_of((pairs, parts, count, LANES), low_type),
            shape_of((count, width), low_type),
            shape_of((8, width), full_type),
        ],
        deps=deps,
        grid=(count // ROWS,),
        in_specs=[row_blocks((ROWS, width)), *(whole(piece.shape) for piece in weights)],
        out_specs=[
            pl.BlockSpec((pairs, parts, ROWS, LANES), lambda i: (0, 0, i, 0)),
            row_blocks((ROWS, width)),
            whole((8, width)),
        ],
        scratch_shapes=[pltpu.VMEM((width, weights[0].shape[1]), low_type)],
    )(rows_low, *weights)


def attention_kernel(len_ref, line_ref, qkv_ref, *refs):
    att_ref, prob_ref, inv_ref, tile_ref = refs[-4:]
    micro, slot = prob_ref.shape[1], prob_ref.shape[3]
    blocks = slot // LANES
    lanes = head_lanes()
    for h in range(2):
        for d in range(2 * blocks - 1):
            piece = jnp.broadcast_to(
                line_ref[0, h : h + 1, d * LANES : (d + 2) * LANES], (LANES, 2 * LANES)
            )
            turned = pltpu.roll(piece, LANES + 1, 1, stride=1, stride_axis=0)
            tile_ref[h, d] = turned[:, :LANES]

    def micro_step(m, carry):
        start = pl.multiple_of(m * slot, slot)
        key_valid = lax.broadcasted_iota(jnp.int32, (1, slot), 1) < len_ref[m]
        keys = qkv_ref[0, 1, pl.ds(start, slot), :]
        values = qkv_ref[0, 2, pl.ds(start, slot), :]
        values = jnp.concatenate([values, jnp.ones_like(values)], axis=1)
        for r in range(slot // ROWS):
            rows = pl.ds(start + r * ROWS, ROWS)
            queries = qkv_ref[0, 0, rows, :]
            queries = jnp.concatenate(
                [queries * lanes[h].astype(low_type) for h in range(2)], axis=0
            )
            first = r * (ROWS // LANES)
            bias = jnp.concatenate(
                [
                    jnp.concatenate(
                        [tile_ref[h, j - first - i + blocks - 1] for j in range(blocks)], axis=1
                    )
                    for h in range(2)
                    for i in range(ROWS // LANES)
                ],
                axis=0,
            )
            scores = dot_nt(queries, keys)
            scores = jnp.where(key_valid, scores + bias, masked_score)
            terms = jnp.exp(scores - jnp.max(scores, axis=1, keepdims=True)).astype(low_type)
            for h in range(2):
                prob_ref[0, m, h, r * ROWS : (r + 1) * ROWS, :] = terms[h * ROWS : (h + 1) * ROWS]
            mixed = dot_nn(terms, values)
            inverse = 1.0 / mixed[:, LANES:]
            mixed = mixed[:, :LANES] * inverse
            att_ref[rows, :] = jnp.where(lanes[0], mixed[:ROWS], mixed[ROWS:]).astype(low_type)
            inv_ref[rows, :] = jnp.where(lanes[0], inverse[:ROWS], inverse[ROWS:])
        return carry

    lax.fori_loop(0, micro, micro_step, 0)


def attention(lengths, lines, qkv, first, number, slot, before=(), deps=()):
    pairs, parts, count, _ = qkv.shape
    micro = count // slot
    spans = 2 * (slot // LANES) - 1
    column = pl.BlockSpec((count, LANES), lambda i: (0, i + first))
    return call(
        attention_kernel,
        "attention_forward",
        [
            shape_of((count, pairs * LANES), low_type),
            shape_of((pairs, micro, 2, slot, slot), low_type),
            shape_of((count, pairs * LANES), full_type),
        ],
        deps=deps,
        grid=(number,),
        in_specs=[
            on_scalars(),
            pl.BlockSpec((1, 2, lines.shape[2]), lambda i: (i + first, 0, 0)),
            pl.BlockSpec((1, parts, count, LANES), lambda i: (i + first, 0, 0, 0)),
            *[in_place()] * len(before),
        ],
        out_specs=[
            column,
            pl.BlockSpec((1, micro, 2, slot, slot), lambda i: (i + first, 0, 0, 0, 0)),
            column,
        ],
        input_output_aliases={3 + i: i for i in range(len(before))},
        scratch_shapes=[pltpu.VMEM((2, spans, LANES, LANES), full_type)],
    )(lengths, lines, qkv, *before)


def branch_kernel(att_ref, *refs):
    *weight_refs, out_ref, w_ref = refs

    @pl.when(pl.program_id(0) == 0)
    def assemble():
        fill_rows(w_ref, weight_refs)

    out_ref[...] = dot_nt(att_ref[...], w_ref[...]).astype(low_type)


def branch_rows(attended, weights, deps=()):
    count, head_width = attended.shape
    width = sum(piece.shape[0] for piece in weights)
    return call(
        branch_kernel,
        "branch",
        shape_of((count, width), low_type),
        deps=deps,
        grid=(count // (2 * ROWS),),
        in_specs=[
            row_blocks((2 * ROWS, head_width)),
            *(pl.BlockSpec((piece.shape[0], head_width), lambda i: (0, 3)) for piece in weights),
        ],
        out_specs=row_blocks((2 * ROWS, width)),
        scratch_shapes=[pltpu.VMEM((width, head_width), low_type)],
    )(attended, *weights)


def hidden_kernel(pieces, len_ref, x_ref, own_ref, came_ref, vector_ref, *refs):
    weight_refs, refs = refs[:pieces], refs[pieces:]
    normed_ref, slope_ref, act_ref, sum_ref, w_ref, rows_ref = refs
    m = pl.program_id(0)
    slot = x_ref.shape[0]

    @pl.when(m == 0)
    def assemble():
        fill_rows(w_ref, weight_refs)

    middle = middle_rows(x_ref, own_ref, came_ref)
    normed = (middle * rms_scale(middle) * vector_ref[1:2]).astype(low_type)
    valid = lax.broadcasted_iota(jnp.int32, (slot, 1), 0) < len_ref[m]
    normed_ref[...] = jnp.where(valid, normed, jnp.zeros_like(normed))
    rows_ref[...] = normed
    sum_ref[0] = jnp.sum(jnp.where(valid, middle, 0.0), axis=0, keepdims=True)
    act_ref[...] = jnp.zeros_like(act_ref)

    def rows_step(i, carry):
        rows = pl.ds(pl.multiple_of(i * ROWS, ROWS), ROWS)
        v = dot_nn(rows_ref[rows, :], w_ref[...])
        square = v * v
        gate = jnp.tanh(v * (gelu_slope + (gelu_slope * gelu_cubic) * square))
        half = 0.5 + 0.5 * gate
        active = (v * half).astype(low_type)
        counted = lax.broadcasted_iota(jnp.int32, (16, ROWS), 1) + i * ROWS < len_ref[m]
        counted = jnp.where(counted, 1.0, 0.0).astype(low_type)
        act_ref[0] += dot_nn(counted, active)[0:1]
        inner = 0.5 * gelu_slope + (1.5 * gelu_slope * gelu_cubic) * square
        slope_ref[rows, :] = (half + v * (1.0 - gate * gate) * inner).astype(low_type)
        return carry

    lax.fori_loop(0, slot // ROWS, rows_step, 0)


def middle_rows(x_ref, own_ref, came_ref):
    branch = own_ref[...].astype(full_type) + came_ref[...].astype(full_type)
    return x_ref[...].astype(full_type) + branch


def hidden(lengths, rows_low, own, came, vectors, weights, slot):
    count, width = rows_low.shape
    micro = count // slot
    inner = weights[0].shape[1]
    return call(
        functools.partial(hidden_kernel, len(weights)),
        "hidden_forward",
        [
            shape_of((count, width), low_type),
            shape_of((count, inner), low_type),
            shape_of((micro, 1, inner), full_type),
            shape_of((micro, 1, width), full_type),
            shape_of((width, inner), low_type),
        ],
        cost=(1200, 20000),
        grid=(micro,),
        in_specs=[
            on_scalars(),
            *[row_blocks((slot, width))] * 3,
            whole(vectors.shape),
            *(whole(piece.shape) for piece in weights),
        ],
        out_specs=[
            row_blocks((slot, width)),
            row_blocks((slot, inner)),
            row_blocks((1, 1, inner)),
            row_blocks((1, 1, width)),
            whole((width, inner)),
        ],
        scratch_shapes=[pltpu.VMEM((slot, width), low_type)],
    )(lengths, rows_low, own, came, vectors, *weights)


def few_rows(rows, count):
    place = lax.broadcasted_iota(jnp.int32, (count, rows[0].shape[1]), 0)
    total = jnp.zeros(place.shape, full_type)
    for i, row in enumerate(rows):
        total = jnp.where(place == i, row, total)
    return total


def pool_kernel(act_ref, *refs):
    *weight_refs, out_ref, w_ref = refs
    fill_rows(w_ref, weight_refs)
    sums = [act_ref[m] for m in range(act_ref.shape[0])]
    highs = [row.astype(low_type).astype(full_type) for row in sums]
    rests = [row - high for row, high in zip(sums, highs)]
    down = dot_nt(few_rows(highs + rests, 16).astype(low_type), w_ref[...])
    micro = len(sums)
    out_ref[...] = few_rows([down[m : m + 1] + down[micro + m : micro + m + 1] for m in range(micro)], 8)


def margin_kernel(len_ref, own_ref, other_ref, sum_ref, act_ref, vector_ref, send_ref):
    margins, rows = [], []
    for m in range(sum_ref.shape[0]):
        length = len_ref[m].astype(full_type)
        total = own_ref[m : m + 1] + other_ref[m : m + 1] + sum_ref[m]
        pooled = (total / length).astype(low_type).astype(full_type)
        final = pooled * rms_scale(pooled) * vector_ref[2:3]
        logits = [
            jnp.sum(final * vector_ref[i : i + 1], axis=1, keepdims=True) * pooled.shape[1] ** (-0.5)
            for i in (3, 4)
        ]
        lane = lax.broadcasted_iota(jnp.int32, pooled.shape, 1)
        margins.append(jnp.where(lane < LANES, logits[0] - logits[1], length))
        rows.append(pooled)
    width = rows[0].shape[1]
    for m in range(sum_ref.shape[0]):
        sums = act_ref[m]
        rows += [sums[:, i * width : (i + 1) * width] for i in range(sums.shape[1] // width)]
    send_ref[...] = few_rows(rows + margins, 8)


def ranking(margins, same, positive):
    place = lax.broadcasted_iota(jnp.int32, margins.shape, 0)
    lane = lax.broadcasted_iota(jnp.int32, margins.shape, 1)
    others = jnp.sum(jnp.where(place == lane, margins, 0.0), axis=0, keepdims=True)
    row_max = jnp.max(jnp.where(same, others, masked_score), axis=1, keepdims=True)
    terms = jnp.where(same, jnp.exp(jnp.where(same, others - row_max, 0.0)), 0.0)
    chance = jnp.exp(margins - row_max) / jnp.sum(terms, axis=1, keepdims=True)
    return LOSS_SCALE * (chance - positive)


def pooled_grad(pooled, d_margin, vector_ref):
    scale = rms_scale(pooled)
    d_logit = d_margin * pooled.shape[1] ** (-0.5)
    d_final = d_logit * (vector_ref[3:4] - vector_ref[4:5])
    return norm_input_grad(d_final, vector_ref[2:3], pooled, scale)


def rank_kernel(
    small_pieces, len_ref, same_ref, positive_ref, vector_ref, slope_ref, down_ref, up_ref, *refs
):
    small_refs, refs = refs[:small_pieces], refs[small_pieces:]
    line_ref, act_ref, rank_ref, hidden_ref, d_ref = refs
    m = pl.program_id(0)

    @pl.when(m == 0)
    def rank():
        lines = []
        for i in range(2):
            margins = stacked_row(small_refs, 6 + i)[:, :LANES]
            d_margins = ranking(margins, same_ref[i] > 0.5, positive_ref[i])
            rank_ref[i] = d_margins
            pooled = small_refs[0][0, i : i + 1, :]
            d_pooled = pooled_grad(pooled, d_margins[0:1, 0:1], vector_ref)
            lines.append(d_pooled / len_ref[i].astype(full_type))
        line_ref[...] = few_rows(lines, 8)
        d_act = dot_nn(few_rows(lines, 16).astype(low_type), down_ref[...])
        act_ref[...] = d_act[:8]

    d_row = jnp.where(m == 0, act_ref[0:1], act_ref[1:2])
    d_hidden = (slope_ref[...].astype(full_type) * d_row).astype(low_type)
    hidden_ref[...] = d_hidden
    d_normed = dot_nt(d_hidden, up_ref[...])
    valid = lax.broadcasted_iota(jnp.int32, (d_normed.shape[0], 1), 0) < len_ref[m]
    d_ref[...] = jnp.where(valid, d_normed, 0.0).astype(low_type)


def rank_back(lengths, same, positive, vectors, slope, small_all, down, up, slot, deps):
    count, inner = slope.shape
    width = vectors.shape[1]
    return call(
        functools.partial(rank_kernel, len(small_all)),
        "rank_backward",
        [
            shape_of((8, width), full_type),
            shape_of((8, inner), full_type),
            shape_of(positive.shape, full_type),
            shape_of((count, inner), low_type),
            shape_of((count, width), low_type),
        ],
        cost=(1200, 20000),
        deps=deps,
        grid=(count // slot,),
        in_specs=[
            on_scalars(),
            *(whole(array.shape) for array in (same, positive, vectors)),
            row_blocks((slot, inner)),
            *(whole(array.shape) for array in (down, up, *small_all)),
        ],
        out_specs=[
            whole((8, width)),
            whole((8, inner)),
            whole(positive.shape),
            row_blocks((slot, inner)),
            row_blocks((slot, width)),
        ],
    )(lengths, same, positive, vectors, slope, down, up, *small_all)


def up_grad_kernel(normed_ref, d_ref, *out_refs):
    for n in range(normed_ref.shape[1] // ROWS):
        columns = slice(n * ROWS, (n + 1) * ROWS)
        spill_rows(dot_tn(normed_ref[:, columns], d_ref[...]), out_refs, n * ROWS)


def up_grad(normed, d_hidden, rows):
    return call(
        up_grad_kernel,
        "hidden_in_gradient",
        [shape_of((r, d_hidden.shape[1]), low_type) for r in rows],
        cost=(1200, 15000),
    )(normed, d_hidden)


def middle_kernel(
    pieces, len_ref, x_ref, branch_ref, other_ref, own_ref, came_ref, vector_ref, line_ref,
    att_ref, inv_ref, *refs
):
    weight_refs, refs = refs[:pieces], refs[pieces:]
    d_ref, d_att_ref, total_ref, w_ref = refs
    m = pl.program_id(0)

    @pl.when(m == 0)
    def assemble():
        fill_rows(w_ref, weight_refs)
        total_ref[...] = jnp.zeros_like(total_ref)

    middle = middle_rows(x_ref, branch_ref, other_ref)
    own = own_ref[...].astype(full_type)
    scale = rms_scale(middle)
    valid = lax.broadcasted_iota(jnp.int32, (middle.shape[0], 1), 0) < len_ref[m]
    line = jnp.where(m == 0, line_ref[0:1], line_ref[1:2])
    d_middle = jnp.where(valid, line, 0.0) + norm_input_grad(
        own + came_ref[...].astype(full_type), vector_ref[1:2], middle, scale
    )
    d_ref[...] = d_middle
    d_low = d_middle.astype(low_type)
    d_att_ref[...] = (dot_nn(d_low, w_ref[...]) * inv_ref[...]).astype(low_type)
    total_ref[...] += dot_tn(d_low, att_ref[...])


def middle_back(
    lengths, rows_low, branch, other, own, came, vectors, lines, attended, inverse, weights, slot
):
    count, width = rows_low.shape
    head_width = attended.shape[1]
    return call(
        functools.partial(middle_kernel, len(weights)),
        "middle_backward",
        [
            shape_of((count, width), full_type),
            shape_of((count, head_width), low_type),
            shape_of((width, head_width), full_type),
        ],
        cost=(600, 15000),
        grid=(count // slot,),
        in_specs=[
            on_scalars(),
            *[row_blocks((slot, width))] * 5,
            whole(vectors.shape),
            whole(lines.shape),
            row_blocks((slot, head_width)),
            row_blocks((slot, head_width)),
            *(
                pl.BlockSpec((piece.shape[0], head_width), lambda i: (0, 3)) for piece in weights
            ),
        ],
        out_specs=[
            row_blocks((slot, width)),
            row_blocks((slot, head_width)),
            whole((width, head_width)),
        ],
        scratch_shapes=[pltpu.VMEM((width, head_width), low_type)],
    )(
        lengths, rows_low, branch, other, own, came, vectors, lines, attended, inverse, *weights
    )


def attention_back_kernel(
    befores, grads, tables, own, prob_ref, qkv_ref, d_ref, att_ref, turned_ref, hot_ref, *refs
):
    table_refs, refs = refs[:tables], refs[tables:]
    grad_refs, refs = refs[:grads], refs[grads:]
    d_out_ref, table_ref, *out_refs, tile_ref, dk_ref, dv_ref = refs[befores:]
    step, last = pl.program_id(0), pl.num_programs(0) - 1
    steps = last - 1 if grads else last

    if grads:

        @pl.when(step == last)
        def projection():
            spill_rows(grad_refs[0][...], out_refs)

    @pl.when(step <= steps)
    def heads():
        pair_back(
            prob_ref, qkv_ref, d_ref, att_ref, turned_ref, hot_ref, d_out_ref, table_ref, out_refs,
            tile_ref, dk_ref, dv_ref
        )
        if tables:
            lines = [
                ref[p, h : h + 1]
                for ref in (*table_refs, table_ref)
                for p in range(ref.shape[0])
                for h in range(2)
            ]
            width = turned_ref.shape[0]
            place = lax.broadcasted_iota(jnp.int32, (width, 16), 0) % own
            pick = place == lax.broadcasted_iota(jnp.int32, (width, 16), 1)
            pick = jnp.where(pick, 1.0, 0.0).astype(low_type)
            spread = dot_nn(pick, few_rows(lines, 16).astype(low_type))
            spill_rows(spread, [ref.at[:, 3 * LANES :] for ref in out_refs])


def pair_back(
    prob_ref, qkv_ref, d_ref, att_ref, turned_ref, hot_ref, d_out_ref, table_ref, out_refs,
    tile_ref, dk_ref, dv_ref
):
    micro, slot = prob_ref.shape[1], prob_ref.shape[3]
    blocks = slot // LANES
    spans = 2 * blocks - 1
    lanes = head_lanes()

    tile_ref[...] = jnp.zeros_like(tile_ref)

    def micro_step(m, carry):
        start = pl.multiple_of(m * slot, slot)
        everything = pl.ds(start, slot)
        keys, values = qkv_ref[0, 1, everything, :], qkv_ref[0, 2, everything, :]
        for r in range(slot // SPAN):
            rows = pl.ds(start + r * SPAN, SPAN)
            queries = qkv_ref[0, 0, rows, :]
            queries = jnp.concatenate(
                [queries * lanes[h].astype(low_type) for h in range(2)], axis=0
            )
            d_att = d_ref[rows, :]
            product = d_att.astype(full_type) * att_ref[rows, :].astype(full_type)
            row_dot = jnp.concatenate(
                [
                    jnp.sum(jnp.where(lanes[h], product, 0.0), axis=1, keepdims=True)
                    for h in range(2)
                ],
                axis=0,
            )
            d_att = jnp.concatenate([d_att * lanes[h].astype(low_type) for h in range(2)], axis=0)
            span = slice(r * SPAN, (r + 1) * SPAN)
            probs = jnp.concatenate([prob_ref[0, m, h, span, :] for h in range(2)], axis=0)
            d_scores = probs.astype(full_type) * (dot_nt(d_att, values) - row_dot)
            d_low = d_scores.astype(low_type)
            for h in range(2):
                for i in range(SPAN // LANES):
                    for j in range(blocks):
                        top = h * SPAN + i * LANES
                        tile_ref[h, j - r * (SPAN // LANES) - i + blocks - 1] += d_scores[
                            top : top + LANES, j * LANES : (j + 1) * LANES
                        ]
            d_queries = dot_nn(d_low, keys)
            d_out_ref[0, 0, rows, :] = jnp.where(
                lanes[0], d_queries[:SPAN], d_queries[SPAN:]
            ).astype(low_type)
            d_keys, d_values = dot_tn(d_low, queries), dot_tn(probs, d_att)
            dk_ref[...] = d_keys if r == 0 else dk_ref[...] + d_keys
            dv_ref[...] = d_values if r == 0 else dv_ref[...] + d_values
        d_out_ref[0, 1, everything, :] = dk_ref[...].astype(low_type)
        d_out_ref[0, 2, everything, :] = dv_ref[...].astype(low_type)
        return carry

    lax.fori_loop(0, micro, micro_step, 0, unroll=True)
    d_project = jnp.concatenate([d_out_ref[0, c] for c in range(3)], axis=1)
    spill_rows(dot_nn(turned_ref[...], d_project), [ref.at[:, : 3 * LANES] for ref in out_refs])
    flip = (
        lax.broadcasted_iota(jnp.int32, (LANES, LANES), 0)
        + lax.broadcasted_iota(jnp.int32, (LANES, LANES), 1)
        == LANES - 1
    )
    flip = jnp.where(flip, 1.0, 0.0).astype(low_type)
    tiles = tile_ref[...].reshape(2 * spans * LANES, LANES)
    high = tiles.astype(low_type)
    rest = (tiles - high.astype(full_type)).astype(low_type)
    flipped = dot_nn(high, flip) + dot_nn(rest, flip)
    zeros = jnp.zeros((LANES, LANES), full_type)
    lines = []
    for h in range(2):
        sums = []
        for d in range(spans):
            top = (h * spans + d) * LANES
            wide = jnp.concatenate([flipped[top : top + LANES], zeros], axis=1)
            turned = pltpu.roll(wide, 0, 1, stride=1, stride_axis=0)
            sums.append(jnp.sum(turned, axis=0, keepdims=True))
        lines.append(jnp.concatenate(sums, axis=1))
    highs = [line.astype(low_type).astype(full_type) for line in lines]
    rests = [line - high for line, high in zip(lines, highs)]
    table = dot_nn(few_rows(highs + rests, 16).astype(low_type), hot_ref[...])
    table_ref[0] = few_rows([table[h : h + 1] + table[2 + h : 3 + h] for h in range(2)], 8)


def attention_back(
    probs, qkv, d_attended, attended, turned, hot, rows, first, number, slot, own,
    grad_out=None, tables=(), before=(), deps=()
):
    width, count = turned.shape
    micro = count // slot
    pairs = qkv.shape[0]
    spans = 2 * (slot // LANES) - 1
    at = lambda i: jnp.minimum(i, number - 1)
    lead = lambda shape: pl.BlockSpec(shape, lambda i: (at(i) + first,) + (0,) * (len(shape) - 1))
    column = pl.BlockSpec((count, LANES), lambda i: (0, at(i) + first))
    if tables:
        steps, extra, extra_specs = number, tables, [whole(table.shape) for table in tables]
        gradients = [shape_of((r, 4 * LANES), low_type) for r in rows]
        gradient_specs = [whole((r, 4 * LANES)) for r in rows]
    else:
        steps = number + (grad_out is not None)
        extra = () if grad_out is None else (grad_out,)
        extra_specs = [whole(array.shape) for array in extra]
        gradients = [shape_of((r, pairs * 3 * LANES), low_type) for r in rows]
        gradient_specs = [pl.BlockSpec((r, 3 * LANES), lambda i: (0, i + first)) for r in rows]
    position = 6 + len(extra)
    return call(
        functools.partial(
            attention_back_kernel, len(before), 0 if grad_out is None else 1, len(tables), own
        ),
        "attention_backward",
        [
            shape_of((pairs, 3, count, LANES), low_type),
            shape_of((number, 8, LANES), full_type),
            *gradients,
        ],
        deps=deps,
        grid=(steps,),
        in_specs=[
            lead((1, micro, 2, slot, slot)),
            lead((1, 3, count, LANES)),
            column,
            column,
            whole(turned.shape),
            whole(hot.shape),
            *extra_specs,
            *[in_place()] * len(before),
        ],
        out_specs=[lead((1, 3, count, LANES)), pl.BlockSpec((1, 8, LANES), lambda i: (at(i), 0, 0)), *gradient_specs],
        input_output_aliases={position + i: i if i == 0 else i + 1 for i in range(len(before))},
        scratch_shapes=[
            pltpu.VMEM((2, spans, LANES, LANES), full_type),
            pltpu.VMEM((slot, LANES), full_type),
            pltpu.VMEM((slot, LANES), full_type),
        ],
    )(probs, qkv, d_attended, attended, turned, hot, *extra, *before)


def normed_back_kernel(d_ref, *refs):
    *weight_refs, out_ref, w_ref = refs
    pairs, parts = d_ref.shape[0], d_ref.shape[1]

    @pl.when(pl.program_id(0) == 0)
    def assemble():
        fill_rows(w_ref, weight_refs, slice(0, w_ref.shape[1]))

    blocks = [d_ref[p, c] for c in range(parts) for p in range(pairs)]
    d_normed = dot_nt(jnp.concatenate(blocks, axis=1), w_ref[...])
    out_ref[...] = d_normed.astype(low_type)


def normed_back(d_project, weights, deps):
    pairs, parts, count, _ = d_project.shape
    width = sum(piece.shape[0] for piece in weights)
    return call(
        normed_back_kernel,
        "normed_backward",
        shape_of((count, width), low_type),
        cost=(900, 15000),
        deps=deps,
        grid=(count // ROWS,),
        in_specs=[
            pl.BlockSpec((pairs, parts, ROWS, LANES), lambda i: (0, 0, i, 0)),
            *(whole(piece.shape) for piece in weights),
        ],
        out_specs=row_blocks((ROWS, width)),
        scratch_shapes=[pltpu.VMEM((width, pairs * parts * LANES), low_type)],
    )(d_project, *weights)


def token_kernel(d_ref, own_ref, came_ref, x_ref, vector_ref, order_ref, out_ref, done_ref):
    x = x_ref[...].astype(full_type)
    d_normed = own_ref[...].astype(full_type) + came_ref[...].astype(full_type)
    grad = d_ref[...] + norm_input_grad(d_normed, vector_ref[0:1], x, rms_scale(x))
    high = grad.astype(low_type)
    rest = (grad - high.astype(full_type)).astype(low_type)
    order = order_ref[...]
    out_ref[...] = dot_nt(high, order) + dot_nt(rest, order)
    done_ref[...] = jnp.zeros_like(done_ref)


def token_back(d_middle, own, came, rows_low, vectors, order, deps):
    count, width = rows_low.shape
    return call(
        token_kernel,
        "token_gradient",
        [shape_of((count, width), full_type), shape_of((8, LANES), full_type)],
        cost=(1200, 15000),
        deps=deps,
        grid=(count // ROWS,),
        in_specs=[row_blocks((ROWS, width))] * 4 + [whole(vectors.shape), whole(order.shape)],
        out_specs=[row_blocks((ROWS, width)), whole((8, LANES))],
    )(d_middle, own, came, rows_low, vectors, order)


def total_kernel(smalls, counts, micro, pairs, *refs):
    small_refs, refs = refs[:smalls], refs[smalls:]
    groups = []
    for count in counts:
        groups.append(refs[:count])
        refs = refs[count:]
    rank_ref, vector_ref, in_ref, up_ref, gain_ref, tied_ref, down_ref, line_ref, *out_refs = refs
    size, width = sum(ref.shape[0] for ref in small_refs), small_refs[0].shape[2]
    row_of = lambda row: stacked_row(small_refs, row)
    own = down_ref.shape[0]
    inverse = 1.0 / LOSS_SCALE
    add_up = lambda values: jnp.sum(values, axis=0, keepdims=True).sum(axis=1, keepdims=True)
    squares, sums = 0.0, []
    for group, out_ref in zip(groups, out_refs):
        total = sum(ref[...].astype(full_type) for ref in group) * inverse
        total, rest = total[:, : out_ref.shape[1]], total[:, out_ref.shape[1] :]
        out_ref[...] = total
        sums.append((total, rest))
        squares = squares + add_up(total * total)
    table = sums[1][1]

    block = lax.broadcasted_iota(jnp.int32, (size, width), 1) // own
    mine = block == lax.broadcasted_iota(jnp.int32, (size, width), 0)
    fold = lax.broadcasted_iota(jnp.int32, (width, LANES), 0) % own == lax.broadcasted_iota(
        jnp.int32, (width, LANES), 1
    )
    fold = jnp.where(fold, 1.0, 0.0).astype(low_type)
    down, ranked = 0.0, 0.0
    lane = lax.broadcasted_iota(jnp.int32, (1, LANES), 1)
    own_factor = (vector_ref[3:4, :LANES] - vector_ref[4:5, :LANES]) * vector_ref[2:3, :LANES]
    own_factor = jnp.where(lane < own, own_factor, 0.0)
    parts = down_ref.shape[1] // width
    for m in range(micro):
        pooled = row_of(m)
        scale = rms_scale(pooled)
        lengths = row_of(micro + micro * parts + m)
        margins, lengths = lengths[:, 0:1], lengths[:, LANES : LANES + 1]
        d_logit = rank_ref[m][:, 0:1] * width ** (-0.5)
        mean = d_logit * margins * (width**0.5 / width) / scale
        mine_low = dot_nn(jnp.where(mine, pooled, 0.0).astype(low_type), fold)
        ranked = ranked + jnp.sum(mine_low * scale * d_logit, axis=0, keepdims=True)
        d_pooled = scale * d_logit * own_factor - mine_low * scale**3 * mean
        lines = (d_pooled / lengths).astype(low_type)
        acts = [row_of(micro + m * parts + i) for i in range(parts)]
        acts = jnp.concatenate(acts, axis=1)
        high = acts.astype(low_type)
        rest = (acts - high.astype(full_type)).astype(low_type)
        down = down + dot_tn(lines, high) + dot_tn(lines, rest)
    down = down[:own] * inverse
    down_ref[...] = down
    squares = squares + add_up(down * down)

    ranked = ranked[:, :own] * inverse
    rounded = lambda ref, i: ref[i : i + 1].astype(low_type).astype(full_type)
    tied_gap = rounded(tied_ref, 0) - rounded(tied_ref, 1)

    def through(products):
        ones = jnp.ones((16, products.shape[1]), low_type)
        high = products.astype(low_type)
        rest = (products - high.astype(full_type)).astype(low_type)
        return (dot_nt(ones, high) + dot_nt(ones, rest))[0:1]

    weighed = lambda ref, total: ref.astype(low_type).astype(full_type) * total
    first = 0.0
    for p in range(pairs):
        source = sums[0][0] if p < pairs - 1 else sums[1][0]
        offset = p * 3 * LANES if p < pairs - 1 else 0
        for c in range(3):
            columns = slice(offset + c * LANES, offset + (c + 1) * LANES)
            first = first + weighed(in_ref[c, :, p * LANES : (p + 1) * LANES], source[:, columns])
    rows = [
        through(first) / rounded(gain_ref, 0),
        through(weighed(up_ref[...], sums[2][0])) / rounded(gain_ref, 1),
        tied_gap * ranked,
        rounded(gain_ref, 2) * ranked,
    ]
    place = lax.broadcasted_iota(jnp.int32, (8, own), 0)
    extra = jnp.zeros((8, own), full_type)
    for i, row in enumerate(rows):
        extra = jnp.where(place == i, row, extra)
    line_ref[...] = jnp.zeros_like(line_ref)
    line_ref[:8, :own] = extra
    line_ref[8:16] = jnp.broadcast_to(squares, (8, LANES))
    line_ref[16 : 16 + 2 * pairs] = table[: 2 * pairs]


def totals(
    small_all, ranks, vectors, grads, heads_in, hidden_in, gains, tied_rows, widths, micro, deps
):
    counts = tuple(len(group) for group in grads)
    flat = [array for group in grads for array in group]
    own, inner = hidden_in.shape
    down, line, *sums = call(
        functools.partial(
            total_kernel, len(small_all), counts, micro, heads_in.shape[2] // LANES
        ),
        "gradient_totals",
        [
            shape_of((own, inner), full_type),
            shape_of((24, LANES), full_type),
            *(shape_of((own, width), full_type) for width in widths),
        ],
        cost=(100, 10000),
        deps=deps,
    )(*small_all, *flat, ranks, vectors, heads_in, hidden_in, gains, tied_rows)
    return down, line, sums


def stage_kernel(*refs):
    count = len(refs) // 2
    for ref, target in zip(refs[:count], refs[count:]):
        target[...] = ref[...]


def adam(weight, first_old, second, grad, factor, rate, decay, step_ref):
    clipped = grad * factor
    next_first = beta_first * first_old + (1.0 - beta_first) * clipped
    next_second = beta_second * second + (1.0 - beta_second) * clipped * clipped
    first_hat = next_first * step_ref[0]
    second_hat = next_second * step_ref[1]
    next_weight = weight - rate * (first_hat / (jnp.sqrt(second_hat) + adam_eps) + decay * weight)
    return next_weight, next_first, next_second


def square_kernel(heads, own_ref, other_ref, out_ref, extra_ref):
    place = lax.broadcasted_iota(jnp.int32, (8, LANES), 0)
    extra = own_ref[:8] + jnp.where(place < 2, other_ref[:8], 0.0)
    extra_ref[...] = extra
    counted = jnp.where(place == 3, 2.0, 1.0) * extra * extra
    add_up = lambda values: jnp.sum(values, axis=0, keepdims=True).sum(axis=1, keepdims=True)
    squares = own_ref[8:16] + other_ref[8:16] + add_up(counted)
    out_ref[:8] = squares
    tables = own_ref[16:24] * own_ref[16:24] + other_ref[16:24] * other_ref[16:24]
    out_ref[8:16] = own_ref[16:24]
    out_ref[16:24] = jnp.broadcast_to(add_up(tables), (8, LANES))


def update_kernel(size, squares, groups, me_ref, step_ref, extra_ref, *refs):
    square_refs, refs = refs[:squares], refs[squares:]
    grad_refs, refs = refs[:groups], refs[groups:]
    state_refs, refs = refs[:21], refs[21:]
    norm_ref, *out_refs = refs
    tiles = stacked(square_refs)
    place = lax.broadcasted_iota(jnp.int32, (tiles.shape[0], 1, 1), 0)
    first = device_of(place, me_ref[0], size) == 0
    tables = jnp.sum(jnp.where(first, tiles[:, 8:24], 0.0), axis=0)
    norm = jnp.sqrt(jnp.sum(tiles[:, 0:8], axis=0)[0:1, 0:1] + tables[8:9, 0:1])
    norm_ref[...] = norm
    factor = jnp.minimum(1.0, clip_limit / (norm + 1e-06))
    weights, firsts, seconds = state_refs[:7], state_refs[7:14], state_refs[14:]
    next_weights, next_firsts, next_seconds = out_refs[:7], out_refs[7:14], out_refs[14:]

    def step(index, where, grad, rate, decay):
        results = adam(
            weights[index][where], firsts[index][where], seconds[index][where], grad, factor,
            rate, decay, step_ref,
        )
        for target, result in zip((next_weights, next_firsts, next_seconds), results):
            target[index][where] = result

    everything = (slice(None), slice(None))
    early_ref, late_ref, up_ref, down_ref = grad_refs
    pairs = weights[0].shape[2] // LANES
    for p in range(pairs):
        source, offset = (early_ref, p * 3) if p < pairs - 1 else (late_ref, 0)
        for c in range(3):
            columns = slice((offset + c) * LANES, (offset + c + 1) * LANES)
            where = (c, slice(None), slice(p * LANES, (p + 1) * LANES))
            step(0, where, source[:, columns], rate_matrix, decay_matrix)
    step(1, everything, early_ref[:, (pairs - 1) * 3 * LANES :], rate_matrix, decay_matrix)
    step(2, everything, up_ref[...], rate_matrix, decay_matrix)
    step(3, everything, down_ref[...], rate_matrix, decay_matrix)
    rows = weights[4].shape[1]
    extra = extra_ref[...]
    step(4, everything, extra[0:3, :rows], rate_vector, 0.0)
    tied = extra[3:4, :rows]
    step(5, everything, jnp.concatenate([tied, -tied], axis=0), rate_vector, 0.0)
    step(6, everything, tables[: 2 * pairs, :BUCKETS], rate_vector, 0.0)


def update(size, pick, corrections, extra, squares, grads, states):
    return call(
        functools.partial(update_kernel, size, len(squares), len(grads)),
        "update",
        [shape_of((1, 1), full_type)] + [shape_of(s.shape, full_type) for s in states],
        cost=(0, 6000),
        grid=(1,),
        in_specs=[
            on_scalars(),
            on_scalars(),
            *(whole(array.shape) for array in (extra, *squares, *grads, *states)),
        ],
    )(pick, corrections, extra, *squares, *grads, *states)


def body(
    tokens,
    pair_lengths,
    query_ids,
    distance_bucket,
    step_count,
    heads_in,
    heads_out,
    hidden_in,
    hidden_out,
    gains,
    tied_rows,
    bias_table,
    first_heads_in,
    first_heads_out,
    first_hidden_in,
    first_hidden_out,
    first_gains,
    first_tied,
    first_table,
    second_heads_in,
    second_heads_out,
    second_hidden_in,
    second_hidden_out,
    second_gains,
    second_tied,
    second_table,
):
    size = lax.axis_size("dp")
    me = lax.axis_index("dp")
    core = lax.axis_index("mp")
    micro, _, slot, width = tokens.shape
    count = micro * slot
    own, local_heads = heads_in.shape[0], bias_table.shape[1]
    head_width = heads_in.shape[2]
    inner = hidden_in.shape[1]
    pairs = local_heads // 2
    spans = 2 * (slot // LANES) - 1
    turn_matrix = lambda array: jnp.transpose(array, (1, 0, 2))
    heads_in, first_heads_in, second_heads_in = (
        turn_matrix(array) for array in (heads_in, first_heads_in, second_heads_in)
    )
    gains, tied_rows, bias_table = gains.T, tied_rows.T, bias_table.T
    first_gains, first_tied, first_table = first_gains.T, first_tied.T, first_table.T
    second_gains, second_tied, second_table = second_gains.T, second_tied.T, second_table.T

    packed_heads = call(
        pack_heads_kernel, "pack_heads", shape_of((own, 4 * head_width + LANES), low_type), vmem=56
    )(heads_in, heads_out, gains, tied_rows)
    packed_up, packed_down = call(
        pack_hidden_kernel, "pack_hidden", [shape_of((own, inner), low_type)] * 2
    )(hidden_in, hidden_out)
    weights = (heads_in, heads_out, hidden_in, hidden_out, gains, tied_rows, bias_table)
    firsts = (
        first_heads_in,
        first_heads_out,
        first_hidden_in,
        first_hidden_out,
        first_gains,
        first_tied,
        first_table,
    )
    seconds = (
        second_heads_in,
        second_heads_out,
        second_hidden_in,
        second_hidden_out,
        second_gains,
        second_tied,
        second_table,
    )
    states = [*weights, *firsts, *seconds]
    large = [index for index, state in enumerate(states) if index % 7 < 4]
    staged = call(
        stage_kernel, "stage", [shape_of(states[i].shape, full_type) for i in large], vmem=56
    )(*(states[i] for i in large))
    for i, array in zip(large, staged):
        states[i] = array

    lengths = pair_lengths.reshape(micro)
    device = me.reshape(1)
    order, lines, hot_spans, same_tile, positive_tile = call(
        functools.partial(prepare_kernel, size),
        "prepare",
        [
            shape_of((width, width), low_type),
            shape_of((pairs, 2, 2 * slot), full_type),
            shape_of((spans * 2 * LANES, LANES), low_type),
            shape_of((micro, size, LANES), full_type),
            shape_of((micro, size, LANES), full_type),
        ],
        grid=(1,),
        in_specs=[
            on_scalars(),
            whole((1, 2 * slot)),
            whole(bias_table.shape),
            whole(query_ids.shape),
        ],
    )(
        device,
        jnp.pad(distance_bucket, (0, 1), constant_values=-1).reshape(1, 2 * slot),
        bias_table,
        query_ids,
    )
    step_float = step_count.astype(full_type)
    corrections = jnp.stack(
        [1.0 / (1.0 - beta_first**step_float), 1.0 / (1.0 - beta_second**step_float)]
    )

    rows_low = call(
        order_kernel,
        "order_tokens",
        shape_of((count, width), low_type),
        cost=(600, 5000),
        grid=(count // ROWS,),
        in_specs=[row_blocks((ROWS, width)), whole((width, width))],
        out_specs=row_blocks((ROWS, width)),
    )(tokens.reshape(count, width), order)
    if size != 16:
        weight_heads, weight_up, weight_down = (
            [gather_doubling(part, size)] for part in (packed_heads, packed_up, packed_down)
        )
        qkv, normed_first, vectors = project(rows_low, weight_heads, pairs, ())
    else:
        heads_line, packed_up, packed_down = join(
            line_parts(packed_heads, size, "heads"),
            deps=(staged[0], order, corrections),
            passing=(packed_up, packed_down),
        )
        heads_sides = side_parts(heads_line, size, "heads")
        up_pair = join(
            [packed_up, swap(packed_up, 8, size, "up")],
            deps=(rows_low,),
        )
        up_near = swap(up_pair, 4, size, "up")
        low, high, packed_down = gather_step(*heads_sides, deps=(up_pair,), passing=(packed_down,))
        down_far = swap(packed_down, 8, size, "down")
        heads_corner = corner_parts(low, high, size, "heads_corner")
        up_line = join([up_pair, up_near], deps=(low,))
        down_pair = join([packed_down, down_far], deps=(up_line,))
        down_near = swap(down_pair, 4, size, "down")
        up_sides = side_parts(up_line, size, "up")
        weight_heads = [heads_line, *heads_sides, *heads_corner]
        qkv, normed_first, vectors = project(rows_low, weight_heads, pairs, (down_pair,))
    filled = attention(lengths, lines, qkv, 0, 1, slot)
    if size == 16:
        down_line = join([down_pair, down_near], deps=(filled[0],))
        down_sides = side_parts(down_line, size, "down")
    if pairs > 1:
        filled = attention(lengths, lines, qkv, 1, pairs - 1, slot, before=filled)
    if size == 16:
        low, high = gather_step(*up_sides, deps=(filled[0],))
        up_corner = corner_parts(low, high, size, "up_corner")
        weight_up = [up_line, *up_sides, *up_corner]
    turned_first = call(turn_kernel, "turn", shape_of((width, count), low_type))(normed_first)
    attended, probs, inverse = filled
    branch = branch_rows(
        attended, weight_heads, (low, *down_sides, turned_first) if size == 16 else ()
    )
    if size == 16:
        low, high = gather_step(*down_sides, deps=(branch,))
        down_corner = corner_parts(low, high, size, "down_corner")
        weight_down = [down_line, *down_sides, *down_corner]
    branch_came = other_core(branch, "branch_other_core")
    normed_second, slope, act_sum, middle_sum, full_up = hidden(
        lengths, rows_low, branch, branch_came, vectors, weight_up, slot
    )
    down, full_down = call(
        pool_kernel,
        "pool",
        [shape_of((8, width), full_type), shape_of((width, inner), low_type)],
        cost=(20, 5000),
    )(act_sum, *weight_down)
    small = call(
        margin_kernel,
        "margin",
        shape_of((8, width), full_type),
        grid=(1,),
        in_specs=[
            on_scalars(),
            *(whole(array.shape) for array in (down, down, middle_sum, act_sum, vectors)),
        ],
        out_specs=whole((8, width)),
    )(lengths, down, other_core(down, "pooled_part_other_core"), middle_sum, act_sum, vectors)
    small_all = gather_small(small, size, "small_sums")

    d_line, _, ranks, d_hidden, d_normed_second = rank_back(
        lengths, same_tile, positive_tile, vectors, slope, small_all, full_down, full_up, slot,
        (turned_first,),
    )
    d_normed_second_came = other_core(d_normed_second, "second_gradient_other_core")
    up_sum = Scatter(
        up_grad(normed_second, d_hidden, piece_rows(size, width)), size, "up_gradient"
    )
    d_middle, d_attended, g_out = middle_back(
        lengths, rows_low, branch, branch_came, d_normed_second, d_normed_second_came, vectors,
        d_line, attended, inverse, weight_heads, slot,
    )
    scatter_sides([up_sum], deps=(d_attended,))
    d_project, tables, *g_early = attention_back(
        probs, qkv, d_attended, attended, turned_first, hot_spans, piece_rows(size, width),
        0, pairs - 1, slot, own, grad_out=g_out,
    )
    early_sum = Scatter(g_early, size, "early_gradient")
    d_project, table, *g_late = attention_back(
        probs, qkv, d_attended, attended, turned_first, hot_spans, piece_rows(size, width),
        pairs - 1, 1, slot, own, tables=(tables,), before=(d_project,),
    )
    late_sum = Scatter(g_late, size, "late_gradient")
    up_sum.near(deps=(table,))
    sides = scatter_sides([early_sum, late_sum], deps=tuple(up_sum.came))
    d_normed_first = normed_back(d_project, weight_heads, sides)
    up_parts = up_sum.far(deps=sides)
    (d_normed_first,) = early_sum.near(deps=tuple(up_parts), passing=(d_normed_first,))
    token_gradient, token_done = token_back(
        d_middle, d_normed_first, other_core(d_normed_first, "first_gradient_other_core"), rows_low,
        vectors, order, early_sum.sources,
    )
    early_parts = early_sum.far(deps=(token_done,))
    late_parts, _ = late_sum.line(deps=(early_parts[0],))

    g_down, line, grad_sums = totals(
        small_all, ranks, vectors, [early_parts, late_parts, up_parts], heads_in, hidden_in, gains, tied_rows,
        (head_width * 3, 3 * LANES, inner), micro, (),
    )
    square_tile, extra = call(
        functools.partial(square_kernel, local_heads),
        "squares",
        [shape_of((24, LANES), full_type), shape_of((8, LANES), full_type)],
    )(line, other_core(line, "totals_other_core"))
    squares_all = gather_small(square_tile, size, "squares")
    grads = [*grad_sums, g_down]
    norm, *results = update(size, device, corrections, extra, squares_all, grads, states)
    for index in (0, 7, 14):
        results[index] = turn_matrix(results[index])
        for other in (4, 5, 6):
            results[index + other] = results[index + other].T
    return (norm.reshape(()), token_gradient.reshape(tokens.shape), *results)


def solution(mesh):
    in_specs = (
        P(None, "dp", None, None),
        P(None, "dp"),
        P(),
        P(),
        P(),
        P("dp", None, "mp"),
        P("dp", "mp"),
        P("dp", "mp"),
        P("dp", "mp"),
        P("dp", None),
        P("dp", None),
        P(None, "mp"),
        P("dp", None, "mp"),
        P("dp", "mp"),
        P("dp", "mp"),
        P("dp", "mp"),
        P("dp", None),
        P("dp", None),
        P(None, "mp"),
        P("dp", None, "mp"),
        P("dp", "mp"),
        P("dp", "mp"),
        P("dp", "mp"),
        P("dp", None),
        P("dp", None),
        P(None, "mp"),
    )
    out_specs = (
        P(),
        P(None, "dp", None, None),
        P("dp", None, "mp"),
        P("dp", "mp"),
        P("dp", "mp"),
        P("dp", "mp"),
        P("dp", None),
        P("dp", None),
        P(None, "mp"),
        P("dp", None, "mp"),
        P("dp", "mp"),
        P("dp", "mp"),
        P("dp", "mp"),
        P("dp", None),
        P("dp", None),
        P(None, "mp"),
        P("dp", None, "mp"),
        P("dp", "mp"),
        P("dp", "mp"),
        P("dp", "mp"),
        P("dp", None),
        P("dp", None),
        P(None, "mp"),
    )
    return jax.shard_map(body, mesh=mesh, in_specs=in_specs, out_specs=out_specs, check_vma=False)
```

profile of v0, /device:TPU:0, one launch (start us, length us, event | category | flops | bytes accessed | tf_op | source)
XLA Modules:
  0.0 205.4 jit_solution(16690443962320532572)
XLA Ops:
  0.7 1.8 pack_heads.1.refs_0_
  2.5 5.0 %collective-permute-start.2 = (bf16[48,1664]{1,0:T(8,128)(2,1)}, bf16[48,1664]{1,0:T(8,128)(2,1)S(1)}, u32[]{:S(2)}, u32[]{:S(2)}) collective-permute-start(bf16[48,1664]{1,0:T(8,128)(2,1)} %pack_heads.1.refs_0_), channel_id=1, source_target_pairs={{0,24},{2,26},{4,28},{6,30},{8,16},{10,18},{12,20},{14,22},{16,8},... | collective-permute-start | bytes 479240 | tf_op jit(solution)/shard_map/heads_across_12/ppermute | solution.py:140
  13.0 1.4 prepare.1
  14.4 3.3 %stage.1 = (f32[3,48,384]{2,1,0:T(8,128)}, f32[48,384]{1,0:T(8,128)}, f32[48,1536]{1,0:T(8,128)}, f32[48,1536]{1,0:T(8,128)}, f32[3,48,384]{2,1,0:T(8,128)}, /*i...) custom-call(f32[3,48,384]{2,1,0:T(8,128)} %bitcast.37, ...), custom_call_target="tpu_custom_call" | custom-call | tf_op jit(solution)/shard_map/stage/pallas_call | solution.py:78
  17.8 3.5 %collective-permute-done.refs_1_ = bf16[48,1664]{1,0:T(8,128)(2,1)S(1)} collective-permute-done((bf16[48,1664]{1,0:T(8,128)(2,1)}, bf16[48,1664]{1,0:T(8,128)(2,1)S(1)}, u32[]{:S(2)}, u32[]{:S(2)}) %collective-permute-start) | collective-permute-done | bytes 159776 | tf_op jit(solution)/shard_map/heads_across_8/ppermute | solution.py:140
  22.3 1.6 collective-permute-start.4
  23.8 1.5 collective-permute-start.3
  25.6 1.9 order_tokens.1.refs_2_.refs_0_.refs_1_.refs_3_
  27.5 5.9 %collective-permute-done.5.refs_1_ = bf16[48,1536]{1,0:T(8,128)(2,1)S(1)} collective-permute-done((bf16[48,1536]{1,0:T(8,128)(2,1)S(1)}, bf16[48,1536]{1,0:T(8,128)(2,1)S(1)}, u32[]{:S(2)}, u32[]{:S(2)}) %collective-permute-start.5) | collective-permute-done | bytes 147488 | tf_op jit(solution)/shard_map/up_across_8/ppermute | solution.py:140
  33.5 4.3 %collective-permute-done.4.refs_1_.refs_3_.refs_12_ = bf16[192,1664]{1,0:T(8,128)(2,1)S(1)} collective-permute-done((bf16[192,1664]{1,0:T(8,128)(2,1)S(1)}, bf16[192,1664]{1,0:T(8,128)(2,1)S(1)}, u32[]{:S(2)}, u32[]{:S(2)}) %collective-permute-start.4) | collective-permute-done | bytes 639008 | tf_op jit(solution)/shard_map/heads_across_1/ppermute | solution.py:140
  37.8 1.2 collective-permute-done.3.refs_0_.refs_2_.refs_11_
  39.1 1.6 collective-permute-start.7
  41.2 1.5 collective-permute-done.9.refs_1_
  42.8 3.8 %collective-permute-done.8.refs_1_ = bf16[48,1536]{1,0:T(8,128)(2,1)S(1)} collective-permute-done((bf16[48,1536]{1,0:T(8,128)(2,1)S(1)}, bf16[48,1536]{1,0:T(8,128)(2,1)S(1)}, u32[]{:S(2)}, u32[]{:S(2)}) %collective-permute-start.8) | collective-permute-done | bytes 147488 | tf_op jit(solution)/shard_map/down_across_8/ppermute | solution.py:140
  47.4 1.5 collective-permute-start.10
  48.9 3.6 %projection.1 = (bf16[3,3,1024,128]{3,2,1,0:T(8,128)(2,1)S(1)}, bf16[1024,768]{1,0:T(8,128)(2,1)S(1)}, f32[8,768]{1,0:T(8,128)S(1)}) custom-call(bf16[1024,768]{1,0:T(8,128)(2,1)S(1)} %order_tokens.1.refs_2_.refs_0_.refs_1_.refs_3_, bf16[192,1664]{1,0:T(8,128)(2,1)S(1)} %get-tuple-element.149.refs_1_.refs_10_, ...), custom_call_target="tpu_custom_call" | custom-call | tf_op jit(solution)/shard_map/projection/pallas_call | solution.py:78
  52.5 3.5 %attention_forward.2 = (bf16[1024,384]{1,0:T(8,128)(2,1)S(1)}, bf16[3,2,2,512,512]{4,3,2,1,0:T(8,128)(2,1)S(1)}, f32[1024,384]{1,0:T(8,128)S(1)}) custom-call(s32[2]{0:T(128)S(1)} %bitcast.49, f32[3,2,1024]{2,1,0:T(2,128)S(1)} %get-tuple-element.145.refs_1_, bf16[3,3,1024,128]{3,2,1,0:T(8,128)(2,1)S(1)} %get-tuple-element.155.refs_2_.refs_1_), custom_call_target="tpu_custom_call" | custom-call | tf_op jit(solution)/shard_map/attention_forward/pallas_call | solution.py:78
  56.0 1.5 collective-permute-start.14
  58.6 6.5 %attention_forward.3 = (bf16[1024,384]{1,0:T(8,128)(2,1)S(1)}, bf16[3,2,2,512,512]{4,3,2,1,0:T(8,128)(2,1)S(1)}, f32[1024,384]{1,0:T(8,128)S(1)}) custom-call(s32[2]{0:T(128)S(1)} %bitcast.50, f32[3,2,1024]{2,1,0:T(2,128)S(1)} %get-tuple-element.145.refs_1_, ...), custom_call_target="tpu_custom_call", output_to_operand_aliasing={{0}: (3, {}), {1}: (4, {}), {2}: (5, {})} | custom-call | tf_op jit(solution)/shard_map/attention_forward/pallas_call | solution.py:78
  65.1 8.4 %collective-permute-done.14.refs_8_.refs_1_.refs_3_ = bf16[192,1536]{1,0:T(8,128)(2,1)S(1)} collective-permute-done((bf16[192,1536]{1,0:T(8,128)(2,1)S(1)}, bf16[192,1536]{1,0:T(8,128)(2,1)S(1)}, u32[]{:S(2)}, u32[]{:S(2)}) %collective-permute-start.14) | collective-permute-done | bytes 589856 | tf_op jit(solution)/shard_map/down_across_1/ppermute | solution.py:140
  73.8 1.4 branch.1.refs_2_
  75.3 1.6 collective-permute-start.17
  76.9 1.4 collective-permute-start.16
  79.5 5.6 %collective-permute-done.17.refs_9_ = bf16[96,1536]{1,0:T(8,128)(2,1)S(1)} collective-permute-done((bf16[96,1536]{1,0:T(8,128)(2,1)S(1)}, bf16[96,1536]{1,0:T(8,128)(2,1)S(1)}, u32[]{:S(2)}, u32[]{:S(2)}) %collective-permute-start.17) | collective-permute-done | bytes 294944 | tf_op jit(solution)/shard_map/up_corner_across_2/ppermute | solution.py:140
  85.1 1.6 collective-permute-done.16.refs_8_
  86.8 7.6 %hidden_forward.1 = (bf16[1024,768]{1,0:T(8,128)(2,1)S(1)}, bf16[1024,1536]{1,0:T(8,128)(2,1)S(1)}, f32[2,1,1536]{2,1,0:T(1,128)S(1)}, f32[2,1,768]{2,1,0:T(1,128)S(1)}, bf16[768,1536]{1,0:T(8,128)(2,1)S(1)}) custom-call(s32[2]{0:T(128)S(1)} %bitcast.51, bf16[1024,768]{1,0:T(8,128)(2,1)S(1)} %order_tokens.1.refs_2_.refs_0_.refs_1_.refs_3_, ...), custom_call_target="tpu_custom_call" | custom-call | flops 2400000000 | bytes 20000000 | tf_op jit(solution)/shard_map/hidden_forward/pallas_call | solution.py:78
  95.2 1.2 collective-permute-done.20.refs_2_
  97.1 2.4 %collective-permute-start.23 = (f32[1,8,768]{2,1,0:T(8,128)S(1)}, f32[1,8,768]{2,1,0:T(8,128)S(1)}, u32[]{:S(2)}, u32[]{:S(2)}) collective-permute-start(f32[1,8,768]{2,1,0:T(8,128)S(1)} %bitcast.39), channel_id=1, source_target_pairs={{0,24},{2,26},{4,28},{6,30},{8,16},{10,18},{12,20},{14,22},{16,8},... | collective-permute-start | bytes 73736 | tf_op jit(solution)/shard_map/small_sums_across_12/ppermute | solution.py:140
  100.3 1.2 collective-permute-start.21
  101.5 1.2 collective-permute-done.23.refs_3_
  103.3 1.7 collective-permute-done.21.refs_1_
  105.0 1.2 collective-permute-start.26
  106.8 1.7 collective-permute-start.24
  108.6 2.0 collective-permute-done.26.refs_10_.refs_3_
  111.6 4.4 %rank_backward.1 = (f32[8,768]{1,0:T(8,128)S(1)}, f32[8,1536]{1,0:T(8,128)}, f32[2,16,128]{2,1,0:T(8,128)S(1)}, bf16[1024,1536]{1,0:T(8,128)(2,1)S(1)}, bf16[1024,768]{1,0:T(8,128)(2,1)S(1)}) custom-call(s32[2]{0:T(128)S(1)} %bitcast.53, f32[2,16,128]{2,1,0:T(8,128)S(1)} %get-tuple-element.170.refs_1_, f32[2,16,128]{2,1,0:T(8,128)S(1)} %get-tuple-element.171.refs_2_, ...), custom_call_target="tpu_custom_call" | custom-call | flops 2400000000 | bytes 20000000 | tf_op jit(solution)/shard_map/rank_backward/pallas_call | solution.py:78
  116.1 2.6 %hidden_in_gradient.1 = (bf16[192,1536]{1,0:T(8,128)(2,1)S(1)}, bf16[192,1536]{1,0:T(8,128)(2,1)S(1)}, bf16[192,1536]{1,0:T(8,128)(2,1)S(1)}, bf16[96,1536]{1,0:T(8,128)(2,1)S(1)}, bf16[96,1536]{1,0:T(8,128)(2,1)S(1)}) custom-call(bf16[1024,768]{1,0:T(8,128)(2,1)S(1)} %get-tuple-element.192.refs_0_, bf16[1024,1536]{1,0:T(8,128)(2,1)S(1)} %get-tuple-element.193.refs_1_), custom_call_target="tpu_custom_call" | custom-call | flops 2400000000 | bytes 15000000 | tf_op jit(solution)/shard_map/hidden_in_gradient/pallas_call | solution.py:78
  118.7 1.5 collective-permute-start.32
  120.3 1.5 collective-permute-start.33
  121.8 4.4 %middle_backward.1 = (f32[1024,768]{1,0:T(8,128)S(1)}, bf16[1024,384]{1,0:T(8,128)(2,1)S(1)}, f32[768,384]{1,0:T(8,128)S(1)}) custom-call(s32[2]{0:T(128)S(1)} %bitcast.54, bf16[1024,768]{1,0:T(8,128)(2,1)S(1)} %order_tokens.1.refs_2_.refs_0_.refs_1_.refs_3_, bf16[1024,768]{1,0:T(8,128)(2,1)S(1)} %branch.1.refs_2_, ...), custom_call_target="tpu_custom_call" | custom-call | flops 1200000000 | bytes 15000000 | tf_op jit(solution)/shard_map/middle_backward/pallas_call | solution.py:78
  126.2 2.0 collective-permute-done.32.refs_2_
  128.2 1.2 collective-permute-done.33.refs_3_
  129.5 1.6 collective-permute-start.34
  131.7 8.7 %attention_backward.2 = (bf16[3,3,1024,128]{3,2,1,0:T(8,128)(2,1)S(1)}, f32[2,8,128]{2,1,0:T(8,128)S(1)}, bf16[192,1152]{1,0:T(8,128)(2,1)S(1)}, bf16[192,1152]{...) custom-call(bf16[3,2,2,512,512]{4,3,2,1,0:T(8,128)(2,1)S(1)} %get-tu, ...), custom_call_target="tpu_custom_call" | custom-call | tf_op jit(solution)/shard_map/attention_backward/pallas_call | solution.py:78
  140.5 4.3 %attention_backward.3 = (bf16[3,3,1024,128]{3,2,1,0:T(8,128)(2,1)S(1)}, f32[1,8,128]{2,1,0:T(8,128)S(1)}, bf16[192,512]{1,0:T(8,128)(2,1)S(1)}, bf16[192,512]{1,...) custom-call(bf16[3,2,2,512,512]{4,3,2,1,0:T(8,128)(2,1)S(1)} %get-tu, ...), custom_call_target="tpu_custom_call", output_to_operand_aliasing={{0}: (7, {})} | custom-call | tf_op jit(solution)/shard_map/attention_backward/pallas_call | solution.py:78
  145.7 1.3 collective-permute-start.36
  148.2 1.3 collective-permute-start.30
  149.5 1.5 collective-permute-start.31
  151.1 3.3 %collective-permute-done.30.refs_6_ = bf16[96,512]{1,0:T(8,128)(2,1)S(1)} collective-permute-done((bf16[96,512]{1,0:T(8,128)(2,1)S(1)}, bf16[96,512]{1,0:T(8,128)(2,1)S(1)}, u32[]{:S(2)}, u32[]{:S(2)}) %collective-permute-start.30) | collective-permute-done | bytes 98336 | tf_op jit(solution)/shard_map/late_gradient_across_1/ppermute | solution.py:140
  157.9 3.2 %normed_backward.1.refs_5_ = bf16[1024,768]{1,0:T(8,128)(2,1)S(1)} custom-call(bf16[3,3,1024,128]{3,2,1,0:T(8,128)(2,1)S(1)} %get-tuple-element.210.refs_0_, bf16[192,1664]{1,0:T(8,128)(2,1)S(1)} %get-tuple-element.149.refs_1_.refs_10_, bf16[192,1664]{1,0:T(8,128)(2,1)S(1)} %collective-permute-done.3.refs_0_.refs_2_.refs_11_, ...), custom_call_target="tpu_custom_call" | custom-call | flops 1800000000 | bytes 15000000 | tf_op jit(solution)/shard_map/normed_backward/pallas_call | solution.py:78
  161.1 3.6 %collective-permute-done.39.refs_4_.refs_11_ = bf16[48,1536]{1,0:T(8,128)(2,1)S(1)} collective-permute-done((bf16[48,1536]{1,0:T(8,128)(2,1)S(1)}, bf16[48,1536]{1,0:T(8,128)(2,1)S(1)}, u32[]{:S(2)}, u32[]{:S(2)}) %collective-permute-start.39) | collective-permute-done | bytes 147488 | tf_op jit(solution)/shard_map/up_gradient_across_8/ppermute | solution.py:140
  165.6 1.6 collective-permute-start.43
  169.0 5.1 %token_gradient.1 = (f32[1024,768]{1,0:T(8,128)}, f32[8,128]{1,0:T(8,128)S(1)}) custom-call(f32[1024,768]{1,0:T(8,128)S(1)} %get-tuple-element.213.refs_0_, bf16[1024,768]{1,0:T(8,128)(2,1)S(1)} %get-tuple-element.214.refs_1_, bf16[1024,768]{1,0:T(8,128)(2,1)S(1)} %collective-permute-done.41.refs_2_, ...), custom_call_target="tpu_custom_call" | custom-call | flops 2400000000 | bytes 15000000 | tf_op jit(solution)/shard_map/token_gradient/pallas_call | solution.py:78
  176.2 2.3 %collective-permute-start.45 = (bf16[48,512]{1,0:T(8,128)(2,1)S(1)}, bf16[48,512]{1,0:T(8,128)(2,1)S(1)}, u32[]{:S(2)}, u32[]{:S(2)}) collective-permute-start(bf16[48,512]{1,0:T(8,128)(2,1)S(1)} %get-tuple-element.220), channel_id=1, source_target_pairs={{0,16},{2,18},{4,20},{6,22},{8,24},{10,26},{12,28},{14,30},{16,0},... | collective-permute-start | bytes 147464 | tf_op jit(solution)/shard_map/late_gradient_across_8/ppermute | solution.py:140
  179.2 1.4 collective-permute-start.47
  180.6 5.7 %collective-permute-done.45.refs_7_ = bf16[48,512]{1,0:T(8,128)(2,1)S(1)} collective-permute-done((bf16[48,512]{1,0:T(8,128)(2,1)S(1)}, bf16[48,512]{1,0:T(8,128)(2,1)S(1)}, u32[]{:S(2)}, u32[]{:S(2)}) %collective-permute-start.45) | collective-permute-done | bytes 49184 | tf_op jit(solution)/shard_map/late_gradient_across_8/ppermute | solution.py:140
  186.4 1.3 gradient_totals.1
  187.8 1.2 collective-permute-done.48.refs_1_
  189.0 1.6 collective-permute-start.51
  190.8 2.6 %collective-permute-start.49 = (f32[1,24,128]{2,1,0:T(8,128)S(1)}, f32[1,24,128]{2,1,0:T(8,128)S(1)}, u32[]{:S(2)}, u32[]{:S(2)}) collective-permute-start(f32[1,24,128]{2,1,0:T(8,128)S(1)} %bitcast.57), channel_id=1, source_target_pairs={{0,16},{2,18},{4,20},{6,22},{8,24},{10,26},{12,28},{14,30},{16,0},... | collective-permute-start | bytes 36872 | tf_op jit(solution)/shard_map/squares_across_8/ppermute | solution.py:140
  195.5 1.5 collective-permute-start.54
  197.0 1.4 collective-permute-start.53
  199.0 1.5 collective-permute-done.54.refs_6_
  201.1 1.4 collective-permute-done.52.refs_4_
  202.7 2.5 %update.1 = (f32[1,1]{1,0:T(1,128)}, f32[3,48,384]{2,1,0:T(8,128)}, f32[48,384]{1,0:T(8,128)}, f32[48,1536]{1,0:T(8,128)}, f32[48,1536]{1,0:T(8,128)}, /*index=5...) custom-call(s32[1]{0:T(128)} %bitcast.refs_0_, ...), custom_call_target="tpu_custom_call" | custom-call | bytes 6000000 | tf_op jit(solution)/shard_map/update/pallas_call | solution.py:78
  (150 shorter events, 30.0 us)
Async XLA Ops:
  2.5 15.3 %collective-permute-start.2 = (bf16[48,1664]{1,0:T(8,128)(2,1)}, bf16[48,1664]{1,0:T(8,128)(2,1)S(1)}, u32[]{:S(2)}, u32[]{:S(2)}) collective-permute-start(bf16[48,1664]{1,0:T(8,128)(2,1)} %pack_heads.1.refs_0_), channel_id=1, source_target_pairs={{0,24},{2,26},{4,28},{6,30},{8,16},{10,18},{12,20},{14,22},{16,8},... | collective-permute-start | bytes 479240 | tf_op jit(solution)/shard_map/heads_across_12/ppermute | solution.py:140
  7.5 10.3 %collective-permute-start.1 = (bf16[48,1664]{1,0:T(8,128)(2,1)}, bf16[48,1664]{1,0:T(8,128)(2,1)S(1)}, u32[]{:S(2)}, u32[]{:S(2)}) collective-permute-start(bf16[48,1664]{1,0:T(8,128)(2,1)} %pack_heads.1.refs_0_), channel_id=1, source_target_pairs={{0,8},{2,10},{4,12},{6,14},{8,0},{10,2},{12,4},{14,6},{16,24},{18,... | collective-permute-start | bytes 479240 | tf_op jit(solution)/shard_map/heads_across_4/ppermute | solution.py:140
  7.5 13.7 %collective-permute-start = (bf16[48,1664]{1,0:T(8,128)(2,1)}, bf16[48,1664]{1,0:T(8,128)(2,1)S(1)}, u32[]{:S(2)}, u32[]{:S(2)}) collective-permute-start(bf16[48,1664]{1,0:T(8,128)(2,1)} %pack_heads.1.refs_0_), channel_id=1, source_target_pairs={{0,16},{2,18},{4,20},{6,22},{8,24},{10,26},{12,28},{14,30},{16,0},... | collective-permute-start | bytes 479240 | tf_op jit(solution)/shard_map/heads_across_8/ppermute | solution.py:140
  22.3 15.5 %collective-permute-start.4 = (bf16[192,1664]{1,0:T(8,128)(2,1)S(1)}, bf16[192,1664]{1,0:T(8,128)(2,1)S(1)}, u32[]{:S(2)}, u32[]{:S(2)}) collective-permute-start(bf16[192,1664]{1,0:T(8,128)(2,1)S(1)} %get-tuple-element.149.refs_1_.refs_10_), channel_id=1, source_target_pairs={{0,2},{2,0},{4,6},{6,4},{8,10},{10,8},{12,14},{14,12},{16,18},{18,... | collective-permute-start | bytes 1916936 | tf_op jit(solution)/shard_map/heads_across_1/ppermute | solution.py:140
  23.8 15.2 %collective-permute-start.3 = (bf16[192,1664]{1,0:T(8,128)(2,1)S(1)}, bf16[192,1664]{1,0:T(8,128)(2,1)S(1)}, u32[]{:S(2)}, u32[]{:S(2)}) collective-permute-start(bf16[192,1664]{1,0:T(8,128)(2,1)S(1)} %get-tuple-element.149.refs_1_.refs_10_), channel_id=1, source_target_pairs={{0,4},{2,6},{4,0},{6,2},{8,12},{10,14},{12,8},{14,10},{16,20},{18,... | collective-permute-start | bytes 1916936 | tf_op jit(solution)/shard_map/heads_across_2/ppermute | solution.py:140
  25.3 8.0 %collective-permute-start.5 = (bf16[48,1536]{1,0:T(8,128)(2,1)S(1)}, bf16[48,1536]{1,0:T(8,128)(2,1)S(1)}, u32[]{:S(2)}, u32[]{:S(2)}) collective-permute-start(bf16[48,1536]{1,0:T(8,128)(2,1)S(1)} %get-tuple-element.150.refs_0_), channel_id=1, source_target_pairs={{0,16},{2,18},{4,20},{6,22},{8,24},{10,26},{12,28},{14,30},{16,0},... | collective-permute-start | bytes 442376 | tf_op jit(solution)/shard_map/up_across_8/ppermute | solution.py:140
  33.4 9.3 %collective-permute-start.9 = (bf16[96,1536]{1,0:T(8,128)(2,1)S(1)}, bf16[96,1536]{1,0:T(8,128)(2,1)S(1)}, u32[]{:S(2)}, u32[]{:S(2)}) collective-permute-start(bf16[96,1536]{1,0:T(8,128)(2,1)S(1)} %join.8.refs_2_.refs_0_), channel_id=1, source_target_pairs={{0,8},{2,10},{4,12},{6,14},{8,0},{10,2},{12,4},{14,6},{16,24},{18,... | collective-permute-start | bytes 884744 | tf_op jit(solution)/shard_map/up_across_4/ppermute | solution.py:140
  39.0 7.6 %collective-permute-start.8 = (bf16[48,1536]{1,0:T(8,128)(2,1)S(1)}, bf16[48,1536]{1,0:T(8,128)(2,1)S(1)}, u32[]{:S(2)}, u32[]{:S(2)}) collective-permute-start(bf16[48,1536]{1,0:T(8,128)(2,1)S(1)} %get-tuple-element.154.refs_0_), channel_id=1, source_target_pairs={{0,16},{2,18},{4,20},{6,22},{8,24},{10,26},{12,28},{14,30},{16,0},... | collective-permute-start | bytes 442376 | tf_op jit(solution)/shard_map/down_across_8/ppermute | solution.py:140
  39.1 9.8 %collective-permute-start.7 = (bf16[96,1664]{1,0:T(8,128)(2,1)S(1)}, bf16[96,1664]{1,0:T(8,128)(2,1)S(1)}, u32[]{:S(2)}, u32[]{:S(2)}) collective-permute-start(bf16[96,1664]{1,0:T(8,128)(2,1)S(1)} %get-tuple-element.153), channel_id=1, source_target_pairs={{0,4},{2,6},{4,0},{6,2},{8,12},{10,14},{12,8},{14,10},{16,20},{18,... | collective-permute-start | bytes 958472 | tf_op jit(solution)/shard_map/heads_corner_across_2/ppermute | solution.py:140
  40.7 8.2 %collective-permute-start.6 = (bf16[96,1664]{1,0:T(8,128)(2,1)S(1)}, bf16[96,1664]{1,0:T(8,128)(2,1)S(1)}, u32[]{:S(2)}, u32[]{:S(2)}) collective-permute-start(bf16[96,1664]{1,0:T(8,128)(2,1)S(1)} %get-tuple-element.152.refs_2_), channel_id=1, source_target_pairs={{0,2},{2,0},{4,6},{6,4},{8,10},{10,8},{12,14},{14,12},{16,18},{18,... | collective-permute-start | bytes 958472 | tf_op jit(solution)/shard_map/heads_corner_across_1/ppermute | solution.py:140
  46.7 9.3 %collective-permute-start.12 = (bf16[96,1536]{1,0:T(8,128)(2,1)S(1)}, bf16[96,1536]{1,0:T(8,128)(2,1)S(1)}, u32[]{:S(2)}, u32[]{:S(2)}) collective-permute-start(bf16[96,1536]{1,0:T(8,128)(2,1)S(1)} %join.10.refs_6_.refs_0_), channel_id=1, source_target_pairs={{0,8},{2,10},{4,12},{6,14},{8,0},{10,2},{12,4},{14,6},{16,24},{18,... | collective-permute-start | bytes 884744 | tf_op jit(solution)/shard_map/down_across_4/ppermute | solution.py:140
  46.7 18.3 %collective-permute-start.11 = (bf16[192,1536]{1,0:T(8,128)(2,1)S(1)}, bf16[192,1536]{1,0:T(8,128)(2,1)S(1)}, u32[]{:S(2)}, u32[]{:S(2)}) collective-permute-start(bf16[192,1536]{1,0:T(8,128)(2,1)S(1)} %join.9.refs_2_.refs_5_), channel_id=1, source_target_pairs={{0,2},{2,0},{4,6},{6,4},{8,10},{10,8},{12,14},{14,12},{16,18},{18,... | collective-permute-start | bytes 1769480 | tf_op jit(solution)/shard_map/up_across_1/ppermute | solution.py:140
  47.4 17.7 %collective-permute-start.10 = (bf16[192,1536]{1,0:T(8,128)(2,1)S(1)}, bf16[192,1536]{1,0:T(8,128)(2,1)S(1)}, u32[]{:S(2)}, u32[]{:S(2)}) collective-permute-start(bf16[192,1536]{1,0:T(8,128)(2,1)S(1)} %join.9.refs_2_.refs_5_), channel_id=1, source_target_pairs={{0,4},{2,6},{4,0},{6,2},{8,12},{10,14},{12,8},{14,10},{16,20},{18,... | collective-permute-start | bytes 1769480 | tf_op jit(solution)/shard_map/up_across_2/ppermute | solution.py:140
  56.0 17.5 %collective-permute-start.14 = (bf16[192,1536]{1,0:T(8,128)(2,1)S(1)}, bf16[192,1536]{1,0:T(8,128)(2,1)S(1)}, u32[]{:S(2)}, u32[]{:S(2)}) collective-permute-start(bf16[192,1536]{1,0:T(8,128)(2,1)S(1)} %join.11.refs_1_), channel_id=1, source_target_pairs={{0,2},{2,0},{4,6},{6,4},{8,10},{10,8},{12,14},{14,12},{16,18},{18,... | collective-permute-start | bytes 1769480 | tf_op jit(solution)/shard_map/down_across_1/ppermute | solution.py:140
  57.6 16.3 %collective-permute-start.13 = (bf16[192,1536]{1,0:T(8,128)(2,1)S(1)}, bf16[192,1536]{1,0:T(8,128)(2,1)S(1)}, u32[]{:S(2)}, u32[]{:S(2)}) collective-permute-start(bf16[192,1536]{1,0:T(8,128)(2,1)S(1)} %join.11.refs_1_), channel_id=1, source_target_pairs={{0,4},{2,6},{4,0},{6,2},{8,12},{10,14},{12,8},{14,10},{16,20},{18,... | collective-permute-start | bytes 1769480 | tf_op jit(solution)/shard_map/down_across_2/ppermute | solution.py:140
  75.2 11.6 %collective-permute-start.15 = (bf16[1024,768]{1,0:T(8,128)(2,1)S(1)}, bf16[1024,768]{1,0:T(8,128)(2,1)S(1)}, u32[]{:S(2)}, u32[]{:S(2)}) collective-permute-start(bf16[1024,768]{1,0:T(8,128)(2,1)S(1)} %branch.1.refs_2_), channel_id=1, source_target_pairs={{0,1},{1,0},{2,3},{3,2},{4,5},{5,4},{6,7},{7,6},{8,9},{9,8},{10,11... | collective-permute-start | bytes 4718600 | tf_op jit(solution)/shard_map/branch_other_core/ppermute | solution.py:149
  75.3 9.9 %collective-permute-start.17 = (bf16[96,1536]{1,0:T(8,128)(2,1)S(1)}, bf16[96,1536]{1,0:T(8,128)(2,1)S(1)}, u32[]{:S(2)}, u32[]{:S(2)}) collective-permute-start(bf16[96,1536]{1,0:T(8,128)(2,1)S(1)} %get-tuple-element.163), channel_id=1, source_target_pairs={{0,4},{2,6},{4,0},{6,2},{8,12},{10,14},{12,8},{14,10},{16,20},{18,... | collective-permute-start | bytes 884744 | tf_op jit(solution)/shard_map/up_corner_across_2/ppermute | solution.py:140
  76.9 9.9 %collective-permute-start.16 = (bf16[96,1536]{1,0:T(8,128)(2,1)S(1)}, bf16[96,1536]{1,0:T(8,128)(2,1)S(1)}, u32[]{:S(2)}, u32[]{:S(2)}) collective-permute-start(bf16[96,1536]{1,0:T(8,128)(2,1)S(1)} %get-tuple-element.160.refs_6_), channel_id=1, source_target_pairs={{0,2},{2,0},{4,6},{6,4},{8,10},{10,8},{12,14},{14,12},{16,18},{18,... | collective-permute-start | bytes 884744 | tf_op jit(solution)/shard_map/up_corner_across_1/ppermute | solution.py:140
  78.4 16.0 %collective-permute-start.18 = (bf16[96,1536]{1,0:T(8,128)(2,1)S(1)}, bf16[96,1536]{1,0:T(8,128)(2,1)S(1)}, u32[]{:S(2)}, u32[]{:S(2)}) collective-permute-start(bf16[96,1536]{1,0:T(8,128)(2,1)S(1)} %get-tuple-element.165), channel_id=1, source_target_pairs={{0,2},{2,0},{4,6},{6,4},{8,10},{10,8},{12,14},{14,12},{16,18},{18,... | collective-permute-start | bytes 884744 | tf_op jit(solution)/shard_map/down_corner_across_1/ppermute | solution.py:140
  79.0 15.4 %collective-permute-start.19 = (bf16[96,1536]{1,0:T(8,128)(2,1)S(1)}, bf16[96,1536]{1,0:T(8,128)(2,1)S(1)}, u32[]{:S(2)}, u32[]{:S(2)}) collective-permute-start(bf16[96,1536]{1,0:T(8,128)(2,1)S(1)} %get-tuple-element.166), channel_id=1, source_target_pairs={{0,4},{2,6},{4,0},{6,2},{8,12},{10,14},{12,8},{14,10},{16,20},{18,... | collective-permute-start | bytes 884744 | tf_op jit(solution)/shard_map/down_corner_across_2/ppermute | solution.py:140
  95.1 1.2 collective-permute-start.20
  97.1 5.6 %collective-permute-start.23 = (f32[1,8,768]{2,1,0:T(8,128)S(1)}, f32[1,8,768]{2,1,0:T(8,128)S(1)}, u32[]{:S(2)}, u32[]{:S(2)}) collective-permute-start(f32[1,8,768]{2,1,0:T(8,128)S(1)} %bitcast.39), channel_id=1, source_target_pairs={{0,24},{2,26},{4,28},{6,30},{8,16},{10,18},{12,20},{14,22},{16,8},... | collective-permute-start | bytes 73736 | tf_op jit(solution)/shard_map/small_sums_across_12/ppermute | solution.py:140
  99.5 3.8 %collective-permute-start.22 = (f32[1,8,768]{2,1,0:T(8,128)S(1)}, f32[1,8,768]{2,1,0:T(8,128)S(1)}, u32[]{:S(2)}, u32[]{:S(2)}) collective-permute-start(f32[1,8,768]{2,1,0:T(8,128)S(1)} %bitcast.40), channel_id=1, source_target_pairs={{0,8},{2,10},{4,12},{6,14},{8,0},{10,2},{12,4},{14,6},{16,24},{18,... | collective-permute-start | bytes 73736 | tf_op jit(solution)/shard_map/small_sums_across_4/ppermute | solution.py:140
  100.3 4.7 %collective-permute-start.21 = (f32[1,8,768]{2,1,0:T(8,128)S(1)}, f32[1,8,768]{2,1,0:T(8,128)S(1)}, u32[]{:S(2)}, u32[]{:S(2)}) collective-permute-start(f32[1,8,768]{2,1,0:T(8,128)S(1)} %bitcast.41), channel_id=1, source_target_pairs={{0,16},{2,18},{4,20},{6,22},{8,24},{10,26},{12,28},{14,30},{16,0},... | collective-permute-start | bytes 73736 | tf_op jit(solution)/shard_map/small_sums_across_8/ppermute | solution.py:140
  105.0 5.6 %collective-permute-start.26 = (f32[4,8,768]{2,1,0:T(8,128)S(1)}, f32[4,8,768]{2,1,0:T(8,128)S(1)}, u32[]{:S(2)}, u32[]{:S(2)}) collective-permute-start(f32[4,8,768]{2,1,0:T(8,128)S(1)} %join.12.refs_7_.refs_0_), channel_id=1, source_target_pairs={{0,6},{2,4},{4,2},{6,0},{8,14},{10,12},{12,10},{14,8},{16,22},{18,... | collective-permute-start | bytes 294920 | tf_op jit(solution)/shard_map/small_sums_across_3/ppermute | solution.py:140
  106.2 4.6 %collective-permute-start.25 = (f32[4,8,768]{2,1,0:T(8,128)S(1)}, f32[4,8,768]{2,1,0:T(8,128)S(1)}, u32[]{:S(2)}, u32[]{:S(2)}) collective-permute-start(f32[4,8,768]{2,1,0:T(8,128)S(1)} %join.12.refs_7_.refs_0_), channel_id=1, source_target_pairs={{0,2},{2,0},{4,6},{6,4},{8,10},{10,8},{12,14},{14,12},{16,18},{18,... | collective-permute-start | bytes 294920 | tf_op jit(solution)/shard_map/small_sums_across_1/ppermute | solution.py:140
  106.8 4.8 %collective-permute-start.24 = (f32[4,8,768]{2,1,0:T(8,128)S(1)}, f32[4,8,768]{2,1,0:T(8,128)S(1)}, u32[]{:S(2)}, u32[]{:S(2)}) collective-permute-start(f32[4,8,768]{2,1,0:T(8,128)S(1)} %join.12.refs_7_.refs_0_), channel_id=1, source_target_pairs={{0,4},{2,6},{4,0},{6,2},{8,12},{10,14},{12,8},{14,10},{16,20},{18,... | collective-permute-start | bytes 294920 | tf_op jit(solution)/shard_map/small_sums_across_2/ppermute | solution.py:140
  116.0 5.8 %collective-permute-start.27 = (bf16[1024,768]{1,0:T(8,128)(2,1)S(1)}, bf16[1024,768]{1,0:T(8,128)(2,1)S(1)}, u32[]{:S(2)}, u32[]{:S(2)}) collective-permute-start(bf16[1024,768]{1,0:T(8,128)(2,1)S(1)} %get-tuple-element.175.refs_4_), channel_id=1, source_target_pairs={{0,1},{1,0},{2,3},{3,2},{4,5},{5,4},{6,7},{7,6},{8,9},{9,8},{10,11... | collective-permute-start | bytes 4718600 | tf_op jit(solution)/shard_map/second_gradient_other_core/ppermute | solution.py:149
  118.7 9.5 %collective-permute-start.32 = (bf16[96,1536]{1,0:T(8,128)(2,1)S(1)}, bf16[96,1536]{1,0:T(8,128)(2,1)S(1)}, u32[]{:S(2)}, u32[]{:S(2)}) collective-permute-start(bf16[96,1536]{1,0:T(8,128)(2,1)S(1)} %get-tuple-element.197), channel_id=1, source_target_pairs={{0,2},{2,0},{4,6},{6,4},{8,10},{10,8},{12,14},{14,12},{16,18},{18,... | collective-permute-start | bytes 884744 | tf_op jit(solution)/shard_map/up_gradient_across_1/ppermute | solution.py:140
  120.3 9.1 %collective-permute-start.33 = (bf16[96,1536]{1,0:T(8,128)(2,1)S(1)}, bf16[96,1536]{1,0:T(8,128)(2,1)S(1)}, u32[]{:S(2)}, u32[]{:S(2)}) collective-permute-start(bf16[96,1536]{1,0:T(8,128)(2,1)S(1)} %get-tuple-element.198), channel_id=1, source_target_pairs={{0,4},{2,6},{4,0},{6,2},{8,12},{10,14},{12,8},{14,10},{16,20},{18,... | collective-permute-start | bytes 884744 | tf_op jit(solution)/shard_map/up_gradient_across_2/ppermute | solution.py:140
  129.5 15.2 %collective-permute-start.34 = (bf16[192,1536]{1,0:T(8,128)(2,1)S(1)}, bf16[192,1536]{1,0:T(8,128)(2,1)S(1)}, u32[]{:S(2)}, u32[]{:S(2)}) collective-permute-start(bf16[192,1536]{1,0:T(8,128)(2,1)S(1)} %get-tuple-element.199), channel_id=1, source_target_pairs={{0,4},{2,6},{4,0},{6,2},{8,12},{10,14},{12,8},{14,10},{16,20},{18,... | collective-permute-start | bytes 1769480 | tf_op jit(solution)/shard_map/up_gradient_across_2/ppermute | solution.py:140
  131.1 14.3 %collective-permute-start.35 = (bf16[192,1536]{1,0:T(8,128)(2,1)S(1)}, bf16[192,1536]{1,0:T(8,128)(2,1)S(1)}, u32[]{:S(2)}, u32[]{:S(2)}) collective-permute-start(bf16[192,1536]{1,0:T(8,128)(2,1)S(1)} %get-tuple-element.200), channel_id=1, source_target_pairs={{0,2},{2,0},{4,6},{6,4},{8,10},{10,8},{12,14},{14,12},{16,18},{18,... | collective-permute-start | bytes 1769480 | tf_op jit(solution)/shard_map/up_gradient_across_1/ppermute | solution.py:140
  145.7 9.8 %collective-permute-start.36 = (bf16[96,1536]{1,0:T(8,128)(2,1)S(1)}, bf16[96,1536]{1,0:T(8,128)(2,1)S(1)}, u32[]{:S(2)}, u32[]{:S(2)}) collective-permute-start(bf16[96,1536]{1,0:T(8,128)(2,1)S(1)} %get-tuple-element.202), channel_id=1, source_target_pairs={{0,8},{2,10},{4,12},{6,14},{8,0},{10,2},{12,4},{14,6},{16,24},{18,... | collective-permute-start | bytes 884744 | tf_op jit(solution)/shard_map/up_gradient_across_4/ppermute | solution.py:140
  147.0 8.5 %collective-permute-start.28 = (bf16[96,1152]{1,0:T(8,128)(2,1)S(1)}, bf16[96,1152]{1,0:T(8,128)(2,1)S(1)}, u32[]{:S(2)}, u32[]{:S(2)}) collective-permute-start(bf16[96,1152]{1,0:T(8,128)(2,1)S(1)} %get-tuple-element.184), channel_id=1, source_target_pairs={{0,2},{2,0},{4,6},{6,4},{8,10},{10,8},{12,14},{14,12},{16,18},{18,... | collective-permute-start | bytes 663560 | tf_op jit(solution)/shard_map/early_gradient_across_1/ppermute | solution.py:140
  147.8 7.7 %collective-permute-start.29 = (bf16[96,1152]{1,0:T(8,128)(2,1)S(1)}, bf16[96,1152]{1,0:T(8,128)(2,1)S(1)}, u32[]{:S(2)}, u32[]{:S(2)}) collective-permute-start(bf16[96,1152]{1,0:T(8,128)(2,1)S(1)} %get-tuple-element.185), channel_id=1, source_target_pairs={{0,4},{2,6},{4,0},{6,2},{8,12},{10,14},{12,8},{14,10},{16,20},{18,... | collective-permute-start | bytes 663560 | tf_op jit(solution)/shard_map/early_gradient_across_2/ppermute | solution.py:140
  148.2 6.1 %collective-permute-start.30 = (bf16[96,512]{1,0:T(8,128)(2,1)S(1)}, bf16[96,512]{1,0:T(8,128)(2,1)S(1)}, u32[]{:S(2)}, u32[]{:S(2)}) collective-permute-start(bf16[96,512]{1,0:T(8,128)(2,1)S(1)} %get-tuple-element.190), channel_id=1, source_target_pairs={{0,2},{2,0},{4,6},{6,4},{8,10},{10,8},{12,14},{14,12},{16,18},{18,... | collective-permute-start | bytes 294920 | tf_op jit(solution)/shard_map/late_gradient_across_1/ppermute | solution.py:140
  149.5 5.9 %collective-permute-start.31 = (bf16[96,512]{1,0:T(8,128)(2,1)S(1)}, bf16[96,512]{1,0:T(8,128)(2,1)S(1)}, u32[]{:S(2)}, u32[]{:S(2)}) collective-permute-start(bf16[96,512]{1,0:T(8,128)(2,1)S(1)} %get-tuple-element.191), channel_id=1, source_target_pairs={{0,4},{2,6},{4,0},{6,2},{8,12},{10,14},{12,8},{14,10},{16,20},{18,... | collective-permute-start | bytes 294920 | tf_op jit(solution)/shard_map/late_gradient_across_2/ppermute | solution.py:140
  155.7 9.5 %collective-permute-start.37 = (bf16[192,1152]{1,0:T(8,128)(2,1)S(1)}, bf16[192,1152]{1,0:T(8,128)(2,1)S(1)}, u32[]{:S(2)}, u32[]{:S(2)}) collective-permute-start(bf16[192,1152]{1,0:T(8,128)(2,1)S(1)} %get-tuple-element.203.refs_2_.refs_6_), channel_id=1, source_target_pairs={{0,4},{2,6},{4,0},{6,2},{8,12},{10,14},{12,8},{14,10},{16,20},{18,... | collective-permute-start | bytes 1327112 | tf_op jit(solution)/shard_map/early_gradient_across_2/ppermute | solution.py:140
  156.2 9.1 %collective-permute-start.38 = (bf16[192,1152]{1,0:T(8,128)(2,1)S(1)}, bf16[192,1152]{1,0:T(8,128)(2,1)S(1)}, u32[]{:S(2)}, u32[]{:S(2)}) collective-permute-start(bf16[192,1152]{1,0:T(8,128)(2,1)S(1)} %get-tuple-element.204.refs_3_.refs_7_), channel_id=1, source_target_pairs={{0,2},{2,0},{4,6},{6,4},{8,10},{10,8},{12,14},{14,12},{16,18},{18,... | collective-permute-start | bytes 1327112 | tf_op jit(solution)/shard_map/early_gradient_across_1/ppermute | solution.py:140
  157.0 7.7 %collective-permute-start.39 = (bf16[48,1536]{1,0:T(8,128)(2,1)S(1)}, bf16[48,1536]{1,0:T(8,128)(2,1)S(1)}, u32[]{:S(2)}, u32[]{:S(2)}) collective-permute-start(bf16[48,1536]{1,0:T(8,128)(2,1)S(1)} %get-tuple-element.209), channel_id=1, source_target_pairs={{0,16},{2,18},{4,20},{6,22},{8,24},{10,26},{12,28},{14,30},{16,0},... | collective-permute-start | bytes 442376 | tf_op jit(solution)/shard_map/up_gradient_across_8/ppermute | solution.py:140
  165.5 3.5 %collective-permute-start.41 = (bf16[1024,768]{1,0:T(8,128)(2,1)S(1)}, bf16[1024,768]{1,0:T(8,128)(2,1)S(1)}, u32[]{:S(2)}, u32[]{:S(2)}) collective-permute-start(bf16[1024,768]{1,0:T(8,128)(2,1)S(1)} %get-tuple-element.214.refs_1_), channel_id=1, source_target_pairs={{0,1},{1,0},{2,3},{3,2},{4,5},{5,4},{6,7},{7,6},{8,9},{9,8},{10,11... | collective-permute-start | bytes 4718600 | tf_op jit(solution)/shard_map/first_gradient_other_core/ppermute | solution.py:149
  165.6 10.5 %collective-permute-start.43 = (bf16[192,512]{1,0:T(8,128)(2,1)S(1)}, bf16[192,512]{1,0:T(8,128)(2,1)S(1)}, u32[]{:S(2)}, u32[]{:S(2)}) collective-permute-start(bf16[192,512]{1,0:T(8,128)(2,1)S(1)} %get-tuple-element.206.refs_4_.refs_8_), channel_id=1, source_target_pairs={{0,4},{2,6},{4,0},{6,2},{8,12},{10,14},{12,8},{14,10},{16,20},{18,... | collective-permute-start | bytes 589832 | tf_op jit(solution)/shard_map/late_gradient_across_2/ppermute | solution.py:140
  167.2 8.9 %collective-permute-start.44 = (bf16[192,512]{1,0:T(8,128)(2,1)S(1)}, bf16[192,512]{1,0:T(8,128)(2,1)S(1)}, u32[]{:S(2)}, u32[]{:S(2)}) collective-permute-start(bf16[192,512]{1,0:T(8,128)(2,1)S(1)} %get-tuple-element.207.refs_5_.refs_9_), channel_id=1, source_target_pairs={{0,2},{2,0},{4,6},{6,4},{8,10},{10,8},{12,14},{14,12},{16,18},{18,... | collective-permute-start | bytes 589832 | tf_op jit(solution)/shard_map/late_gradient_across_1/ppermute | solution.py:140
  167.8 7.2 %collective-permute-start.40 = (bf16[96,1152]{1,0:T(8,128)(2,1)S(1)}, bf16[96,1152]{1,0:T(8,128)(2,1)S(1)}, u32[]{:S(2)}, u32[]{:S(2)}) collective-permute-start(bf16[96,1152]{1,0:T(8,128)(2,1)S(1)} %get-tuple-element.212.refs_6_), channel_id=1, source_target_pairs={{0,8},{2,10},{4,12},{6,14},{8,0},{10,2},{12,4},{14,6},{16,24},{18,... | collective-permute-start | bytes 663560 | tf_op jit(solution)/shard_map/early_gradient_across_4/ppermute | solution.py:140
  175.1 27.4 %copy-start.5 = (f32[3,48,384]{2,1,0:T(8,128)S(1)}, f32[3,48,384]{2,1,0:T(8,128)}, u32[]{:S(2)}) copy-start(f32[3,48,384]{2,1,0:T(8,128)} %get-tuple-element.146.refs_4_.refs_11_) | copy-start | bytes 663556
  175.1 27.4 %copy-start.7 = (f32[48,1536]{1,0:T(8,128)S(1)}, f32[48,1536]{1,0:T(8,128)}, u32[]{:S(2)}) copy-start(f32[48,1536]{1,0:T(8,128)} %get-tuple-element.232.refs_13_) | copy-start | bytes 884740
  175.1 27.4 %copy-start.8 = (f32[48,1536]{1,0:T(8,128)S(1)}, f32[48,1536]{1,0:T(8,128)}, u32[]{:S(2)}) copy-start(f32[48,1536]{1,0:T(8,128)} %get-tuple-element.233.refs_14_) | copy-start | bytes 884740
  175.1 27.4 %copy-start.9 = (f32[48,1536]{1,0:T(8,128)S(1)}, f32[48,1536]{1,0:T(8,128)}, u32[]{:S(2)}) copy-start(f32[48,1536]{1,0:T(8,128)} %get-tuple-element.236.refs_20_) | copy-start | bytes 884740
  175.1 27.4 %copy-start.10 = (f32[48,1536]{1,0:T(8,128)S(1)}, f32[48,1536]{1,0:T(8,128)}, u32[]{:S(2)}) copy-start(f32[48,1536]{1,0:T(8,128)} %get-tuple-element.237.refs_21_) | copy-start | bytes 884740
  175.2 27.4 %copy-start.11 = (f32[48,1536]{1,0:T(8,128)S(1)}, f32[48,1536]{1,0:T(8,128)}, u32[]{:S(2)}) copy-start(f32[48,1536]{1,0:T(8,128)} %get-tuple-element.240.refs_27_) | copy-start | bytes 884740
  175.2 27.4 %copy-start.12 = (f32[48,1536]{1,0:T(8,128)S(1)}, f32[48,1536]{1,0:T(8,128)}, u32[]{:S(2)}) copy-start(f32[48,1536]{1,0:T(8,128)} %get-tuple-element.241.refs_28_) | copy-start | bytes 884740
  175.2 27.4 %copy-start.13 = (f32[3,48,384]{2,1,0:T(8,128)S(1)}, f32[3,48,384]{2,1,0:T(8,128)}, u32[]{:S(2)}) copy-start(f32[3,48,384]{2,1,0:T(8,128)} %get-tuple-element.234.refs_18_) | copy-start | bytes 663556
  175.2 27.4 %copy-start.14 = (f32[3,48,384]{2,1,0:T(8,128)S(1)}, f32[3,48,384]{2,1,0:T(8,128)}, u32[]{:S(2)}) copy-start(f32[3,48,384]{2,1,0:T(8,128)} %get-tuple-element.238.refs_25_) | copy-start | bytes 663556
  175.3 11.0 %collective-permute-start.42 = (bf16[48,1152]{1,0:T(8,128)(2,1)S(1)}, bf16[48,1152]{1,0:T(8,128)(2,1)S(1)}, u32[]{:S(2)}, u32[]{:S(2)}) collective-permute-start(bf16[48,1152]{1,0:T(8,128)(2,1)S(1)} %get-tuple-element.217), channel_id=1, source_target_pairs={{0,16},{2,18},{4,20},{6,22},{8,24},{10,26},{12,28},{14,30},{16,0},... | collective-permute-start | bytes 331784 | tf_op jit(solution)/shard_map/early_gradient_across_8/ppermute | solution.py:140
  176.2 10.1 %collective-permute-start.45 = (bf16[48,512]{1,0:T(8,128)(2,1)S(1)}, bf16[48,512]{1,0:T(8,128)(2,1)S(1)}, u32[]{:S(2)}, u32[]{:S(2)}) collective-permute-start(bf16[48,512]{1,0:T(8,128)(2,1)S(1)} %get-tuple-element.220), channel_id=1, source_target_pairs={{0,16},{2,18},{4,20},{6,22},{8,24},{10,26},{12,28},{14,30},{16,0},... | collective-permute-start | bytes 147464 | tf_op jit(solution)/shard_map/late_gradient_across_8/ppermute | solution.py:140
  178.5 7.8 %collective-permute-start.46 = (bf16[48,512]{1,0:T(8,128)(2,1)S(1)}, bf16[48,512]{1,0:T(8,128)(2,1)S(1)}, u32[]{:S(2)}, u32[]{:S(2)}) collective-permute-start(bf16[48,512]{1,0:T(8,128)(2,1)S(1)} %get-tuple-element.221), channel_id=1, source_target_pairs={{0,8},{2,10},{4,12},{6,14},{8,0},{10,2},{12,4},{14,6},{16,24},{18,... | collective-permute-start | bytes 147464 | tf_op jit(solution)/shard_map/late_gradient_across_4/ppermute | solution.py:140
  179.2 7.1 %collective-permute-start.47 = (bf16[48,512]{1,0:T(8,128)(2,1)S(1)}, bf16[48,512]{1,0:T(8,128)(2,1)S(1)}, u32[]{:S(2)}, u32[]{:S(2)}) collective-permute-start(bf16[48,512]{1,0:T(8,128)(2,1)S(1)} %get-tuple-element.222), channel_id=1, source_target_pairs={{0,24},{2,26},{4,28},{6,30},{8,16},{10,18},{12,20},{14,22},{16,8},... | collective-permute-start | bytes 147464 | tf_op jit(solution)/shard_map/late_gradient_across_12/ppermute | solution.py:140
  187.7 1.2 collective-permute-start.48
  189.0 5.5 %collective-permute-start.51 = (f32[1,24,128]{2,1,0:T(8,128)S(1)}, f32[1,24,128]{2,1,0:T(8,128)S(1)}, u32[]{:S(2)}, u32[]{:S(2)}) collective-permute-start(f32[1,24,128]{2,1,0:T(8,128)S(1)} %bitcast.55), channel_id=1, source_target_pairs={{0,24},{2,26},{4,28},{6,30},{8,16},{10,18},{12,20},{14,22},{16,8},... | collective-permute-start | bytes 36872 | tf_op jit(solution)/shard_map/squares_across_12/ppermute | solution.py:140
  190.6 3.9 %collective-permute-start.50 = (f32[1,24,128]{2,1,0:T(8,128)S(1)}, f32[1,24,128]{2,1,0:T(8,128)S(1)}, u32[]{:S(2)}, u32[]{:S(2)}) collective-permute-start(f32[1,24,128]{2,1,0:T(8,128)S(1)} %bitcast.56), channel_id=1, source_target_pairs={{0,8},{2,10},{4,12},{6,14},{8,0},{10,2},{12,4},{14,6},{16,24},{18,... | collective-permute-start | bytes 36872 | tf_op jit(solution)/shard_map/squares_across_4/ppermute | solution.py:140
  190.8 4.7 %collective-permute-start.49 = (f32[1,24,128]{2,1,0:T(8,128)S(1)}, f32[1,24,128]{2,1,0:T(8,128)S(1)}, u32[]{:S(2)}, u32[]{:S(2)}) collective-permute-start(f32[1,24,128]{2,1,0:T(8,128)S(1)} %bitcast.57), channel_id=1, source_target_pairs={{0,16},{2,18},{4,20},{6,22},{8,24},{10,26},{12,28},{14,30},{16,0},... | collective-permute-start | bytes 36872 | tf_op jit(solution)/shard_map/squares_across_8/ppermute | solution.py:140
  195.5 5.0 %collective-permute-start.54 = (f32[4,24,128]{2,1,0:T(8,128)S(1)}, f32[4,24,128]{2,1,0:T(8,128)S(1)}, u32[]{:S(2)}, u32[]{:S(2)}) collective-permute-start(f32[4,24,128]{2,1,0:T(8,128)S(1)} %join.13.refs_3_), channel_id=1, source_target_pairs={{0,6},{2,4},{4,2},{6,0},{8,14},{10,12},{12,10},{14,8},{16,22},{18,... | collective-permute-start | bytes 147464 | tf_op jit(solution)/shard_map/squares_across_3/ppermute | solution.py:140
  197.0 4.1 %collective-permute-start.53 = (f32[4,24,128]{2,1,0:T(8,128)S(1)}, f32[4,24,128]{2,1,0:T(8,128)S(1)}, u32[]{:S(2)}, u32[]{:S(2)}) collective-permute-start(f32[4,24,128]{2,1,0:T(8,128)S(1)} %join.13.refs_3_), channel_id=1, source_target_pairs={{0,2},{2,0},{4,6},{6,4},{8,10},{10,8},{12,14},{14,12},{16,18},{18,... | collective-permute-start | bytes 147464 | tf_op jit(solution)/shard_map/squares_across_1/ppermute | solution.py:140
  198.4 4.1 %collective-permute-start.52 = (f32[4,24,128]{2,1,0:T(8,128)S(1)}, f32[4,24,128]{2,1,0:T(8,128)S(1)}, u32[]{:S(2)}, u32[]{:S(2)}) collective-permute-start(f32[4,24,128]{2,1,0:T(8,128)S(1)} %join.13.refs_3_), channel_id=1, source_target_pairs={{0,4},{2,6},{4,0},{6,2},{8,12},{10,14},{12,8},{14,10},{16,20},{18,... | collective-permute-start | bytes 147464 | tf_op jit(solution)/shard_map/squares_across_2/ppermute | solution.py:140
  (22 other events, 363.8 us)
where the time goes:
time: 206 us; the launch traced here: 205 us
  Pallas kernels  70.8 us (34%)
  waiting for transfers between devices  70.4 us (34%)
  starting transfers between devices  56.6 us (27%)
  local copies, waits for them, and re-layouts  5.1 us (2%)
  between operations  2.36 us (1%)
    pallas_call x40, Pallas kernels, apply(): pl.pallas_call(run, out_shape=[*out_shapes, *(shape_of(a.shape, a.dtype)...  70.8 us
    ppermute x50, waiting for transfers between devices, swap(): return lax.ppermute(array, 'dp', [(i, i ^ mask) for i in range(size)])  67.6 us
    ppermute x50, starting transfers between devices, swap(): return lax.ppermute(array, 'dp', [(i, i ^ mask) for i in range(size)])  56.4 us
    unnamed x62, local copies, waits for them, and re-layouts  4.41 us
  transfers between devices with their start and end apart: 55, of which 34 were waited for; matrix products, arithmetic and copies ran while one was open for 0% of the time, Pallas kernels for 28%

commit v1 on v0

--- a/solution.py
+++ b/solution.py
@@ -340,6 +340,7 @@
             passing=passing,
         )(keep, *self.came)
         came = [swap(other, mask, size, label) for other, mask in zip(others, (8, 4, 12))]
+        self.sources = (own,)
         return [own] + came, others[3:]
 
 
@@ -373,9 +374,25 @@
     a_ref[:, (parts + 1) * width :] = extra.astype(low_type)
 
 
-def pack_hidden_kernel(up_ref, down_ref, b_ref, c_ref):
-    b_ref[...] = up_ref[...].astype(low_type)
-    c_ref[...] = down_ref[...].astype(low_type)
+def pack_hidden_kernel(up_ref, down_ref, packed_ref, *part_refs):
+    packed_ref[...] = up_ref[...].astype(low_type)
+    start = 0
+    for ref in part_refs:
+        width = ref.shape[1]
+        ref[...] = down_ref[:, start : start + width].astype(low_type)
+        start += width
+
+
+def fill_down(target, line_pieces, plane_pieces):
+    width = line_pieces[0].shape[1]
+    fill_rows(target.at[:, :width], line_pieces)
+    own = target.shape[0] // 16
+    for i, piece in enumerate(plane_pieces):
+        for f in range(2):
+            for q in range(4):
+                rows = piece[(f * 4 + q) * own : (f * 4 + q + 1) * own, :]
+                place = (4 * q + 2 * i + f) * own
+                target[place : place + own, width:] = rows
 
 
 def prepare_kernel(
@@ -591,7 +608,7 @@
 
 def hidden_kernel(pieces, len_ref, x_ref, own_ref, came_ref, vector_ref, *refs):
     weight_refs, refs = refs[:pieces], refs[pieces:]
-    normed_ref, slope_ref, act_ref, sum_ref, w_ref, rows_ref = refs
+    normed_ref, slope_ref, act_ref, sum_ref, w_ref = refs
     m = pl.program_id(0)
     slot = x_ref.shape[0]
 
@@ -603,25 +620,16 @@
     normed = (middle * rms_scale(middle) * vector_ref[1:2]).astype(low_type)
     valid = lax.broadcasted_iota(jnp.int32, (slot, 1), 0) < len_ref[m]
     normed_ref[...] = jnp.where(valid, normed, jnp.zeros_like(normed))
-    rows_ref[...] = normed
     sum_ref[0] = jnp.sum(jnp.where(valid, middle, 0.0), axis=0, keepdims=True)
-    act_ref[...] = jnp.zeros_like(act_ref)
-
-    def rows_step(i, carry):
-        rows = pl.ds(pl.multiple_of(i * ROWS, ROWS), ROWS)
-        v = dot_nn(rows_ref[rows, :], w_ref[...])
-        square = v * v
-        gate = jnp.tanh(v * (gelu_slope + (gelu_slope * gelu_cubic) * square))
-        half = 0.5 + 0.5 * gate
-        active = (v * half).astype(low_type)
-        counted = lax.broadcasted_iota(jnp.int32, (16, ROWS), 1) + i * ROWS < len_ref[m]
-        counted = jnp.where(counted, 1.0, 0.0).astype(low_type)
-        act_ref[0] += dot_nn(counted, active)[0:1]
-        inner = 0.5 * gelu_slope + (1.5 * gelu_slope * gelu_cubic) * square
-        slope_ref[rows, :] = (half + v * (1.0 - gate * gate) * inner).astype(low_type)
-        return carry
-
-    lax.fori_loop(0, slot // ROWS, rows_step, 0)
+    v = dot_nn(normed, w_ref[...])
+    square = v * v
+    gate = jnp.tanh(v * (gelu_slope + (gelu_slope * gelu_cubic) * square))
+    half = 0.5 + 0.5 * gate
+    active = (v * half).astype(low_type)
+    counted = lax.broadcasted_iota(jnp.int32, (16, slot), 1) < len_ref[m]
+    act_ref[0] = dot_nn(jnp.where(counted, 1.0, 0.0).astype(low_type), active)[0:1]
+    inner = 0.5 * gelu_slope + (1.5 * gelu_slope * gelu_cubic) * square
+    slope_ref[...] = (half + v * (1.0 - gate * gate) * inner).astype(low_type)
 
 
 def middle_rows(x_ref, own_ref, came_ref):
@@ -658,7 +666,6 @@
             row_blocks((1, 1, width)),
             whole((width, inner)),
         ],
-        scratch_shapes=[pltpu.VMEM((slot, width), low_type)],
     )(lengths, rows_low, own, came, vectors, *weights)
 
 
@@ -670,9 +677,9 @@
     return total
 
 
-def pool_kernel(act_ref, *refs):
+def pool_kernel(lines, act_ref, *refs):
     *weight_refs, out_ref, w_ref = refs
-    fill_rows(w_ref, weight_refs)
+    fill_down(w_ref, weight_refs[:lines], weight_refs[lines:])
     sums = [act_ref[m] for m in range(act_ref.shape[0])]
     highs = [row.astype(low_type).astype(full_type) for row in sums]
     rests = [row - high for row, high in zip(sums, highs)]
@@ -1332,8 +1339,11 @@
     packed_heads = call(
         pack_heads_kernel, "pack_heads", shape_of((own, 4 * head_width + LANES), low_type), vmem=56
     )(heads_in, heads_out, gains, tied_rows)
-    packed_up, packed_down = call(
-        pack_hidden_kernel, "pack_hidden", [shape_of((own, inner), low_type)] * 2
+    down_widths = [inner] if size != 16 else [inner - inner // 3, inner // 3]
+    packed_up, packed_down, *packed_plane = call(
+        pack_hidden_kernel,
+        "pack_hidden",
+        [shape_of((own, width_here), low_type) for width_here in (inner, *down_widths)],
     )(hidden_in, hidden_out)
     weights = (heads_in, heads_out, hidden_in, hidden_out, gains, tied_rows, bias_table)
     firsts = (
@@ -1405,20 +1415,22 @@
         weight_heads, weight_up, weight_down = (
             [gather_doubling(part, size)] for part in (packed_heads, packed_up, packed_down)
         )
+        planes = []
         qkv, normed_first, vectors = project(rows_low, weight_heads, pairs, ())
     else:
+        plane_sides = side_parts(*packed_plane, size, "down_plane")
         heads_line, packed_up, packed_down = join(
             line_parts(packed_heads, size, "heads"),
-            deps=(staged[0], order, corrections),
+            deps=(staged[0], order, corrections, *plane_sides),
             passing=(packed_up, packed_down),
         )
         heads_sides = side_parts(heads_line, size, "heads")
-        up_pair = join(
-            [packed_up, swap(packed_up, 8, size, "up")],
-            deps=(rows_low,),
+        up_pair = join([packed_up, swap(packed_up, 8, size, "up")], deps=(rows_low,))
+        up_near = swap(up_pair, 4, size, "up")
+        plane_corner = swap(plane_sides[0], 1, size, "down_plane_corner")
+        low, high, packed_down = gather_step(
+            *heads_sides, deps=(up_pair, plane_corner), passing=(packed_down,)
         )
-        up_near = swap(up_pair, 4, size, "up")
-        low, high, packed_down = gather_step(*heads_sides, deps=(up_pair,), passing=(packed_down,))
         down_far = swap(packed_down, 8, size, "down")
         heads_corner = corner_parts(low, high, size, "heads_corner")
         up_line = join([up_pair, up_near], deps=(low,))
@@ -1426,21 +1438,27 @@
         down_near = swap(down_pair, 4, size, "down")
         up_sides = side_parts(up_line, size, "up")
         weight_heads = [heads_line, *heads_sides, *heads_corner]
-        qkv, normed_first, vectors = project(rows_low, weight_heads, pairs, (down_pair,))
-    filled = attention(lengths, lines, qkv, 0, 1, slot)
+        qkv, normed_first, vectors = project(rows_low, weight_heads, pairs, ())
+    filled = attention(
+        lengths, lines, qkv, 0, 1, slot, deps=(down_pair,) if size == 16 else ()
+    )
     if size == 16:
         down_line = join([down_pair, down_near], deps=(filled[0],))
         down_sides = side_parts(down_line, size, "down")
+        plane = join([*packed_plane, *plane_sides, plane_corner], deps=(down_line,))
+        plane_far = swap(plane, 8, size, "down_plane")
     if pairs > 1:
         filled = attention(lengths, lines, qkv, 1, pairs - 1, slot, before=filled)
     if size == 16:
         low, high = gather_step(*up_sides, deps=(filled[0],))
         up_corner = corner_parts(low, high, size, "up_corner")
+        plane_pair = join([plane, plane_far], deps=(filled[0],))
+        planes = [plane_pair, swap(plane_pair, 4, size, "down_plane")]
         weight_up = [up_line, *up_sides, *up_corner]
     turned_first = call(turn_kernel, "turn", shape_of((width, count), low_type))(normed_first)
     attended, probs, inverse = filled
     branch = branch_rows(
-        attended, weight_heads, (low, *down_sides, turned_first) if size == 16 else ()
+        attended, weight_heads, (*up_corner, *down_sides, *planes, turned_first) if size == 16 else ()
     )
     if size == 16:
         low, high = gather_step(*down_sides, deps=(branch,))
@@ -1451,11 +1469,11 @@
         lengths, rows_low, branch, branch_came, vectors, weight_up, slot
     )
     down, full_down = call(
-        pool_kernel,
+        functools.partial(pool_kernel, len(weight_down)),
         "pool",
         [shape_of((8, width), full_type), shape_of((width, inner), low_type)],
         cost=(20, 5000),
-    )(act_sum, *weight_down)
+    )(act_sum, *weight_down, *planes)
     small = call(
         margin_kernel,
         "margin",
@@ -1497,16 +1515,17 @@
     d_normed_first = normed_back(d_project, weight_heads, sides)
     up_parts = up_sum.far(deps=sides)
     (d_normed_first,) = early_sum.near(deps=tuple(up_parts), passing=(d_normed_first,))
+    early_parts = early_sum.far()
+    late_parts, _ = late_sum.line(deps=(early_parts[0],))
+
     token_gradient, token_done = token_back(
         d_middle, d_normed_first, other_core(d_normed_first, "first_gradient_other_core"), rows_low,
-        vectors, order, early_sum.sources,
-    )
-    early_parts = early_sum.far(deps=(token_done,))
-    late_parts, _ = late_sum.line(deps=(early_parts[0],))
+        vectors, order, late_sum.sources,
+    )
 
     g_down, line, grad_sums = totals(
         small_all, ranks, vectors, [early_parts, late_parts, up_parts], heads_in, hidden_in, gains, tied_rows,
-        (head_width * 3, 3 * LANES, inner), micro, (),
+        (head_width * 3, 3 * LANES, inner), micro, (token_done,),
     )
     square_tile, extra = call(
         functools.partial(square_kernel, local_heads),

time: 206 us -> 199 us (0.966)
  waiting for transfers between devices: 70.4 us -> 57.7 us
  starting transfers between devices: 56.6 us -> 64.3 us
    ppermute x50 -> x55, waiting for transfers between devices: 67.6 us -> 54.7 us  [swap(): return lax.ppermute(array, 'dp', [(i, i ^ mask) for i in range(size)])]
    ppermute x50 -> x55, starting transfers between devices: 56.4 us -> 63.9 us  [swap(): return lax.ppermute(array, 'dp', [(i, i ^ mask) for i in range(size)])]
    pallas_call x40 -> x42, Pallas kernels: 70.8 us -> 69.7 us  [apply(): pl.pallas_call(run, out_shape=[*out_shapes, *(shape_of(a.shape, a.dtype)...]
  transfers between devices with their start and end apart: 55 -> 60, of which waited for: 34 -> 32; matrix products, arithmetic and copies ran while one was open for 0% -> 0% of each run, Pallas kernels for 28% -> 28%
where the time goes in v1:
time: 199 us
  Pallas kernels  69.7 us (35%)
  starting transfers between devices  64.3 us (32%)
  waiting for transfers between devices  57.7 us (29%)
  local copies, waits for them, and re-layouts  5.06 us (3%)
  between operations  2.37 us (1%)
    pallas_call x42, Pallas kernels, apply(): pl.pallas_call(run, out_shape=[*out_shapes, *(shape_of(a.shape, a.dtype)...  69.7 us
    ppermute x55, starting transfers between devices, swap(): return lax.ppermute(array, 'dp', [(i, i ^ mask) for i in range(size)])  63.9 us
    ppermute x55, waiting for transfers between devices, swap(): return lax.ppermute(array, 'dp', [(i, i ^ mask) for i in range(size)])  54.7 us
    unnamed x62, local copies, waits for them, and re-layouts  4.37 us
  transfers between devices with their start and end apart: 60, of which 32 were waited for; matrix products, arithmetic and copies ran while one was open for 0% of the time, Pallas kernels for 28%

profile of v1, /device:TPU:0, one launch (start us, length us, event | category | flops | bytes accessed | tf_op | source)
XLA Modules:
  0.0 199.2 jit_solution(10573857368265723486)
XLA Ops:
  0.7 1.8 pack_heads.1.refs_0_
  2.5 5.0 %collective-permute-start.2 = (bf16[48,1664]{1,0:T(8,128)(2,1)}, bf16[48,1664]{1,0:T(8,128)(2,1)S(1)}, u32[]{:S(2)}, u32[]{:S(2)}) collective-permute-start(bf16[48,1664]{1,0:T(8,128)(2,1)} %pack_heads.1.refs_0_), channel_id=1, source_target_pairs={{0,24},{2,26},{4,28},{6,30},{8,16},{10,18},{12,20},{14,22},{16,8},... | collective-permute-start | bytes 479240 | tf_op jit(solution)/shard_map/heads_across_12/ppermute | solution.py:140
  10.1 1.8 collective-permute-start.4
  11.8 1.5 collective-permute-start.3
  16.3 1.4 prepare.1
  17.7 3.3 %stage.1 = (f32[3,48,384]{2,1,0:T(8,128)}, f32[48,384]{1,0:T(8,128)}, f32[48,1536]{1,0:T(8,128)}, f32[48,1536]{1,0:T(8,128)}, f32[3,48,384]{2,1,0:T(8,128)}, /*i...) custom-call(f32[3,48,384]{2,1,0:T(8,128)} %bitcast.37, ...), custom_call_target="tpu_custom_call" | custom-call | tf_op jit(solution)/shard_map/stage/pallas_call | solution.py:78
  22.3 1.6 collective-permute-start.6
  23.8 1.5 collective-permute-start.5
  25.6 1.9 order_tokens.1.refs_2_.refs_0_.refs_1_.refs_3_
  27.5 5.9 %collective-permute-done.7.refs_1_ = bf16[48,1536]{1,0:T(8,128)(2,1)S(1)} collective-permute-done((bf16[48,1536]{1,0:T(8,128)(2,1)S(1)}, bf16[48,1536]{1,0:T(8,128)(2,1)S(1)}, u32[]{:S(2)}, u32[]{:S(2)}) %collective-permute-start.7) | collective-permute-done | bytes 147488 | tf_op jit(solution)/shard_map/up_across_8/ppermute | solution.py:140
  34.1 4.7 %collective-permute-done.8.refs_3_ = bf16[48,512]{1,0:T(8,128)(2,1)S(1)} collective-permute-done((bf16[48,512]{1,0:T(8,128)(2,1)S(1)}, bf16[48,512]{1,0:T(8,128)(2,1)S(1)}, u32[]{:S(2)}, u32[]{:S(2)}) %collective-permute-start.8) | collective-permute-done | bytes 49184 | tf_op jit(solution)/shard_map/down_plane_corner_across_1/ppermute | solution.py:140
  39.0 1.6 collective-permute-start.10
  40.6 1.4 collective-permute-start.9
  43.1 1.5 collective-permute-start.13
  44.7 3.3 %collective-permute-done.11.refs_1_ = bf16[48,1024]{1,0:T(8,128)(2,1)S(1)} collective-permute-done((bf16[48,1024]{1,0:T(8,128)(2,1)S(1)}, bf16[48,1024]{1,0:T(8,128)(2,1)S(1)}, u32[]{:S(2)}, u32[]{:S(2)}) %collective-permute-start.11) | collective-permute-done | bytes 98336 | tf_op jit(solution)/shard_map/down_across_8/ppermute | solution.py:140
  48.1 1.5 collective-permute-done.10.refs_5_.refs_14_
  49.6 1.5 collective-permute-done.9.refs_4_.refs_13_
  51.1 3.6 %projection.1 = (bf16[3,3,1024,128]{3,2,1,0:T(8,128)(2,1)S(1)}, bf16[1024,768]{1,0:T(8,128)(2,1)S(1)}, f32[8,768]{1,0:T(8,128)S(1)}) custom-call(bf16[1024,768]{1,0:T(8,128)(2,1)S(1)} %order_tokens.1.refs_2_.refs_0_.refs_1_.refs_3_, bf16[192,1664]{1,0:T(8,128)(2,1)S(1)} %get-tuple-element.151.refs_1_.refs_10_, ...), custom_call_target="tpu_custom_call" | custom-call | tf_op jit(solution)/shard_map/projection/pallas_call | solution.py:78
  54.7 3.5 %attention_forward.2 = (bf16[1024,384]{1,0:T(8,128)(2,1)S(1)}, bf16[3,2,2,512,512]{4,3,2,1,0:T(8,128)(2,1)S(1)}, f32[1024,384]{1,0:T(8,128)S(1)}) custom-call(s32[2]{0:T(128)S(1)} %bitcast.49, f32[3,2,1024]{2,1,0:T(2,128)S(1)} %get-tuple-element.146.refs_1_, bf16[3,3,1024,128]{3,2,1,0:T(8,128)(2,1)S(1)} %get-tuple-element.156.refs_2_.refs_1_, ...), custom_call_target="tpu_custom_call" | custom-call | tf_op jit(solution)/shard_map/attention_forward/pallas_call | solution.py:78
  58.3 1.5 collective-permute-start.19
  60.9 6.5 %attention_forward.3 = (bf16[1024,384]{1,0:T(8,128)(2,1)S(1)}, bf16[3,2,2,512,512]{4,3,2,1,0:T(8,128)(2,1)S(1)}, f32[1024,384]{1,0:T(8,128)S(1)}) custom-call(s32[2]{0:T(128)S(1)} %bitcast.50, f32[3,2,1024]{2,1,0:T(2,128)S(1)} %get-tuple-element.146.refs_1_, ...), custom_call_target="tpu_custom_call", output_to_operand_aliasing={{0}: (3, {}), {1}: (4, {}), {2}: (5, {})} | custom-call | tf_op jit(solution)/shard_map/attention_forward/pallas_call | solution.py:78
  67.4 2.2 %collective-permute-start.21 = (bf16[384,512]{1,0:T(8,128)(2,1)S(1)}, bf16[384,512]{1,0:T(8,128)(2,1)S(1)}, u32[]{:S(2)}, u32[]{:S(2)}) collective-permute-start(bf16[384,512]{1,0:T(8,128)(2,1)S(1)} %join.15.refs_10_.refs_6_), channel_id=1, source_target_pairs={{0,8},{2,10},{4,12},{6,14},{8,0},{10,2},{12,4},{14,6},{16,24},{18,... | collective-permute-start | bytes 1179656 | tf_op jit(solution)/shard_map/down_plane_across_4/ppermute | solution.py:140
  70.7 1.2 collective-permute-start.16
  72.4 4.0 %collective-permute-done.15.refs_6_.refs_8_ = bf16[96,1536]{1,0:T(8,128)(2,1)S(1)} collective-permute-done((bf16[96,1536]{1,0:T(8,128)(2,1)S(1)}, bf16[96,1536]{1,0:T(8,128)(2,1)S(1)}, u32[]{:S(2)}, u32[]{:S(2)}) %collective-permute-start.15) | collective-permute-done | bytes 294944 | tf_op jit(solution)/shard_map/up_corner_across_1/ppermute | solution.py:140
  77.4 1.4 branch.1.refs_2_
  78.9 1.1 collective-permute-start.23
  80.0 1.5 collective-permute-start.24
  82.2 6.6 %hidden_forward.1 = (bf16[1024,768]{1,0:T(8,128)(2,1)S(1)}, bf16[1024,1536]{1,0:T(8,128)(2,1)S(1)}, f32[2,1,1536]{2,1,0:T(1,128)S(1)}, f32[2,1,768]{2,1,0:T(1,128)S(1)}, bf16[768,1536]{1,0:T(8,128)(2,1)S(1)}) custom-call(s32[2]{0:T(128)S(1)} %bitcast.51, bf16[1024,768]{1,0:T(8,128)(2,1)S(1)} %order_tokens.1.refs_2_.refs_0_.refs_1_.refs_3_, ...), custom_call_target="tpu_custom_call" | custom-call | flops 2400000000 | bytes 20000000 | tf_op jit(solution)/shard_map/hidden_forward/pallas_call | solution.py:78
  91.6 1.3 collective-permute-start.28
  92.8 3.1 %collective-permute-start.26 = (f32[1,8,768]{2,1,0:T(8,128)S(1)}, f32[1,8,768]{2,1,0:T(8,128)S(1)}, u32[]{:S(2)}, u32[]{:S(2)}) collective-permute-start(f32[1,8,768]{2,1,0:T(8,128)S(1)} %bitcast.41), channel_id=1, source_target_pairs={{0,16},{2,18},{4,20},{6,22},{8,24},{10,26},{12,28},{14,30},{16,0},... | collective-permute-start | bytes 73736 | tf_op jit(solution)/shard_map/small_sums_across_8/ppermute | solution.py:140
  96.0 1.2 collective-permute-done.28.refs_3_
  98.0 2.3 %collective-permute-start.31 = (f32[4,8,768]{2,1,0:T(8,128)S(1)}, f32[4,8,768]{2,1,0:T(8,128)S(1)}, u32[]{:S(2)}, u32[]{:S(2)}) collective-permute-start(f32[4,8,768]{2,1,0:T(8,128)S(1)} %join.16.refs_7_.refs_0_), channel_id=1, source_target_pairs={{0,6},{2,4},{4,2},{6,0},{8,14},{10,12},{12,10},{14,8},{16,22},{18,... | collective-permute-start | bytes 294920 | tf_op jit(solution)/shard_map/small_sums_across_3/ppermute | solution.py:140
  101.5 2.1 %collective-permute-done.31.refs_10_.refs_3_ = f32[4,8,768]{2,1,0:T(8,128)S(1)} collective-permute-done((f32[4,8,768]{2,1,0:T(8,128)S(1)}, f32[4,8,768]{2,1,0:T(8,128)S(1)}, u32[]{:S(2)}, u32[]{:S(2)}) %collective-permute-start.31) | collective-permute-done | bytes 98336 | tf_op jit(solution)/shard_map/small_sums_across_3/ppermute | solution.py:140
  103.6 1.2 collective-permute-done.30.refs_9_.refs_2_
  105.5 4.2 %rank_backward.1 = (f32[8,768]{1,0:T(8,128)S(1)}, f32[8,1536]{1,0:T(8,128)}, f32[2,16,128]{2,1,0:T(8,128)S(1)}, bf16[1024,1536]{1,0:T(8,128)(2,1)S(1)}, bf16[1024,768]{1,0:T(8,128)(2,1)S(1)}) custom-call(s32[2]{0:T(128)S(1)} %bitcast.53, f32[2,16,128]{2,1,0:T(8,128)S(1)} %get-tuple-element.172.refs_1_, f32[2,16,128]{2,1,0:T(8,128)S(1)} %get-tuple-element.173.refs_2_, ...), custom_call_target="tpu_custom_call" | custom-call | flops 2400000000 | bytes 20000000 | tf_op jit(solution)/shard_map/rank_backward/pallas_call | solution.py:78
  109.8 2.6 %hidden_in_gradient.1 = (bf16[192,1536]{1,0:T(8,128)(2,1)S(1)}, bf16[192,1536]{1,0:T(8,128)(2,1)S(1)}, bf16[192,1536]{1,0:T(8,128)(2,1)S(1)}, bf16[96,1536]{1,0:T(8,128)(2,1)S(1)}, bf16[96,1536]{1,0:T(8,128)(2,1)S(1)}) custom-call(bf16[1024,768]{1,0:T(8,128)(2,1)S(1)} %get-tuple-element.194.refs_0_, bf16[1024,1536]{1,0:T(8,128)(2,1)S(1)} %get-tuple-element.195.refs_1_), custom_call_target="tpu_custom_call" | custom-call | flops 2400000000 | bytes 15000000 | tf_op jit(solution)/shard_map/hidden_in_gradient/pallas_call | solution.py:78
  112.4 1.4 collective-permute-start.37
  114.3 4.4 %middle_backward.1 = (f32[1024,768]{1,0:T(8,128)S(1)}, bf16[1024,384]{1,0:T(8,128)(2,1)S(1)}, f32[768,384]{1,0:T(8,128)S(1)}) custom-call(s32[2]{0:T(128)S(1)} %bitcast.54, bf16[1024,768]{1,0:T(8,128)(2,1)S(1)} %order_tokens.1.refs_2_.refs_0_.refs_1_.refs_3_, bf16[1024,768]{1,0:T(8,128)(2,1)S(1)} %branch.1.refs_2_, ...), custom_call_target="tpu_custom_call" | custom-call | flops 1200000000 | bytes 15000000 | tf_op jit(solution)/shard_map/middle_backward/pallas_call | solution.py:78
  118.7 3.2 %collective-permute-done.37.refs_2_ = bf16[96,1536]{1,0:T(8,128)(2,1)S(1)} collective-permute-done((bf16[96,1536]{1,0:T(8,128)(2,1)S(1)}, bf16[96,1536]{1,0:T(8,128)(2,1)S(1)}, u32[]{:S(2)}, u32[]{:S(2)}) %collective-permute-start.37) | collective-permute-done | bytes 294944 | tf_op jit(solution)/shard_map/up_gradient_across_1/ppermute | solution.py:140
  124.5 8.7 %attention_backward.2 = (bf16[3,3,1024,128]{3,2,1,0:T(8,128)(2,1)S(1)}, f32[2,8,128]{2,1,0:T(8,128)S(1)}, bf16[192,1152]{1,0:T(8,128)(2,1)S(1)}, bf16[192,1152]{...) custom-call(bf16[3,2,2,512,512]{4,3,2,1,0:T(8,128)(2,1)S(1)} %get-tu, ...), custom_call_target="tpu_custom_call" | custom-call | tf_op jit(solution)/shard_map/attention_backward/pallas_call | solution.py:78
  133.2 4.3 %attention_backward.3 = (bf16[3,3,1024,128]{3,2,1,0:T(8,128)(2,1)S(1)}, f32[1,8,128]{2,1,0:T(8,128)S(1)}, bf16[192,512]{1,0:T(8,128)(2,1)S(1)}, bf16[192,512]{1,...) custom-call(bf16[3,2,2,512,512]{4,3,2,1,0:T(8,128)(2,1)S(1)} %get-tu, ...), custom_call_target="tpu_custom_call", output_to_operand_aliasing={{0}: (7, {})} | custom-call | tf_op jit(solution)/shard_map/attention_backward/pallas_call | solution.py:78
  138.2 1.8 collective-permute-start.41
  140.8 1.5 collective-permute-start.34
  142.4 1.3 collective-permute-start.35
  144.1 3.4 %collective-permute-done.35.refs_6_ = bf16[96,512]{1,0:T(8,128)(2,1)S(1)} collective-permute-done((bf16[96,512]{1,0:T(8,128)(2,1)S(1)}, bf16[96,512]{1,0:T(8,128)(2,1)S(1)}, u32[]{:S(2)}, u32[]{:S(2)}) %collective-permute-start.35) | collective-permute-done | bytes 98336 | tf_op jit(solution)/shard_map/late_gradient_across_1/ppermute | solution.py:140
  148.7 1.6 collective-permute-start.42
  151.1 1.2 collective-permute-start.44
  152.3 3.2 %normed_backward.1.refs_5_ = bf16[1024,768]{1,0:T(8,128)(2,1)S(1)} custom-call(bf16[3,3,1024,128]{3,2,1,0:T(8,128)(2,1)S(1)} %get-tuple-element.212.refs_0_, bf16[192,1664]{1,0:T(8,128)(2,1)S(1)} %get-tuple-element.151.refs_1_.refs_10_, bf16[192,1664]{1,0:T(8,128)(2,1)S(1)} %collective-permute-done.5.refs_0_.refs_2_.refs_11_, ...), custom_call_target="tpu_custom_call" | custom-call | flops 1800000000 | bytes 15000000 | tf_op jit(solution)/shard_map/normed_backward/pallas_call | solution.py:78
  155.5 3.0 %collective-permute-done.44.refs_4_.refs_11_ = bf16[48,1536]{1,0:T(8,128)(2,1)S(1)} collective-permute-done((bf16[48,1536]{1,0:T(8,128)(2,1)S(1)}, bf16[48,1536]{1,0:T(8,128)(2,1)S(1)}, u32[]{:S(2)}, u32[]{:S(2)}) %collective-permute-start.44) | collective-permute-done | bytes 147488 | tf_op jit(solution)/shard_map/up_gradient_across_8/ppermute | solution.py:140
  161.3 6.3 %collective-permute-done.45.refs_1_ = bf16[96,1152]{1,0:T(8,128)(2,1)S(1)} collective-permute-done((bf16[96,1152]{1,0:T(8,128)(2,1)S(1)}, bf16[96,1152]{1,0:T(8,128)(2,1)S(1)}, u32[]{:S(2)}, u32[]{:S(2)}) %collective-permute-start.45) | collective-permute-done | bytes 221216 | tf_op jit(solution)/shard_map/early_gradient_across_4/ppermute | solution.py:140
  167.7 2.1 %collective-permute-start.49 = (bf16[48,512]{1,0:T(8,128)(2,1)S(1)}, bf16[48,512]{1,0:T(8,128)(2,1)S(1)}, u32[]{:S(2)}, u32[]{:S(2)}) collective-permute-start(bf16[48,512]{1,0:T(8,128)(2,1)S(1)} %get-tuple-element.219), channel_id=1, source_target_pairs={{0,16},{2,18},{4,20},{6,22},{8,24},{10,26},{12,28},{14,30},{16,0},... | collective-permute-start | bytes 147464 | tf_op jit(solution)/shard_map/late_gradient_across_8/ppermute | solution.py:140
  170.6 1.5 collective-permute-start.51
  172.2 1.1 collective-permute-start.46
  173.4 5.1 %token_gradient.1 = (f32[1024,768]{1,0:T(8,128)}, f32[8,128]{1,0:T(8,128)S(1)}) custom-call(f32[1024,768]{1,0:T(8,128)S(1)} %get-tuple-element.223.refs_0_, bf16[1024,768]{1,0:T(8,128)(2,1)S(1)} %get-tuple-element.224.refs_1_, bf16[1024,768]{1,0:T(8,128)(2,1)S(1)} %collective-permute-done.52.refs_2_, ...), custom_call_target="tpu_custom_call" | custom-call | flops 2400000000 | bytes 15000000 | tf_op jit(solution)/shard_map/token_gradient/pallas_call | solution.py:78
  178.7 1.9 collective-permute-done.46.refs_5_
  180.6 1.4 gradient_totals.1
  182.0 1.2 collective-permute-done.53.refs_1_
  183.2 1.8 collective-permute-start.56
  185.0 2.6 %collective-permute-start.54 = (f32[1,24,128]{2,1,0:T(8,128)S(1)}, f32[1,24,128]{2,1,0:T(8,128)S(1)}, u32[]{:S(2)}, u32[]{:S(2)}) collective-permute-start(f32[1,24,128]{2,1,0:T(8,128)S(1)} %bitcast.57), channel_id=1, source_target_pairs={{0,16},{2,18},{4,20},{6,22},{8,24},{10,26},{12,28},{14,30},{16,0},... | collective-permute-start | bytes 36872 | tf_op jit(solution)/shard_map/squares_across_8/ppermute | solution.py:140
  187.6 1.2 collective-permute-done.56.refs_3_
  190.7 1.5 collective-permute-start.58
  193.1 1.5 collective-permute-done.59.refs_6_
  194.8 1.5 collective-permute-done.57.refs_4_
  196.4 2.5 %update.1 = (f32[1,1]{1,0:T(1,128)}, f32[3,48,384]{2,1,0:T(8,128)}, f32[48,384]{1,0:T(8,128)}, f32[48,1536]{1,0:T(8,128)}, f32[48,1536]{1,0:T(8,128)}, /*index=5...) custom-call(s32[1]{0:T(128)} %bitcast.refs_0_, ...), custom_call_target="tpu_custom_call" | custom-call | bytes 6000000 | tf_op jit(solution)/shard_map/update/pallas_call | solution.py:78
  (162 shorter events, 32.2 us)
Async XLA Ops:
  2.5 18.6 %collective-permute-start.2 = (bf16[48,1664]{1,0:T(8,128)(2,1)}, bf16[48,1664]{1,0:T(8,128)(2,1)S(1)}, u32[]{:S(2)}, u32[]{:S(2)}) collective-permute-start(bf16[48,1664]{1,0:T(8,128)(2,1)} %pack_heads.1.refs_0_), channel_id=1, source_target_pairs={{0,24},{2,26},{4,28},{6,30},{8,16},{10,18},{12,20},{14,22},{16,8},... | collective-permute-start | bytes 479240 | tf_op jit(solution)/shard_map/heads_across_12/ppermute | solution.py:140
  7.5 13.5 %collective-permute-start.1 = (bf16[48,1664]{1,0:T(8,128)(2,1)}, bf16[48,1664]{1,0:T(8,128)(2,1)S(1)}, u32[]{:S(2)}, u32[]{:S(2)}) collective-permute-start(bf16[48,1664]{1,0:T(8,128)(2,1)} %pack_heads.1.refs_0_), channel_id=1, source_target_pairs={{0,8},{2,10},{4,12},{6,14},{8,0},{10,2},{12,4},{14,6},{16,24},{18,... | collective-permute-start | bytes 479240 | tf_op jit(solution)/shard_map/heads_across_4/ppermute | solution.py:140
  7.5 13.7 %collective-permute-start = (bf16[48,1664]{1,0:T(8,128)(2,1)}, bf16[48,1664]{1,0:T(8,128)(2,1)S(1)}, u32[]{:S(2)}, u32[]{:S(2)}) collective-permute-start(bf16[48,1664]{1,0:T(8,128)(2,1)} %pack_heads.1.refs_0_), channel_id=1, source_target_pairs={{0,16},{2,18},{4,20},{6,22},{8,24},{10,26},{12,28},{14,30},{16,0},... | collective-permute-start | bytes 479240 | tf_op jit(solution)/shard_map/heads_across_8/ppermute | solution.py:140
  10.1 11.0 %collective-permute-start.4 = (bf16[48,512]{1,0:T(8,128)(2,1)S(1)}, bf16[48,512]{1,0:T(8,128)(2,1)S(1)}, u32[]{:S(2)}, u32[]{:S(2)}) collective-permute-start(bf16[48,512]{1,0:T(8,128)(2,1)S(1)} %get-tuple-element.148.refs_0_), channel_id=1, source_target_pairs={{0,2},{2,0},{4,6},{6,4},{8,10},{10,8},{12,14},{14,12},{16,18},{18,... | collective-permute-start | bytes 147464 | tf_op jit(solution)/shard_map/down_plane_across_1/ppermute | solution.py:140
  11.8 9.2 %collective-permute-start.3 = (bf16[48,512]{1,0:T(8,128)(2,1)S(1)}, bf16[48,512]{1,0:T(8,128)(2,1)S(1)}, u32[]{:S(2)}, u32[]{:S(2)}) collective-permute-start(bf16[48,512]{1,0:T(8,128)(2,1)S(1)} %get-tuple-element.148.refs_0_), channel_id=1, source_target_pairs={{0,4},{2,6},{4,0},{6,2},{8,12},{10,14},{12,8},{14,10},{16,20},{18,... | collective-permute-start | bytes 147464 | tf_op jit(solution)/shard_map/down_plane_across_2/ppermute | solution.py:140
  22.3 16.6 %collective-permute-start.6 = (bf16[192,1664]{1,0:T(8,128)(2,1)S(1)}, bf16[192,1664]{1,0:T(8,128)(2,1)S(1)}, u32[]{:S(2)}, u32[]{:S(2)}) collective-permute-start(bf16[192,1664]{1,0:T(8,128)(2,1)S(1)} %get-tuple-element.151.refs_1_.refs_10_), channel_id=1, source_target_pairs={{0,2},{2,0},{4,6},{6,4},{8,10},{10,8},{12,14},{14,12},{16,18},{18,... | collective-permute-start | bytes 1916936 | tf_op jit(solution)/shard_map/heads_across_1/ppermute | solution.py:140
  23.8 15.2 %collective-permute-start.5 = (bf16[192,1664]{1,0:T(8,128)(2,1)S(1)}, bf16[192,1664]{1,0:T(8,128)(2,1)S(1)}, u32[]{:S(2)}, u32[]{:S(2)}) collective-permute-start(bf16[192,1664]{1,0:T(8,128)(2,1)S(1)} %get-tuple-element.151.refs_1_.refs_10_), channel_id=1, source_target_pairs={{0,4},{2,6},{4,0},{6,2},{8,12},{10,14},{12,8},{14,10},{16,20},{18,... | collective-permute-start | bytes 1916936 | tf_op jit(solution)/shard_map/heads_across_2/ppermute | solution.py:140
  25.3 8.0 %collective-permute-start.7 = (bf16[48,1536]{1,0:T(8,128)(2,1)S(1)}, bf16[48,1536]{1,0:T(8,128)(2,1)S(1)}, u32[]{:S(2)}, u32[]{:S(2)}) collective-permute-start(bf16[48,1536]{1,0:T(8,128)(2,1)S(1)} %get-tuple-element.152.refs_0_), channel_id=1, source_target_pairs={{0,16},{2,18},{4,20},{6,22},{8,24},{10,26},{12,28},{14,30},{16,0},... | collective-permute-start | bytes 442376 | tf_op jit(solution)/shard_map/up_across_8/ppermute | solution.py:140
  33.4 8.7 %collective-permute-start.12 = (bf16[96,1536]{1,0:T(8,128)(2,1)S(1)}, bf16[96,1536]{1,0:T(8,128)(2,1)S(1)}, u32[]{:S(2)}, u32[]{:S(2)}) collective-permute-start(bf16[96,1536]{1,0:T(8,128)(2,1)S(1)} %join.10.refs_2_.refs_0_), channel_id=1, source_target_pairs={{0,8},{2,10},{4,12},{6,14},{8,0},{10,2},{12,4},{14,6},{16,24},{18,... | collective-permute-start | bytes 884744 | tf_op jit(solution)/shard_map/up_across_4/ppermute | solution.py:140
  33.5 5.3 %collective-permute-start.8 = (bf16[48,512]{1,0:T(8,128)(2,1)S(1)}, bf16[48,512]{1,0:T(8,128)(2,1)S(1)}, u32[]{:S(2)}, u32[]{:S(2)}) collective-permute-start(bf16[48,512]{1,0:T(8,128)(2,1)S(1)} %collective-permute-done.3.refs_7_.refs_1_), channel_id=1, source_target_pairs={{0,2},{2,0},{4,6},{6,4},{8,10},{10,8},{12,14},{14,12},{16,18},{18,... | collective-permute-start | bytes 147464 | tf_op jit(solution)/shard_map/down_plane_corner_across_1/ppermute | solution.py:140
  39.0 10.5 %collective-permute-start.10 = (bf16[96,1664]{1,0:T(8,128)(2,1)S(1)}, bf16[96,1664]{1,0:T(8,128)(2,1)S(1)}, u32[]{:S(2)}, u32[]{:S(2)}) collective-permute-start(bf16[96,1664]{1,0:T(8,128)(2,1)S(1)} %get-tuple-element.155), channel_id=1, source_target_pairs={{0,4},{2,6},{4,0},{6,2},{8,12},{10,14},{12,8},{14,10},{16,20},{18,... | collective-permute-start | bytes 958472 | tf_op jit(solution)/shard_map/heads_corner_across_2/ppermute | solution.py:140
  40.6 10.5 %collective-permute-start.9 = (bf16[96,1664]{1,0:T(8,128)(2,1)S(1)}, bf16[96,1664]{1,0:T(8,128)(2,1)S(1)}, u32[]{:S(2)}, u32[]{:S(2)}) collective-permute-start(bf16[96,1664]{1,0:T(8,128)(2,1)S(1)} %get-tuple-element.154.refs_2_), channel_id=1, source_target_pairs={{0,2},{2,0},{4,6},{6,4},{8,10},{10,8},{12,14},{14,12},{16,18},{18,... | collective-permute-start | bytes 958472 | tf_op jit(solution)/shard_map/heads_corner_across_1/ppermute | solution.py:140
  42.0 6.0 %collective-permute-start.11 = (bf16[48,1024]{1,0:T(8,128)(2,1)S(1)}, bf16[48,1024]{1,0:T(8,128)(2,1)S(1)}, u32[]{:S(2)}, u32[]{:S(2)}) collective-permute-start(bf16[48,1024]{1,0:T(8,128)(2,1)S(1)} %get-tuple-element.157.refs_0_), channel_id=1, source_target_pairs={{0,16},{2,18},{4,20},{6,22},{8,24},{10,26},{12,28},{14,30},{16,0},... | collective-permute-start | bytes 294920 | tf_op jit(solution)/shard_map/down_across_8/ppermute | solution.py:140
  42.1 27.5 %collective-permute-start.14 = (bf16[192,1536]{1,0:T(8,128)(2,1)S(1)}, bf16[192,1536]{1,0:T(8,128)(2,1)S(1)}, u32[]{:S(2)}, u32[]{:S(2)}) collective-permute-start(bf16[192,1536]{1,0:T(8,128)(2,1)S(1)} %join.11.refs_2_.refs_5_), channel_id=1, source_target_pairs={{0,2},{2,0},{4,6},{6,4},{8,10},{10,8},{12,14},{14,12},{16,18},{18,... | collective-permute-start | bytes 1769480 | tf_op jit(solution)/shard_map/up_across_1/ppermute | solution.py:140
  43.1 26.5 %collective-permute-start.13 = (bf16[192,1536]{1,0:T(8,128)(2,1)S(1)}, bf16[192,1536]{1,0:T(8,128)(2,1)S(1)}, u32[]{:S(2)}, u32[]{:S(2)}) collective-permute-start(bf16[192,1536]{1,0:T(8,128)(2,1)S(1)} %join.11.refs_2_.refs_5_), channel_id=1, source_target_pairs={{0,4},{2,6},{4,0},{6,2},{8,12},{10,14},{12,8},{14,10},{16,20},{18,... | collective-permute-start | bytes 1769480 | tf_op jit(solution)/shard_map/up_across_2/ppermute | solution.py:140
  48.0 10.2 %collective-permute-start.17 = (bf16[96,1024]{1,0:T(8,128)(2,1)S(1)}, bf16[96,1024]{1,0:T(8,128)(2,1)S(1)}, u32[]{:S(2)}, u32[]{:S(2)}) collective-permute-start(bf16[96,1024]{1,0:T(8,128)(2,1)S(1)} %join.12.refs_3_.refs_0_), channel_id=1, source_target_pairs={{0,8},{2,10},{4,12},{6,14},{8,0},{10,2},{12,4},{14,6},{16,24},{18,... | collective-permute-start | bytes 589832 | tf_op jit(solution)/shard_map/down_across_4/ppermute | solution.py:140
  58.2 9.1 %collective-permute-start.20 = (bf16[192,512]{1,0:T(8,128)(2,1)S(1)}, bf16[192,512]{1,0:T(8,128)(2,1)S(1)}, u32[]{:S(2)}, u32[]{:S(2)}) collective-permute-start(bf16[192,512]{1,0:T(8,128)(2,1)S(1)} %join.14.refs_0_), channel_id=1, source_target_pairs={{0,16},{2,18},{4,20},{6,22},{8,24},{10,26},{12,28},{14,30},{16,0},... | collective-permute-start | bytes 589832 | tf_op jit(solution)/shard_map/down_plane_across_8/ppermute | solution.py:140
  58.3 14.1 %collective-permute-start.19 = (bf16[192,1024]{1,0:T(8,128)(2,1)S(1)}, bf16[192,1024]{1,0:T(8,128)(2,1)S(1)}, u32[]{:S(2)}, u32[]{:S(2)}) collective-permute-start(bf16[192,1024]{1,0:T(8,128)(2,1)S(1)} %join.13.refs_4_.refs_1_), channel_id=1, source_target_pairs={{0,2},{2,0},{4,6},{6,4},{8,10},{10,8},{12,14},{14,12},{16,18},{18,... | collective-permute-start | bytes 1179656 | tf_op jit(solution)/shard_map/down_across_1/ppermute | solution.py:140
  59.8 12.7 %collective-permute-start.18 = (bf16[192,1024]{1,0:T(8,128)(2,1)S(1)}, bf16[192,1024]{1,0:T(8,128)(2,1)S(1)}, u32[]{:S(2)}, u32[]{:S(2)}) collective-permute-start(bf16[192,1024]{1,0:T(8,128)(2,1)S(1)} %join.13.refs_4_.refs_1_), channel_id=1, source_target_pairs={{0,4},{2,6},{4,0},{6,2},{8,12},{10,14},{12,8},{14,10},{16,20},{18,... | collective-permute-start | bytes 1179656 | tf_op jit(solution)/shard_map/down_across_2/ppermute | solution.py:140
  67.4 10.0 %collective-permute-start.21 = (bf16[384,512]{1,0:T(8,128)(2,1)S(1)}, bf16[384,512]{1,0:T(8,128)(2,1)S(1)}, u32[]{:S(2)}, u32[]{:S(2)}) collective-permute-start(bf16[384,512]{1,0:T(8,128)(2,1)S(1)} %join.15.refs_10_.refs_6_), channel_id=1, source_target_pairs={{0,8},{2,10},{4,12},{6,14},{8,0},{10,2},{12,4},{14,6},{16,24},{18,... | collective-permute-start | bytes 1179656 | tf_op jit(solution)/shard_map/down_plane_across_4/ppermute | solution.py:140
  69.7 6.8 %collective-permute-start.15 = (bf16[96,1536]{1,0:T(8,128)(2,1)S(1)}, bf16[96,1536]{1,0:T(8,128)(2,1)S(1)}, u32[]{:S(2)}, u32[]{:S(2)}) collective-permute-start(bf16[96,1536]{1,0:T(8,128)(2,1)S(1)} %get-tuple-element.162), channel_id=1, source_target_pairs={{0,2},{2,0},{4,6},{6,4},{8,10},{10,8},{12,14},{14,12},{16,18},{18,... | collective-permute-start | bytes 884744 | tf_op jit(solution)/shard_map/up_corner_across_1/ppermute | solution.py:140
  70.7 6.7 %collective-permute-start.16 = (bf16[96,1536]{1,0:T(8,128)(2,1)S(1)}, bf16[96,1536]{1,0:T(8,128)(2,1)S(1)}, u32[]{:S(2)}, u32[]{:S(2)}) collective-permute-start(bf16[96,1536]{1,0:T(8,128)(2,1)S(1)} %get-tuple-element.163), channel_id=1, source_target_pairs={{0,4},{2,6},{4,0},{6,2},{8,12},{10,14},{12,8},{14,10},{16,20},{18,... | collective-permute-start | bytes 884744 | tf_op jit(solution)/shard_map/up_corner_across_2/ppermute | solution.py:140
  78.8 3.5 %collective-permute-start.22 = (bf16[1024,768]{1,0:T(8,128)(2,1)S(1)}, bf16[1024,768]{1,0:T(8,128)(2,1)S(1)}, u32[]{:S(2)}, u32[]{:S(2)}) collective-permute-start(bf16[1024,768]{1,0:T(8,128)(2,1)S(1)} %branch.1.refs_2_), channel_id=1, source_target_pairs={{0,1},{1,0},{2,3},{3,2},{4,5},{5,4},{6,7},{7,6},{8,9},{9,8},{10,11... | collective-permute-start | bytes 4718600 | tf_op jit(solution)/shard_map/branch_other_core/ppermute | solution.py:149
  78.9 10.0 %collective-permute-start.23 = (bf16[96,1024]{1,0:T(8,128)(2,1)S(1)}, bf16[96,1024]{1,0:T(8,128)(2,1)S(1)}, u32[]{:S(2)}, u32[]{:S(2)}) collective-permute-start(bf16[96,1024]{1,0:T(8,128)(2,1)S(1)} %get-tuple-element.167), channel_id=1, source_target_pairs={{0,2},{2,0},{4,6},{6,4},{8,10},{10,8},{12,14},{14,12},{16,18},{18,... | collective-permute-start | bytes 589832 | tf_op jit(solution)/shard_map/down_corner_across_1/ppermute | solution.py:140
  80.0 8.9 %collective-permute-start.24 = (bf16[96,1024]{1,0:T(8,128)(2,1)S(1)}, bf16[96,1024]{1,0:T(8,128)(2,1)S(1)}, u32[]{:S(2)}, u32[]{:S(2)}) collective-permute-start(bf16[96,1024]{1,0:T(8,128)(2,1)S(1)} %get-tuple-element.168), channel_id=1, source_target_pairs={{0,4},{2,6},{4,0},{6,2},{8,12},{10,14},{12,8},{14,10},{16,20},{18,... | collective-permute-start | bytes 589832 | tf_op jit(solution)/shard_map/down_corner_across_2/ppermute | solution.py:140
  89.6 1.2 collective-permute-start.25
  91.6 5.6 %collective-permute-start.28 = (f32[1,8,768]{2,1,0:T(8,128)S(1)}, f32[1,8,768]{2,1,0:T(8,128)S(1)}, u32[]{:S(2)}, u32[]{:S(2)}) collective-permute-start(f32[1,8,768]{2,1,0:T(8,128)S(1)} %bitcast.39), channel_id=1, source_target_pairs={{0,24},{2,26},{4,28},{6,30},{8,16},{10,18},{12,20},{14,22},{16,8},... | collective-permute-start | bytes 73736 | tf_op jit(solution)/shard_map/small_sums_across_12/ppermute | solution.py:140
  92.8 4.4 %collective-permute-start.27 = (f32[1,8,768]{2,1,0:T(8,128)S(1)}, f32[1,8,768]{2,1,0:T(8,128)S(1)}, u32[]{:S(2)}, u32[]{:S(2)}) collective-permute-start(f32[1,8,768]{2,1,0:T(8,128)S(1)} %bitcast.40), channel_id=1, source_target_pairs={{0,8},{2,10},{4,12},{6,14},{8,0},{10,2},{12,4},{14,6},{16,24},{18,... | collective-permute-start | bytes 73736 | tf_op jit(solution)/shard_map/small_sums_across_4/ppermute | solution.py:140
  92.8 5.1 %collective-permute-start.26 = (f32[1,8,768]{2,1,0:T(8,128)S(1)}, f32[1,8,768]{2,1,0:T(8,128)S(1)}, u32[]{:S(2)}, u32[]{:S(2)}) collective-permute-start(f32[1,8,768]{2,1,0:T(8,128)S(1)} %bitcast.41), channel_id=1, source_target_pairs={{0,16},{2,18},{4,20},{6,22},{8,24},{10,26},{12,28},{14,30},{16,0},... | collective-permute-start | bytes 73736 | tf_op jit(solution)/shard_map/small_sums_across_8/ppermute | solution.py:140
  98.0 5.7 %collective-permute-start.31 = (f32[4,8,768]{2,1,0:T(8,128)S(1)}, f32[4,8,768]{2,1,0:T(8,128)S(1)}, u32[]{:S(2)}, u32[]{:S(2)}) collective-permute-start(f32[4,8,768]{2,1,0:T(8,128)S(1)} %join.16.refs_7_.refs_0_), channel_id=1, source_target_pairs={{0,6},{2,4},{4,2},{6,0},{8,14},{10,12},{12,10},{14,8},{16,22},{18,... | collective-permute-start | bytes 294920 | tf_op jit(solution)/shard_map/small_sums_across_3/ppermute | solution.py:140
  100.2 4.6 %collective-permute-start.30 = (f32[4,8,768]{2,1,0:T(8,128)S(1)}, f32[4,8,768]{2,1,0:T(8,128)S(1)}, u32[]{:S(2)}, u32[]{:S(2)}) collective-permute-start(f32[4,8,768]{2,1,0:T(8,128)S(1)} %join.16.refs_7_.refs_0_), channel_id=1, source_target_pairs={{0,2},{2,0},{4,6},{6,4},{8,10},{10,8},{12,14},{14,12},{16,18},{18,... | collective-permute-start | bytes 294920 | tf_op jit(solution)/shard_map/small_sums_across_1/ppermute | solution.py:140
  100.9 4.6 %collective-permute-start.29 = (f32[4,8,768]{2,1,0:T(8,128)S(1)}, f32[4,8,768]{2,1,0:T(8,128)S(1)}, u32[]{:S(2)}, u32[]{:S(2)}) collective-permute-start(f32[4,8,768]{2,1,0:T(8,128)S(1)} %join.16.refs_7_.refs_0_), channel_id=1, source_target_pairs={{0,4},{2,6},{4,0},{6,2},{8,12},{10,14},{12,8},{14,10},{16,20},{18,... | collective-permute-start | bytes 294920 | tf_op jit(solution)/shard_map/small_sums_across_2/ppermute | solution.py:140
  109.7 4.6 %collective-permute-start.32 = (bf16[1024,768]{1,0:T(8,128)(2,1)S(1)}, bf16[1024,768]{1,0:T(8,128)(2,1)S(1)}, u32[]{:S(2)}, u32[]{:S(2)}) collective-permute-start(bf16[1024,768]{1,0:T(8,128)(2,1)S(1)} %get-tuple-element.177.refs_4_), channel_id=1, source_target_pairs={{0,1},{1,0},{2,3},{3,2},{4,5},{5,4},{6,7},{7,6},{8,9},{9,8},{10,11... | collective-permute-start | bytes 4718600 | tf_op jit(solution)/shard_map/second_gradient_other_core/ppermute | solution.py:149
  112.4 9.5 %collective-permute-start.37 = (bf16[96,1536]{1,0:T(8,128)(2,1)S(1)}, bf16[96,1536]{1,0:T(8,128)(2,1)S(1)}, u32[]{:S(2)}, u32[]{:S(2)}) collective-permute-start(bf16[96,1536]{1,0:T(8,128)(2,1)S(1)} %get-tuple-element.199), channel_id=1, source_target_pairs={{0,2},{2,0},{4,6},{6,4},{8,10},{10,8},{12,14},{14,12},{16,18},{18,... | collective-permute-start | bytes 884744 | tf_op jit(solution)/shard_map/up_gradient_across_1/ppermute | solution.py:140
  113.8 9.1 %collective-permute-start.38 = (bf16[96,1536]{1,0:T(8,128)(2,1)S(1)}, bf16[96,1536]{1,0:T(8,128)(2,1)S(1)}, u32[]{:S(2)}, u32[]{:S(2)}) collective-permute-start(bf16[96,1536]{1,0:T(8,128)(2,1)S(1)} %get-tuple-element.200), channel_id=1, source_target_pairs={{0,4},{2,6},{4,0},{6,2},{8,12},{10,14},{12,8},{14,10},{16,20},{18,... | collective-permute-start | bytes 884744 | tf_op jit(solution)/shard_map/up_gradient_across_2/ppermute | solution.py:140
  123.1 14.7 %collective-permute-start.39 = (bf16[192,1536]{1,0:T(8,128)(2,1)S(1)}, bf16[192,1536]{1,0:T(8,128)(2,1)S(1)}, u32[]{:S(2)}, u32[]{:S(2)}) collective-permute-start(bf16[192,1536]{1,0:T(8,128)(2,1)S(1)} %get-tuple-element.201), channel_id=1, source_target_pairs={{0,4},{2,6},{4,0},{6,2},{8,12},{10,14},{12,8},{14,10},{16,20},{18,... | collective-permute-start | bytes 1769480 | tf_op jit(solution)/shard_map/up_gradient_across_2/ppermute | solution.py:140
  123.7 14.3 %collective-permute-start.40 = (bf16[192,1536]{1,0:T(8,128)(2,1)S(1)}, bf16[192,1536]{1,0:T(8,128)(2,1)S(1)}, u32[]{:S(2)}, u32[]{:S(2)}) collective-permute-start(bf16[192,1536]{1,0:T(8,128)(2,1)S(1)} %get-tuple-element.202), channel_id=1, source_target_pairs={{0,2},{2,0},{4,6},{6,4},{8,10},{10,8},{12,14},{14,12},{16,18},{18,... | collective-permute-start | bytes 1769480 | tf_op jit(solution)/shard_map/up_gradient_across_1/ppermute | solution.py:140
  138.2 10.3 %collective-permute-start.41 = (bf16[96,1536]{1,0:T(8,128)(2,1)S(1)}, bf16[96,1536]{1,0:T(8,128)(2,1)S(1)}, u32[]{:S(2)}, u32[]{:S(2)}) collective-permute-start(bf16[96,1536]{1,0:T(8,128)(2,1)S(1)} %get-tuple-element.204), channel_id=1, source_target_pairs={{0,8},{2,10},{4,12},{6,14},{8,0},{10,2},{12,4},{14,6},{16,24},{18,... | collective-permute-start | bytes 884744 | tf_op jit(solution)/shard_map/up_gradient_across_4/ppermute | solution.py:140
  140.1 8.5 %collective-permute-start.33 = (bf16[96,1152]{1,0:T(8,128)(2,1)S(1)}, bf16[96,1152]{1,0:T(8,128)(2,1)S(1)}, u32[]{:S(2)}, u32[]{:S(2)}) collective-permute-start(bf16[96,1152]{1,0:T(8,128)(2,1)S(1)} %get-tuple-element.186), channel_id=1, source_target_pairs={{0,2},{2,0},{4,6},{6,4},{8,10},{10,8},{12,14},{14,12},{16,18},{18,... | collective-permute-start | bytes 663560 | tf_op jit(solution)/shard_map/early_gradient_across_1/ppermute | solution.py:140
  140.8 7.7 %collective-permute-start.34 = (bf16[96,1152]{1,0:T(8,128)(2,1)S(1)}, bf16[96,1152]{1,0:T(8,128)(2,1)S(1)}, u32[]{:S(2)}, u32[]{:S(2)}) collective-permute-start(bf16[96,1152]{1,0:T(8,128)(2,1)S(1)} %get-tuple-element.187), channel_id=1, source_target_pairs={{0,4},{2,6},{4,0},{6,2},{8,12},{10,14},{12,8},{14,10},{16,20},{18,... | collective-permute-start | bytes 663560 | tf_op jit(solution)/shard_map/early_gradient_across_2/ppermute | solution.py:140
  142.4 5.1 %collective-permute-start.35 = (bf16[96,512]{1,0:T(8,128)(2,1)S(1)}, bf16[96,512]{1,0:T(8,128)(2,1)S(1)}, u32[]{:S(2)}, u32[]{:S(2)}) collective-permute-start(bf16[96,512]{1,0:T(8,128)(2,1)S(1)} %get-tuple-element.192), channel_id=1, source_target_pairs={{0,2},{2,0},{4,6},{6,4},{8,10},{10,8},{12,14},{14,12},{16,18},{18,... | collective-permute-start | bytes 294920 | tf_op jit(solution)/shard_map/late_gradient_across_1/ppermute | solution.py:140
  143.6 4.9 %collective-permute-start.36 = (bf16[96,512]{1,0:T(8,128)(2,1)S(1)}, bf16[96,512]{1,0:T(8,128)(2,1)S(1)}, u32[]{:S(2)}, u32[]{:S(2)}) collective-permute-start(bf16[96,512]{1,0:T(8,128)(2,1)S(1)} %get-tuple-element.193), channel_id=1, source_target_pairs={{0,4},{2,6},{4,0},{6,2},{8,12},{10,14},{12,8},{14,10},{16,20},{18,... | collective-permute-start | bytes 294920 | tf_op jit(solution)/shard_map/late_gradient_across_2/ppermute | solution.py:140
  148.7 9.8 %collective-permute-start.42 = (bf16[192,1152]{1,0:T(8,128)(2,1)S(1)}, bf16[192,1152]{1,0:T(8,128)(2,1)S(1)}, u32[]{:S(2)}, u32[]{:S(2)}) collective-permute-start(bf16[192,1152]{1,0:T(8,128)(2,1)S(1)} %get-tuple-element.205.refs_2_.refs_6_), channel_id=1, source_target_pairs={{0,4},{2,6},{4,0},{6,2},{8,12},{10,14},{12,8},{14,10},{16,20},{18,... | collective-permute-start | bytes 1327112 | tf_op jit(solution)/shard_map/early_gradient_across_2/ppermute | solution.py:140
  150.3 9.1 %collective-permute-start.43 = (bf16[192,1152]{1,0:T(8,128)(2,1)S(1)}, bf16[192,1152]{1,0:T(8,128)(2,1)S(1)}, u32[]{:S(2)}, u32[]{:S(2)}) collective-permute-start(bf16[192,1152]{1,0:T(8,128)(2,1)S(1)} %get-tuple-element.206.refs_3_.refs_7_), channel_id=1, source_target_pairs={{0,2},{2,0},{4,6},{6,4},{8,10},{10,8},{12,14},{14,12},{16,18},{18,... | collective-permute-start | bytes 1327112 | tf_op jit(solution)/shard_map/early_gradient_across_1/ppermute | solution.py:140
  151.1 7.5 %collective-permute-start.44 = (bf16[48,1536]{1,0:T(8,128)(2,1)S(1)}, bf16[48,1536]{1,0:T(8,128)(2,1)S(1)}, u32[]{:S(2)}, u32[]{:S(2)}) collective-permute-start(bf16[48,1536]{1,0:T(8,128)(2,1)S(1)} %get-tuple-element.211), channel_id=1, source_target_pairs={{0,16},{2,18},{4,20},{6,22},{8,24},{10,26},{12,28},{14,30},{16,0},... | collective-permute-start | bytes 442376 | tf_op jit(solution)/shard_map/up_gradient_across_8/ppermute | solution.py:140
  159.6 13.7 %collective-permute-start.52 = (bf16[1024,768]{1,0:T(8,128)(2,1)S(1)}, bf16[1024,768]{1,0:T(8,128)(2,1)S(1)}, u32[]{:S(2)}, u32[]{:S(2)}) collective-permute-start(bf16[1024,768]{1,0:T(8,128)(2,1)S(1)} %get-tuple-element.224.refs_1_), channel_id=1, source_target_pairs={{0,1},{1,0},{2,3},{3,2},{4,5},{5,4},{6,7},{7,6},{8,9},{9,8},{10,11... | collective-permute-start | bytes 4718600 | tf_op jit(solution)/shard_map/first_gradient_other_core/ppermute | solution.py:149
  159.7 7.8 %collective-permute-start.45 = (bf16[96,1152]{1,0:T(8,128)(2,1)S(1)}, bf16[96,1152]{1,0:T(8,128)(2,1)S(1)}, u32[]{:S(2)}, u32[]{:S(2)}) collective-permute-start(bf16[96,1152]{1,0:T(8,128)(2,1)S(1)} %get-tuple-element.214), channel_id=1, source_target_pairs={{0,8},{2,10},{4,12},{6,14},{8,0},{10,2},{12,4},{14,6},{16,24},{18,... | collective-permute-start | bytes 663560 | tf_op jit(solution)/shard_map/early_gradient_across_4/ppermute | solution.py:140
  160.2 7.4 %collective-permute-start.47 = (bf16[192,512]{1,0:T(8,128)(2,1)S(1)}, bf16[192,512]{1,0:T(8,128)(2,1)S(1)}, u32[]{:S(2)}, u32[]{:S(2)}) collective-permute-start(bf16[192,512]{1,0:T(8,128)(2,1)S(1)} %get-tuple-element.208.refs_4_.refs_8_), channel_id=1, source_target_pairs={{0,4},{2,6},{4,0},{6,2},{8,12},{10,14},{12,8},{14,10},{16,20},{18,... | collective-permute-start | bytes 589832 | tf_op jit(solution)/shard_map/late_gradient_across_2/ppermute | solution.py:140
  160.7 6.9 %collective-permute-start.48 = (bf16[192,512]{1,0:T(8,128)(2,1)S(1)}, bf16[192,512]{1,0:T(8,128)(2,1)S(1)}, u32[]{:S(2)}, u32[]{:S(2)}) collective-permute-start(bf16[192,512]{1,0:T(8,128)(2,1)S(1)} %get-tuple-element.209.refs_5_.refs_9_), channel_id=1, source_target_pairs={{0,2},{2,0},{4,6},{6,4},{8,10},{10,8},{12,14},{14,12},{16,18},{18,... | collective-permute-start | bytes 589832 | tf_op jit(solution)/shard_map/late_gradient_across_1/ppermute | solution.py:140
  167.7 10.9 %collective-permute-start.49 = (bf16[48,512]{1,0:T(8,128)(2,1)S(1)}, bf16[48,512]{1,0:T(8,128)(2,1)S(1)}, u32[]{:S(2)}, u32[]{:S(2)}) collective-permute-start(bf16[48,512]{1,0:T(8,128)(2,1)S(1)} %get-tuple-element.219), channel_id=1, source_target_pairs={{0,16},{2,18},{4,20},{6,22},{8,24},{10,26},{12,28},{14,30},{16,0},... | collective-permute-start | bytes 147464 | tf_op jit(solution)/shard_map/late_gradient_across_8/ppermute | solution.py:140
  169.8 8.8 %collective-permute-start.50 = (bf16[48,512]{1,0:T(8,128)(2,1)S(1)}, bf16[48,512]{1,0:T(8,128)(2,1)S(1)}, u32[]{:S(2)}, u32[]{:S(2)}) collective-permute-start(bf16[48,512]{1,0:T(8,128)(2,1)S(1)} %get-tuple-element.220), channel_id=1, source_target_pairs={{0,8},{2,10},{4,12},{6,14},{8,0},{10,2},{12,4},{14,6},{16,24},{18,... | collective-permute-start | bytes 147464 | tf_op jit(solution)/shard_map/late_gradient_across_4/ppermute | solution.py:140
  170.6 8.0 %collective-permute-start.51 = (bf16[48,512]{1,0:T(8,128)(2,1)S(1)}, bf16[48,512]{1,0:T(8,128)(2,1)S(1)}, u32[]{:S(2)}, u32[]{:S(2)}) collective-permute-start(bf16[48,512]{1,0:T(8,128)(2,1)S(1)} %get-tuple-element.221), channel_id=1, source_target_pairs={{0,24},{2,26},{4,28},{6,30},{8,16},{10,18},{12,20},{14,22},{16,8},... | collective-permute-start | bytes 147464 | tf_op jit(solution)/shard_map/late_gradient_across_12/ppermute | solution.py:140
  172.2 8.4 %collective-permute-start.46 = (bf16[48,1152]{1,0:T(8,128)(2,1)S(1)}, bf16[48,1152]{1,0:T(8,128)(2,1)S(1)}, u32[]{:S(2)}, u32[]{:S(2)}) collective-permute-start(bf16[48,1152]{1,0:T(8,128)(2,1)S(1)} %get-tuple-element.216), channel_id=1, source_target_pairs={{0,16},{2,18},{4,20},{6,22},{8,24},{10,26},{12,28},{14,30},{16,0},... | collective-permute-start | bytes 331784 | tf_op jit(solution)/shard_map/early_gradient_across_8/ppermute | solution.py:140
  173.3 23.0 %copy-start.13 = (f32[3,48,384]{2,1,0:T(8,128)S(1)}, f32[3,48,384]{2,1,0:T(8,128)}, u32[]{:S(2)}) copy-start(f32[3,48,384]{2,1,0:T(8,128)} %get-tuple-element.236.refs_18_) | copy-start | bytes 663556
  173.3 22.9 %copy-start.14 = (f32[3,48,384]{2,1,0:T(8,128)S(1)}, f32[3,48,384]{2,1,0:T(8,128)}, u32[]{:S(2)}) copy-start(f32[3,48,384]{2,1,0:T(8,128)} %get-tuple-element.240.refs_25_) | copy-start | bytes 663556
  173.3 22.9 %copy-start.17 = (f32[48,384]{1,0:T(8,128)S(1)}, f32[48,384]{1,0:T(8,128)}, u32[]{:S(2)}) copy-start(f32[48,384]{1,0:T(8,128)} %get-tuple-element.241.refs_26_) | copy-start | bytes 221188
  173.4 22.9 %copy-start.26 = (f32[48,3]{0,1:T(4,128)S(1)}, f32[48,3]{0,1:T(4,128)}, u32[]{:S(2)}) copy-start(f32[48,3]{0,1:T(4,128)} %param.49) | copy-start | bytes 1732
  181.9 1.2 collective-permute-start.53
  183.2 5.6 %collective-permute-start.56 = (f32[1,24,128]{2,1,0:T(8,128)S(1)}, f32[1,24,128]{2,1,0:T(8,128)S(1)}, u32[]{:S(2)}, u32[]{:S(2)}) collective-permute-start(f32[1,24,128]{2,1,0:T(8,128)S(1)} %bitcast.55), channel_id=1, source_target_pairs={{0,24},{2,26},{4,28},{6,30},{8,16},{10,18},{12,20},{14,22},{16,8},... | collective-permute-start | bytes 36872 | tf_op jit(solution)/shard_map/squares_across_12/ppermute | solution.py:140
  185.0 3.8 %collective-permute-start.55 = (f32[1,24,128]{2,1,0:T(8,128)S(1)}, f32[1,24,128]{2,1,0:T(8,128)S(1)}, u32[]{:S(2)}, u32[]{:S(2)}) collective-permute-start(f32[1,24,128]{2,1,0:T(8,128)S(1)} %bitcast.56), channel_id=1, source_target_pairs={{0,8},{2,10},{4,12},{6,14},{8,0},{10,2},{12,4},{14,6},{16,24},{18,... | collective-permute-start | bytes 36872 | tf_op jit(solution)/shard_map/squares_across_4/ppermute | solution.py:140
  185.0 4.6 %collective-permute-start.54 = (f32[1,24,128]{2,1,0:T(8,128)S(1)}, f32[1,24,128]{2,1,0:T(8,128)S(1)}, u32[]{:S(2)}, u32[]{:S(2)}) collective-permute-start(f32[1,24,128]{2,1,0:T(8,128)S(1)} %bitcast.57), channel_id=1, source_target_pairs={{0,16},{2,18},{4,20},{6,22},{8,24},{10,26},{12,28},{14,30},{16,0},... | collective-permute-start | bytes 36872 | tf_op jit(solution)/shard_map/squares_across_8/ppermute | solution.py:140
  189.6 5.0 %collective-permute-start.59 = (f32[4,24,128]{2,1,0:T(8,128)S(1)}, f32[4,24,128]{2,1,0:T(8,128)S(1)}, u32[]{:S(2)}, u32[]{:S(2)}) collective-permute-start(f32[4,24,128]{2,1,0:T(8,128)S(1)} %join.17.refs_3_), channel_id=1, source_target_pairs={{0,6},{2,4},{4,2},{6,0},{8,14},{10,12},{12,10},{14,8},{16,22},{18,... | collective-permute-start | bytes 147464 | tf_op jit(solution)/shard_map/squares_across_3/ppermute | solution.py:140
  190.7 4.1 %collective-permute-start.58 = (f32[4,24,128]{2,1,0:T(8,128)S(1)}, f32[4,24,128]{2,1,0:T(8,128)S(1)}, u32[]{:S(2)}, u32[]{:S(2)}) collective-permute-start(f32[4,24,128]{2,1,0:T(8,128)S(1)} %join.17.refs_3_), channel_id=1, source_target_pairs={{0,2},{2,0},{4,6},{6,4},{8,10},{10,8},{12,14},{14,12},{16,18},{18,... | collective-permute-start | bytes 147464 | tf_op jit(solution)/shard_map/squares_across_1/ppermute | solution.py:140
  192.2 4.1 %collective-permute-start.57 = (f32[4,24,128]{2,1,0:T(8,128)S(1)}, f32[4,24,128]{2,1,0:T(8,128)S(1)}, u32[]{:S(2)}, u32[]{:S(2)}) collective-permute-start(f32[4,24,128]{2,1,0:T(8,128)S(1)} %join.17.refs_3_), channel_id=1, source_target_pairs={{0,4},{2,6},{4,0},{6,2},{8,12},{10,14},{12,8},{14,10},{16,20},{18,... | collective-permute-start | bytes 147464 | tf_op jit(solution)/shard_map/squares_across_2/ppermute | solution.py:140
  (27 other events, 336.8 us)

commit v2 on v1

--- a/solution.py
+++ b/solution.py
@@ -1458,7 +1458,7 @@
     turned_first = call(turn_kernel, "turn", shape_of((width, count), low_type))(normed_first)
     attended, probs, inverse = filled
     branch = branch_rows(
-        attended, weight_heads, (*up_corner, *down_sides, *planes, turned_first) if size == 16 else ()
+        attended, weight_heads, (low, plane_pair, *down_sides, turned_first) if size == 16 else ()
     )
     if size == 16:
         low, high = gather_step(*down_sides, deps=(branch,))
@@ -1511,7 +1511,7 @@
     )
     late_sum = Scatter(g_late, size, "late_gradient")
     up_sum.near(deps=(table,))
-    sides = scatter_sides([early_sum, late_sum], deps=tuple(up_sum.came))
+    sides = scatter_sides([early_sum, late_sum], deps=up_sum.sources)
     d_normed_first = normed_back(d_project, weight_heads, sides)
     up_parts = up_sum.far(deps=sides)
     (d_normed_first,) = early_sum.near(deps=tuple(up_parts), passing=(d_normed_first,))

time: 199 us -> 197 us (0.990)
  waiting for transfers between devices: 57.7 us -> 55.5 us
  transfers between devices with their start and end apart: 60 -> 60, of which waited for: 32 -> 34; matrix products, arithmetic and copies ran while one was open for 0% -> 0% of each run, Pallas kernels for 28% -> 29%
where the time goes in v2:
time: 197 us
  Pallas kernels  69.6 us (35%)
  starting transfers between devices  63.9 us (32%)
  waiting for transfers between devices  55.5 us (28%)
  local copies, waits for them, and re-layouts  5.06 us (3%)
  between operations  2.38 us (1%)
    pallas_call x42, Pallas kernels, apply(): pl.pallas_call(run, out_shape=[*out_shapes, *(shape_of(a.shape, a.dtype)...  69.6 us
    ppermute x55, starting transfers between devices, swap(): return lax.ppermute(array, 'dp', [(i, i ^ mask) for i in range(size)])  63.6 us
    ppermute x55, waiting for transfers between devices, swap(): return lax.ppermute(array, 'dp', [(i, i ^ mask) for i in range(size)])  53.1 us
    unnamed x62, local copies, waits for them, and re-layouts  4.37 us
  transfers between devices with their start and end apart: 60, of which 34 were waited for; matrix products, arithmetic and copies ran while one was open for 0% of the time, Pallas kernels for 29%

profile of v2, /device:TPU:0, one launch (start us, length us, event | category | flops | bytes accessed | tf_op | source)
XLA Modules:
  0.0 196.5 jit_solution(15304771543580943322)
XLA Ops:
  0.7 1.8 pack_heads.1.refs_0_
  2.5 5.0 %collective-permute-start.2 = (bf16[48,1664]{1,0:T(8,128)(2,1)}, bf16[48,1664]{1,0:T(8,128)(2,1)S(1)}, u32[]{:S(2)}, u32[]{:S(2)}) collective-permute-start(bf16[48,1664]{1,0:T(8,128)(2,1)} %pack_heads.1.refs_0_), channel_id=1, source_target_pairs={{0,24},{2,26},{4,28},{6,30},{8,16},{10,18},{12,20},{14,22},{16,8},... | collective-permute-start | bytes 479240 | tf_op jit(solution)/shard_map/heads_across_12/ppermute | solution.py:140
  10.1 1.8 collective-permute-start.4
  11.8 1.5 collective-permute-start.3
  16.3 1.4 prepare.1
  17.7 3.3 %stage.1 = (f32[3,48,384]{2,1,0:T(8,128)}, f32[48,384]{1,0:T(8,128)}, f32[48,1536]{1,0:T(8,128)}, f32[48,1536]{1,0:T(8,128)}, f32[3,48,384]{2,1,0:T(8,128)}, /*i...) custom-call(f32[3,48,384]{2,1,0:T(8,128)} %bitcast.37, ...), custom_call_target="tpu_custom_call" | custom-call | tf_op jit(solution)/shard_map/stage/pallas_call | solution.py:78
  22.3 1.6 collective-permute-start.6
  23.8 1.5 collective-permute-start.5
  25.6 1.9 order_tokens.1.refs_2_.refs_0_.refs_1_.refs_3_
  27.5 5.9 %collective-permute-done.7.refs_1_ = bf16[48,1536]{1,0:T(8,128)(2,1)S(1)} collective-permute-done((bf16[48,1536]{1,0:T(8,128)(2,1)S(1)}, bf16[48,1536]{1,0:T(8,128)(2,1)S(1)}, u32[]{:S(2)}, u32[]{:S(2)}) %collective-permute-start.7) | collective-permute-done | bytes 147488 | tf_op jit(solution)/shard_map/up_across_8/ppermute | solution.py:140
  34.1 4.7 %collective-permute-done.8.refs_3_ = bf16[48,512]{1,0:T(8,128)(2,1)S(1)} collective-permute-done((bf16[48,512]{1,0:T(8,128)(2,1)S(1)}, bf16[48,512]{1,0:T(8,128)(2,1)S(1)}, u32[]{:S(2)}, u32[]{:S(2)}) %collective-permute-start.8) | collective-permute-done | bytes 49184 | tf_op jit(solution)/shard_map/down_plane_corner_across_1/ppermute | solution.py:140
  39.0 1.6 collective-permute-start.10
  40.6 1.3 collective-permute-start.9
  43.1 4.8 %collective-permute-done.11.refs_1_ = bf16[48,1024]{1,0:T(8,128)(2,1)S(1)} collective-permute-done((bf16[48,1024]{1,0:T(8,128)(2,1)S(1)}, bf16[48,1024]{1,0:T(8,128)(2,1)S(1)}, u32[]{:S(2)}, u32[]{:S(2)}) %collective-permute-start.11) | collective-permute-done | bytes 98336 | tf_op jit(solution)/shard_map/down_across_8/ppermute | solution.py:140
  48.6 2.5 %collective-permute-done.9.refs_4_.refs_13_ = bf16[96,1664]{1,0:T(8,128)(2,1)S(1)} collective-permute-done((bf16[96,1664]{1,0:T(8,128)(2,1)S(1)}, bf16[96,1664]{1,0:T(8,128)(2,1)S(1)}, u32[]{:S(2)}, u32[]{:S(2)}) %collective-permute-start.9) | collective-permute-done | bytes 319520 | tf_op jit(solution)/shard_map/heads_corner_across_1/ppermute | solution.py:140
  51.1 3.6 %projection.1 = (bf16[3,3,1024,128]{3,2,1,0:T(8,128)(2,1)S(1)}, bf16[1024,768]{1,0:T(8,128)(2,1)S(1)}, f32[8,768]{1,0:T(8,128)S(1)}) custom-call(bf16[1024,768]{1,0:T(8,128)(2,1)S(1)} %order_tokens.1.refs_2_.refs_0_.refs_1_.refs_3_, bf16[192,1664]{1,0:T(8,128)(2,1)S(1)} %get-tuple-element.151.refs_1_.refs_10_, ...), custom_call_target="tpu_custom_call" | custom-call | tf_op jit(solution)/shard_map/projection/pallas_call | solution.py:78
  54.7 3.5 %attention_forward.2 = (bf16[1024,384]{1,0:T(8,128)(2,1)S(1)}, bf16[3,2,2,512,512]{4,3,2,1,0:T(8,128)(2,1)S(1)}, f32[1024,384]{1,0:T(8,128)S(1)}) custom-call(s32[2]{0:T(128)S(1)} %bitcast.49, f32[3,2,1024]{2,1,0:T(2,128)S(1)} %get-tuple-element.146.refs_1_, bf16[3,3,1024,128]{3,2,1,0:T(8,128)(2,1)S(1)} %get-tuple-element.156.refs_2_.refs_1_, ...), custom_call_target="tpu_custom_call" | custom-call | tf_op jit(solution)/shard_map/attention_forward/pallas_call | solution.py:78
  58.2 1.4 collective-permute-start.18
  61.4 6.5 %attention_forward.3 = (bf16[1024,384]{1,0:T(8,128)(2,1)S(1)}, bf16[3,2,2,512,512]{4,3,2,1,0:T(8,128)(2,1)S(1)}, f32[1024,384]{1,0:T(8,128)S(1)}) custom-call(s32[2]{0:T(128)S(1)} %bitcast.50, f32[3,2,1024]{2,1,0:T(2,128)S(1)} %get-tuple-element.146.refs_1_, ...), custom_call_target="tpu_custom_call", output_to_operand_aliasing={{0}: (3, {}), {1}: (4, {}), {2}: (5, {})} | custom-call | tf_op jit(solution)/shard_map/attention_forward/pallas_call | solution.py:78
  68.9 1.3 branch.1.refs_2_
  72.4 1.5 collective-permute-start.24
  74.0 1.4 collective-permute-start.22
  75.4 4.4 %collective-permute-done.21.refs_9_ = bf16[96,1536]{1,0:T(8,128)(2,1)S(1)} collective-permute-done((bf16[96,1536]{1,0:T(8,128)(2,1)S(1)}, bf16[96,1536]{1,0:T(8,128)(2,1)S(1)}, u32[]{:S(2)}, u32[]{:S(2)}) %collective-permute-start.21) | collective-permute-done | bytes 294944 | tf_op jit(solution)/shard_map/up_corner_across_2/ppermute | solution.py:140
  81.3 6.6 %hidden_forward.1 = (bf16[1024,768]{1,0:T(8,128)(2,1)S(1)}, bf16[1024,1536]{1,0:T(8,128)(2,1)S(1)}, f32[2,1,1536]{2,1,0:T(1,128)S(1)}, f32[2,1,768]{2,1,0:T(1,128)S(1)}, bf16[768,1536]{1,0:T(8,128)(2,1)S(1)}) custom-call(s32[2]{0:T(128)S(1)} %bitcast.51, bf16[1024,768]{1,0:T(8,128)(2,1)S(1)} %order_tokens.1.refs_2_.refs_0_.refs_1_.refs_3_, ...), custom_call_target="tpu_custom_call" | custom-call | flops 2400000000 | bytes 20000000 | tf_op jit(solution)/shard_map/hidden_forward/pallas_call | solution.py:78
  88.7 1.2 collective-permute-done.25.refs_2_
  90.6 1.9 collective-permute-start.28
  93.1 1.9 collective-permute-start.26
  95.0 1.6 collective-permute-done.28.refs_3_
  97.8 1.9 collective-permute-start.31
  100.3 1.1 collective-permute-start.29
  101.4 2.0 %collective-permute-done.31.refs_10_.refs_3_ = f32[4,8,768]{2,1,0:T(8,128)S(1)} collective-permute-done((f32[4,8,768]{2,1,0:T(8,128)S(1)}, f32[4,8,768]{2,1,0:T(8,128)S(1)}, u32[]{:S(2)}, u32[]{:S(2)}) %collective-permute-start.31) | collective-permute-done | bytes 98336 | tf_op jit(solution)/shard_map/small_sums_across_3/ppermute | solution.py:140
  104.9 4.2 %rank_backward.1 = (f32[8,768]{1,0:T(8,128)S(1)}, f32[8,1536]{1,0:T(8,128)}, f32[2,16,128]{2,1,0:T(8,128)S(1)}, bf16[1024,1536]{1,0:T(8,128)(2,1)S(1)}, bf16[1024,768]{1,0:T(8,128)(2,1)S(1)}) custom-call(s32[2]{0:T(128)S(1)} %bitcast.53, f32[2,16,128]{2,1,0:T(8,128)S(1)} %get-tuple-element.172.refs_1_, f32[2,16,128]{2,1,0:T(8,128)S(1)} %get-tuple-element.173.refs_2_, ...), custom_call_target="tpu_custom_call" | custom-call | flops 2400000000 | bytes 20000000 | tf_op jit(solution)/shard_map/rank_backward/pallas_call | solution.py:78
  109.2 2.6 %hidden_in_gradient.1 = (bf16[192,1536]{1,0:T(8,128)(2,1)S(1)}, bf16[192,1536]{1,0:T(8,128)(2,1)S(1)}, bf16[192,1536]{1,0:T(8,128)(2,1)S(1)}, bf16[96,1536]{1,0:T(8,128)(2,1)S(1)}, bf16[96,1536]{1,0:T(8,128)(2,1)S(1)}) custom-call(bf16[1024,768]{1,0:T(8,128)(2,1)S(1)} %get-tuple-element.194.refs_0_, bf16[1024,1536]{1,0:T(8,128)(2,1)S(1)} %get-tuple-element.195.refs_1_), custom_call_target="tpu_custom_call" | custom-call | flops 2400000000 | bytes 15000000 | tf_op jit(solution)/shard_map/hidden_in_gradient/pallas_call | solution.py:78
  111.8 1.6 collective-permute-start.37
  114.0 4.4 %middle_backward.1 = (f32[1024,768]{1,0:T(8,128)S(1)}, bf16[1024,384]{1,0:T(8,128)(2,1)S(1)}, f32[768,384]{1,0:T(8,128)S(1)}) custom-call(s32[2]{0:T(128)S(1)} %bitcast.54, bf16[1024,768]{1,0:T(8,128)(2,1)S(1)} %order_tokens.1.refs_2_.refs_0_.refs_1_.refs_3_, bf16[1024,768]{1,0:T(8,128)(2,1)S(1)} %branch.1.refs_2_, ...), custom_call_target="tpu_custom_call" | custom-call | flops 1200000000 | bytes 15000000 | tf_op jit(solution)/shard_map/middle_backward/pallas_call | solution.py:78
  118.3 3.0 %collective-permute-done.37.refs_2_ = bf16[96,1536]{1,0:T(8,128)(2,1)S(1)} collective-permute-done((bf16[96,1536]{1,0:T(8,128)(2,1)S(1)}, bf16[96,1536]{1,0:T(8,128)(2,1)S(1)}, u32[]{:S(2)}, u32[]{:S(2)}) %collective-permute-start.37) | collective-permute-done | bytes 294944 | tf_op jit(solution)/shard_map/up_gradient_across_1/ppermute | solution.py:140
  121.3 1.2 collective-permute-done.38.refs_3_
  124.4 8.7 %attention_backward.2 = (bf16[3,3,1024,128]{3,2,1,0:T(8,128)(2,1)S(1)}, f32[2,8,128]{2,1,0:T(8,128)S(1)}, bf16[192,1152]{1,0:T(8,128)(2,1)S(1)}, bf16[192,1152]{...) custom-call(bf16[3,2,2,512,512]{4,3,2,1,0:T(8,128)(2,1)S(1)} %get-tu, ...), custom_call_target="tpu_custom_call" | custom-call | tf_op jit(solution)/shard_map/attention_backward/pallas_call | solution.py:78
  134.1 1.5 collective-permute-start.34
  135.6 4.3 %attention_backward.3 = (bf16[3,3,1024,128]{3,2,1,0:T(8,128)(2,1)S(1)}, f32[1,8,128]{2,1,0:T(8,128)S(1)}, bf16[192,512]{1,0:T(8,128)(2,1)S(1)}, bf16[192,512]{1,...) custom-call(bf16[3,2,2,512,512]{4,3,2,1,0:T(8,128)(2,1)S(1)} %get-tu, ...), custom_call_target="tpu_custom_call", output_to_operand_aliasing={{0}: (7, {})} | custom-call | tf_op jit(solution)/shard_map/attention_backward/pallas_call | solution.py:78
  140.5 1.1 collective-permute-start.36
  141.8 1.5 collective-permute-start.43
  143.3 1.2 collective-permute-done.35.refs_6_
  145.3 1.2 collective-permute-start.41
  147.4 1.2 collective-permute-done.43.refs_1_
  148.6 2.0 %collective-permute-start.44 = (bf16[48,1536]{1,0:T(8,128)(2,1)S(1)}, bf16[48,1536]{1,0:T(8,128)(2,1)S(1)}, u32[]{:S(2)}, u32[]{:S(2)}) collective-permute-start(bf16[48,1536]{1,0:T(8,128)(2,1)S(1)} %get-tuple-element.211), channel_id=1, source_target_pairs={{0,16},{2,18},{4,20},{6,22},{8,24},{10,26},{12,28},{14,30},{16,0},... | collective-permute-start | bytes 442376 | tf_op jit(solution)/shard_map/up_gradient_across_8/ppermute | solution.py:140
  150.6 3.2 %normed_backward.1.refs_5_ = bf16[1024,768]{1,0:T(8,128)(2,1)S(1)} custom-call(bf16[3,3,1024,128]{3,2,1,0:T(8,128)(2,1)S(1)} %get-tuple-element.212.refs_0_, bf16[192,1664]{1,0:T(8,128)(2,1)S(1)} %get-tuple-element.151.refs_1_.refs_10_, bf16[192,1664]{1,0:T(8,128)(2,1)S(1)} %collective-permute-done.5.refs_0_.refs_2_.refs_11_, ...), custom_call_target="tpu_custom_call" | custom-call | flops 1800000000 | bytes 15000000 | tf_op jit(solution)/shard_map/normed_backward/pallas_call | solution.py:78
  153.9 2.5 %collective-permute-done.44.refs_4_.refs_11_ = bf16[48,1536]{1,0:T(8,128)(2,1)S(1)} collective-permute-done((bf16[48,1536]{1,0:T(8,128)(2,1)S(1)}, bf16[48,1536]{1,0:T(8,128)(2,1)S(1)}, u32[]{:S(2)}, u32[]{:S(2)}) %collective-permute-start.44) | collective-permute-done | bytes 147488 | tf_op jit(solution)/shard_map/up_gradient_across_8/ppermute | solution.py:140
  156.6 1.7 collective-permute-start.45
  158.3 1.1 collective-permute-start.47
  160.0 4.4 %collective-permute-done.45.refs_1_ = bf16[96,1152]{1,0:T(8,128)(2,1)S(1)} collective-permute-done((bf16[96,1152]{1,0:T(8,128)(2,1)S(1)}, bf16[96,1152]{1,0:T(8,128)(2,1)S(1)}, u32[]{:S(2)}, u32[]{:S(2)}) %collective-permute-start.45) | collective-permute-done | bytes 221216 | tf_op jit(solution)/shard_map/early_gradient_across_4/ppermute | solution.py:140
  166.8 1.7 collective-permute-start.50
  168.5 2.1 %collective-permute-start.51 = (bf16[48,512]{1,0:T(8,128)(2,1)S(1)}, bf16[48,512]{1,0:T(8,128)(2,1)S(1)}, u32[]{:S(2)}, u32[]{:S(2)}) collective-permute-start(bf16[48,512]{1,0:T(8,128)(2,1)S(1)} %get-tuple-element.221), channel_id=1, source_target_pairs={{0,24},{2,26},{4,28},{6,30},{8,16},{10,18},{12,20},{14,22},{16,8},... | collective-permute-start | bytes 147464 | tf_op jit(solution)/shard_map/late_gradient_across_12/ppermute | solution.py:140
  170.7 5.1 %token_gradient.1 = (f32[1024,768]{1,0:T(8,128)}, f32[8,128]{1,0:T(8,128)S(1)}) custom-call(f32[1024,768]{1,0:T(8,128)S(1)} %get-tuple-element.223.refs_0_, bf16[1024,768]{1,0:T(8,128)(2,1)S(1)} %get-tuple-element.224.refs_1_, bf16[1024,768]{1,0:T(8,128)(2,1)S(1)} %collective-permute-done.52.refs_2_, ...), custom_call_target="tpu_custom_call" | custom-call | flops 2400000000 | bytes 15000000 | tf_op jit(solution)/shard_map/token_gradient/pallas_call | solution.py:78
  176.0 1.8 collective-permute-done.46.refs_5_
  177.8 1.4 gradient_totals.1
  179.2 1.2 collective-permute-done.53.refs_1_
  180.5 2.0 %collective-permute-start.56 = (f32[1,24,128]{2,1,0:T(8,128)S(1)}, f32[1,24,128]{2,1,0:T(8,128)S(1)}, u32[]{:S(2)}, u32[]{:S(2)}) collective-permute-start(f32[1,24,128]{2,1,0:T(8,128)S(1)} %bitcast.55), channel_id=1, source_target_pairs={{0,24},{2,26},{4,28},{6,30},{8,16},{10,18},{12,20},{14,22},{16,8},... | collective-permute-start | bytes 36872 | tf_op jit(solution)/shard_map/squares_across_12/ppermute | solution.py:140
  182.5 2.4 %collective-permute-start.54 = (f32[1,24,128]{2,1,0:T(8,128)S(1)}, f32[1,24,128]{2,1,0:T(8,128)S(1)}, u32[]{:S(2)}, u32[]{:S(2)}) collective-permute-start(f32[1,24,128]{2,1,0:T(8,128)S(1)} %bitcast.57), channel_id=1, source_target_pairs={{0,16},{2,18},{4,20},{6,22},{8,24},{10,26},{12,28},{14,30},{16,0},... | collective-permute-start | bytes 36872 | tf_op jit(solution)/shard_map/squares_across_8/ppermute | solution.py:140
  184.9 1.2 collective-permute-done.56.refs_3_
  188.2 1.4 collective-permute-start.58
  190.6 1.5 collective-permute-done.59.refs_6_
  192.3 1.4 collective-permute-done.57.refs_4_
  193.8 2.5 %update.1 = (f32[1,1]{1,0:T(1,128)}, f32[3,48,384]{2,1,0:T(8,128)}, f32[48,384]{1,0:T(8,128)}, f32[48,1536]{1,0:T(8,128)}, f32[48,1536]{1,0:T(8,128)}, /*index=5...) custom-call(s32[1]{0:T(128)} %bitcast.refs_0_, ...), custom_call_target="tpu_custom_call" | custom-call | bytes 6000000 | tf_op jit(solution)/shard_map/update/pallas_call | solution.py:78
  (162 shorter events, 33.4 us)
Async XLA Ops:
  2.5 18.6 %collective-permute-start.2 = (bf16[48,1664]{1,0:T(8,128)(2,1)}, bf16[48,1664]{1,0:T(8,128)(2,1)S(1)}, u32[]{:S(2)}, u32[]{:S(2)}) collective-permute-start(bf16[48,1664]{1,0:T(8,128)(2,1)} %pack_heads.1.refs_0_), channel_id=1, source_target_pairs={{0,24},{2,26},{4,28},{6,30},{8,16},{10,18},{12,20},{14,22},{16,8},... | collective-permute-start | bytes 479240 | tf_op jit(solution)/shard_map/heads_across_12/ppermute | solution.py:140
  7.5 13.5 %collective-permute-start.1 = (bf16[48,1664]{1,0:T(8,128)(2,1)}, bf16[48,1664]{1,0:T(8,128)(2,1)S(1)}, u32[]{:S(2)}, u32[]{:S(2)}) collective-permute-start(bf16[48,1664]{1,0:T(8,128)(2,1)} %pack_heads.1.refs_0_), channel_id=1, source_target_pairs={{0,8},{2,10},{4,12},{6,14},{8,0},{10,2},{12,4},{14,6},{16,24},{18,... | collective-permute-start | bytes 479240 | tf_op jit(solution)/shard_map/heads_across_4/ppermute | solution.py:140
  7.5 13.7 %collective-permute-start = (bf16[48,1664]{1,0:T(8,128)(2,1)}, bf16[48,1664]{1,0:T(8,128)(2,1)S(1)}, u32[]{:S(2)}, u32[]{:S(2)}) collective-permute-start(bf16[48,1664]{1,0:T(8,128)(2,1)} %pack_heads.1.refs_0_), channel_id=1, source_target_pairs={{0,16},{2,18},{4,20},{6,22},{8,24},{10,26},{12,28},{14,30},{16,0},... | collective-permute-start | bytes 479240 | tf_op jit(solution)/shard_map/heads_across_8/ppermute | solution.py:140
  10.1 11.0 %collective-permute-start.4 = (bf16[48,512]{1,0:T(8,128)(2,1)S(1)}, bf16[48,512]{1,0:T(8,128)(2,1)S(1)}, u32[]{:S(2)}, u32[]{:S(2)}) collective-permute-start(bf16[48,512]{1,0:T(8,128)(2,1)S(1)} %get-tuple-element.148.refs_0_), channel_id=1, source_target_pairs={{0,2},{2,0},{4,6},{6,4},{8,10},{10,8},{12,14},{14,12},{16,18},{18,... | collective-permute-start | bytes 147464 | tf_op jit(solution)/shard_map/down_plane_across_1/ppermute | solution.py:140
  11.8 9.2 %collective-permute-start.3 = (bf16[48,512]{1,0:T(8,128)(2,1)S(1)}, bf16[48,512]{1,0:T(8,128)(2,1)S(1)}, u32[]{:S(2)}, u32[]{:S(2)}) collective-permute-start(bf16[48,512]{1,0:T(8,128)(2,1)S(1)} %get-tuple-element.148.refs_0_), channel_id=1, source_target_pairs={{0,4},{2,6},{4,0},{6,2},{8,12},{10,14},{12,8},{14,10},{16,20},{18,... | collective-permute-start | bytes 147464 | tf_op jit(solution)/shard_map/down_plane_across_2/ppermute | solution.py:140
  22.3 16.6 %collective-permute-start.6 = (bf16[192,1664]{1,0:T(8,128)(2,1)S(1)}, bf16[192,1664]{1,0:T(8,128)(2,1)S(1)}, u32[]{:S(2)}, u32[]{:S(2)}) collective-permute-start(bf16[192,1664]{1,0:T(8,128)(2,1)S(1)} %get-tuple-element.151.refs_1_.refs_10_), channel_id=1, source_target_pairs={{0,2},{2,0},{4,6},{6,4},{8,10},{10,8},{12,14},{14,12},{16,18},{18,... | collective-permute-start | bytes 1916936 | tf_op jit(solution)/shard_map/heads_across_1/ppermute | solution.py:140
  23.8 15.2 %collective-permute-start.5 = (bf16[192,1664]{1,0:T(8,128)(2,1)S(1)}, bf16[192,1664]{1,0:T(8,128)(2,1)S(1)}, u32[]{:S(2)}, u32[]{:S(2)}) collective-permute-start(bf16[192,1664]{1,0:T(8,128)(2,1)S(1)} %get-tuple-element.151.refs_1_.refs_10_), channel_id=1, source_target_pairs={{0,4},{2,6},{4,0},{6,2},{8,12},{10,14},{12,8},{14,10},{16,20},{18,... | collective-permute-start | bytes 1916936 | tf_op jit(solution)/shard_map/heads_across_2/ppermute | solution.py:140
  25.3 8.0 %collective-permute-start.7 = (bf16[48,1536]{1,0:T(8,128)(2,1)S(1)}, bf16[48,1536]{1,0:T(8,128)(2,1)S(1)}, u32[]{:S(2)}, u32[]{:S(2)}) collective-permute-start(bf16[48,1536]{1,0:T(8,128)(2,1)S(1)} %get-tuple-element.152.refs_0_), channel_id=1, source_target_pairs={{0,16},{2,18},{4,20},{6,22},{8,24},{10,26},{12,28},{14,30},{16,0},... | collective-permute-start | bytes 442376 | tf_op jit(solution)/shard_map/up_across_8/ppermute | solution.py:140
  33.4 8.7 %collective-permute-start.12 = (bf16[96,1536]{1,0:T(8,128)(2,1)S(1)}, bf16[96,1536]{1,0:T(8,128)(2,1)S(1)}, u32[]{:S(2)}, u32[]{:S(2)}) collective-permute-start(bf16[96,1536]{1,0:T(8,128)(2,1)S(1)} %join.10.refs_2_.refs_0_), channel_id=1, source_target_pairs={{0,8},{2,10},{4,12},{6,14},{8,0},{10,2},{12,4},{14,6},{16,24},{18,... | collective-permute-start | bytes 884744 | tf_op jit(solution)/shard_map/up_across_4/ppermute | solution.py:140
  33.5 5.3 %collective-permute-start.8 = (bf16[48,512]{1,0:T(8,128)(2,1)S(1)}, bf16[48,512]{1,0:T(8,128)(2,1)S(1)}, u32[]{:S(2)}, u32[]{:S(2)}) collective-permute-start(bf16[48,512]{1,0:T(8,128)(2,1)S(1)} %collective-permute-done.3.refs_7_.refs_1_), channel_id=1, source_target_pairs={{0,2},{2,0},{4,6},{6,4},{8,10},{10,8},{12,14},{14,12},{16,18},{18,... | collective-permute-start | bytes 147464 | tf_op jit(solution)/shard_map/down_plane_corner_across_1/ppermute | solution.py:140
  39.0 9.6 %collective-permute-start.10 = (bf16[96,1664]{1,0:T(8,128)(2,1)S(1)}, bf16[96,1664]{1,0:T(8,128)(2,1)S(1)}, u32[]{:S(2)}, u32[]{:S(2)}) collective-permute-start(bf16[96,1664]{1,0:T(8,128)(2,1)S(1)} %get-tuple-element.155), channel_id=1, source_target_pairs={{0,4},{2,6},{4,0},{6,2},{8,12},{10,14},{12,8},{14,10},{16,20},{18,... | collective-permute-start | bytes 958472 | tf_op jit(solution)/shard_map/heads_corner_across_2/ppermute | solution.py:140
  40.6 10.5 %collective-permute-start.9 = (bf16[96,1664]{1,0:T(8,128)(2,1)S(1)}, bf16[96,1664]{1,0:T(8,128)(2,1)S(1)}, u32[]{:S(2)}, u32[]{:S(2)}) collective-permute-start(bf16[96,1664]{1,0:T(8,128)(2,1)S(1)} %get-tuple-element.154.refs_2_), channel_id=1, source_target_pairs={{0,2},{2,0},{4,6},{6,4},{8,10},{10,8},{12,14},{14,12},{16,18},{18,... | collective-permute-start | bytes 958472 | tf_op jit(solution)/shard_map/heads_corner_across_1/ppermute | solution.py:140
  42.0 6.0 %collective-permute-start.11 = (bf16[48,1024]{1,0:T(8,128)(2,1)S(1)}, bf16[48,1024]{1,0:T(8,128)(2,1)S(1)}, u32[]{:S(2)}, u32[]{:S(2)}) collective-permute-start(bf16[48,1024]{1,0:T(8,128)(2,1)S(1)} %get-tuple-element.157.refs_0_), channel_id=1, source_target_pairs={{0,16},{2,18},{4,20},{6,22},{8,24},{10,26},{12,28},{14,30},{16,0},... | collective-permute-start | bytes 294920 | tf_op jit(solution)/shard_map/down_across_8/ppermute | solution.py:140
  42.1 26.2 %collective-permute-start.14 = (bf16[192,1536]{1,0:T(8,128)(2,1)S(1)}, bf16[192,1536]{1,0:T(8,128)(2,1)S(1)}, u32[]{:S(2)}, u32[]{:S(2)}) collective-permute-start(bf16[192,1536]{1,0:T(8,128)(2,1)S(1)} %join.11.refs_2_.refs_5_), channel_id=1, source_target_pairs={{0,2},{2,0},{4,6},{6,4},{8,10},{10,8},{12,14},{14,12},{16,18},{18,... | collective-permute-start | bytes 1769480 | tf_op jit(solution)/shard_map/up_across_1/ppermute | solution.py:140
  48.0 10.2 %collective-permute-start.15 = (bf16[96,1024]{1,0:T(8,128)(2,1)S(1)}, bf16[96,1024]{1,0:T(8,128)(2,1)S(1)}, u32[]{:S(2)}, u32[]{:S(2)}) collective-permute-start(bf16[96,1024]{1,0:T(8,128)(2,1)S(1)} %join.12.refs_3_.refs_0_), channel_id=1, source_target_pairs={{0,8},{2,10},{4,12},{6,14},{8,0},{10,2},{12,4},{14,6},{16,24},{18,... | collective-permute-start | bytes 589832 | tf_op jit(solution)/shard_map/down_across_4/ppermute | solution.py:140
  48.1 20.2 %collective-permute-start.13 = (bf16[192,1536]{1,0:T(8,128)(2,1)S(1)}, bf16[192,1536]{1,0:T(8,128)(2,1)S(1)}, u32[]{:S(2)}, u32[]{:S(2)}) collective-permute-start(bf16[192,1536]{1,0:T(8,128)(2,1)S(1)} %join.11.refs_2_.refs_5_), channel_id=1, source_target_pairs={{0,4},{2,6},{4,0},{6,2},{8,12},{10,14},{12,8},{14,10},{16,20},{18,... | collective-permute-start | bytes 1769480 | tf_op jit(solution)/shard_map/up_across_2/ppermute | solution.py:140
  58.2 10.7 %collective-permute-start.18 = (bf16[192,1024]{1,0:T(8,128)(2,1)S(1)}, bf16[192,1024]{1,0:T(8,128)(2,1)S(1)}, u32[]{:S(2)}, u32[]{:S(2)}) collective-permute-start(bf16[192,1024]{1,0:T(8,128)(2,1)S(1)} %join.13.refs_4_.refs_1_), channel_id=1, source_target_pairs={{0,2},{2,0},{4,6},{6,4},{8,10},{10,8},{12,14},{14,12},{16,18},{18,... | collective-permute-start | bytes 1179656 | tf_op jit(solution)/shard_map/down_across_1/ppermute | solution.py:140
  59.6 9.3 %collective-permute-start.17 = (bf16[192,1024]{1,0:T(8,128)(2,1)S(1)}, bf16[192,1024]{1,0:T(8,128)(2,1)S(1)}, u32[]{:S(2)}, u32[]{:S(2)}) collective-permute-start(bf16[192,1024]{1,0:T(8,128)(2,1)S(1)} %join.13.refs_4_.refs_1_), channel_id=1, source_target_pairs={{0,4},{2,6},{4,0},{6,2},{8,12},{10,14},{12,8},{14,10},{16,20},{18,... | collective-permute-start | bytes 1179656 | tf_op jit(solution)/shard_map/down_across_2/ppermute | solution.py:140
  60.1 8.1 %collective-permute-start.16 = (bf16[192,512]{1,0:T(8,128)(2,1)S(1)}, bf16[192,512]{1,0:T(8,128)(2,1)S(1)}, u32[]{:S(2)}, u32[]{:S(2)}) collective-permute-start(bf16[192,512]{1,0:T(8,128)(2,1)S(1)} %join.14.refs_0_), channel_id=1, source_target_pairs={{0,16},{2,18},{4,20},{6,22},{8,24},{10,26},{12,28},{14,30},{16,0},... | collective-permute-start | bytes 589832 | tf_op jit(solution)/shard_map/down_plane_across_8/ppermute | solution.py:140
  70.3 11.0 %collective-permute-start.19 = (bf16[1024,768]{1,0:T(8,128)(2,1)S(1)}, bf16[1024,768]{1,0:T(8,128)(2,1)S(1)}, u32[]{:S(2)}, u32[]{:S(2)}) collective-permute-start(bf16[1024,768]{1,0:T(8,128)(2,1)S(1)} %branch.1.refs_2_), channel_id=1, source_target_pairs={{0,1},{1,0},{2,3},{3,2},{4,5},{5,4},{6,7},{7,6},{8,9},{9,8},{10,11... | collective-permute-start | bytes 4718600 | tf_op jit(solution)/shard_map/branch_other_core/ppermute | solution.py:149
  70.4 9.4 %collective-permute-start.21 = (bf16[96,1536]{1,0:T(8,128)(2,1)S(1)}, bf16[96,1536]{1,0:T(8,128)(2,1)S(1)}, u32[]{:S(2)}, u32[]{:S(2)}) collective-permute-start(bf16[96,1536]{1,0:T(8,128)(2,1)S(1)} %get-tuple-element.165), channel_id=1, source_target_pairs={{0,4},{2,6},{4,0},{6,2},{8,12},{10,14},{12,8},{14,10},{16,20},{18,... | collective-permute-start | bytes 884744 | tf_op jit(solution)/shard_map/up_corner_across_2/ppermute | solution.py:140
  71.4 9.9 %collective-permute-start.20 = (bf16[96,1536]{1,0:T(8,128)(2,1)S(1)}, bf16[96,1536]{1,0:T(8,128)(2,1)S(1)}, u32[]{:S(2)}, u32[]{:S(2)}) collective-permute-start(bf16[96,1536]{1,0:T(8,128)(2,1)S(1)} %get-tuple-element.162.refs_6_), channel_id=1, source_target_pairs={{0,2},{2,0},{4,6},{6,4},{8,10},{10,8},{12,14},{14,12},{16,18},{18,... | collective-permute-start | bytes 884744 | tf_op jit(solution)/shard_map/up_corner_across_1/ppermute | solution.py:140
  72.4 15.5 %collective-permute-start.24 = (bf16[384,512]{1,0:T(8,128)(2,1)S(1)}, bf16[384,512]{1,0:T(8,128)(2,1)S(1)}, u32[]{:S(2)}, u32[]{:S(2)}) collective-permute-start(bf16[384,512]{1,0:T(8,128)(2,1)S(1)} %join.15.refs_7_.refs_6_), channel_id=1, source_target_pairs={{0,8},{2,10},{4,12},{6,14},{8,0},{10,2},{12,4},{14,6},{16,24},{18,... | collective-permute-start | bytes 1179656 | tf_op jit(solution)/shard_map/down_plane_across_4/ppermute | solution.py:140
  74.0 13.9 %collective-permute-start.22 = (bf16[96,1024]{1,0:T(8,128)(2,1)S(1)}, bf16[96,1024]{1,0:T(8,128)(2,1)S(1)}, u32[]{:S(2)}, u32[]{:S(2)}) collective-permute-start(bf16[96,1024]{1,0:T(8,128)(2,1)S(1)} %get-tuple-element.167), channel_id=1, source_target_pairs={{0,2},{2,0},{4,6},{6,4},{8,10},{10,8},{12,14},{14,12},{16,18},{18,... | collective-permute-start | bytes 589832 | tf_op jit(solution)/shard_map/down_corner_across_1/ppermute | solution.py:140
  79.8 8.1 %collective-permute-start.23 = (bf16[96,1024]{1,0:T(8,128)(2,1)S(1)}, bf16[96,1024]{1,0:T(8,128)(2,1)S(1)}, u32[]{:S(2)}, u32[]{:S(2)}) collective-permute-start(bf16[96,1024]{1,0:T(8,128)(2,1)S(1)} %get-tuple-element.168), channel_id=1, source_target_pairs={{0,4},{2,6},{4,0},{6,2},{8,12},{10,14},{12,8},{14,10},{16,20},{18,... | collective-permute-start | bytes 589832 | tf_op jit(solution)/shard_map/down_corner_across_2/ppermute | solution.py:140
  88.6 1.2 collective-permute-start.25
  90.6 6.0 %collective-permute-start.28 = (f32[1,8,768]{2,1,0:T(8,128)S(1)}, f32[1,8,768]{2,1,0:T(8,128)S(1)}, u32[]{:S(2)}, u32[]{:S(2)}) collective-permute-start(f32[1,8,768]{2,1,0:T(8,128)S(1)} %bitcast.39), channel_id=1, source_target_pairs={{0,24},{2,26},{4,28},{6,30},{8,16},{10,18},{12,20},{14,22},{16,8},... | collective-permute-start | bytes 73736 | tf_op jit(solution)/shard_map/small_sums_across_12/ppermute | solution.py:140
  92.5 4.3 %collective-permute-start.27 = (f32[1,8,768]{2,1,0:T(8,128)S(1)}, f32[1,8,768]{2,1,0:T(8,128)S(1)}, u32[]{:S(2)}, u32[]{:S(2)}) collective-permute-start(f32[1,8,768]{2,1,0:T(8,128)S(1)} %bitcast.40), channel_id=1, source_target_pairs={{0,8},{2,10},{4,12},{6,14},{8,0},{10,2},{12,4},{14,6},{16,24},{18,... | collective-permute-start | bytes 73736 | tf_op jit(solution)/shard_map/small_sums_across_4/ppermute | solution.py:140
  93.1 4.7 %collective-permute-start.26 = (f32[1,8,768]{2,1,0:T(8,128)S(1)}, f32[1,8,768]{2,1,0:T(8,128)S(1)}, u32[]{:S(2)}, u32[]{:S(2)}) collective-permute-start(f32[1,8,768]{2,1,0:T(8,128)S(1)} %bitcast.41), channel_id=1, source_target_pairs={{0,16},{2,18},{4,20},{6,22},{8,24},{10,26},{12,28},{14,30},{16,0},... | collective-permute-start | bytes 73736 | tf_op jit(solution)/shard_map/small_sums_across_8/ppermute | solution.py:140
  97.8 5.6 %collective-permute-start.31 = (f32[4,8,768]{2,1,0:T(8,128)S(1)}, f32[4,8,768]{2,1,0:T(8,128)S(1)}, u32[]{:S(2)}, u32[]{:S(2)}) collective-permute-start(f32[4,8,768]{2,1,0:T(8,128)S(1)} %join.16.refs_7_.refs_0_), channel_id=1, source_target_pairs={{0,6},{2,4},{4,2},{6,0},{8,14},{10,12},{12,10},{14,8},{16,22},{18,... | collective-permute-start | bytes 294920 | tf_op jit(solution)/shard_map/small_sums_across_3/ppermute | solution.py:140
  99.8 4.6 %collective-permute-start.30 = (f32[4,8,768]{2,1,0:T(8,128)S(1)}, f32[4,8,768]{2,1,0:T(8,128)S(1)}, u32[]{:S(2)}, u32[]{:S(2)}) collective-permute-start(f32[4,8,768]{2,1,0:T(8,128)S(1)} %join.16.refs_7_.refs_0_), channel_id=1, source_target_pairs={{0,2},{2,0},{4,6},{6,4},{8,10},{10,8},{12,14},{14,12},{16,18},{18,... | collective-permute-start | bytes 294920 | tf_op jit(solution)/shard_map/small_sums_across_1/ppermute | solution.py:140
  100.3 4.6 %collective-permute-start.29 = (f32[4,8,768]{2,1,0:T(8,128)S(1)}, f32[4,8,768]{2,1,0:T(8,128)S(1)}, u32[]{:S(2)}, u32[]{:S(2)}) collective-permute-start(f32[4,8,768]{2,1,0:T(8,128)S(1)} %join.16.refs_7_.refs_0_), channel_id=1, source_target_pairs={{0,4},{2,6},{4,0},{6,2},{8,12},{10,14},{12,8},{14,10},{16,20},{18,... | collective-permute-start | bytes 294920 | tf_op jit(solution)/shard_map/small_sums_across_2/ppermute | solution.py:140
  109.1 4.8 %collective-permute-start.32 = (bf16[1024,768]{1,0:T(8,128)(2,1)S(1)}, bf16[1024,768]{1,0:T(8,128)(2,1)S(1)}, u32[]{:S(2)}, u32[]{:S(2)}) collective-permute-start(bf16[1024,768]{1,0:T(8,128)(2,1)S(1)} %get-tuple-element.177.refs_4_), channel_id=1, source_target_pairs={{0,1},{1,0},{2,3},{3,2},{4,5},{5,4},{6,7},{7,6},{8,9},{9,8},{10,11... | collective-permute-start | bytes 4718600 | tf_op jit(solution)/shard_map/second_gradient_other_core/ppermute | solution.py:149
  111.8 9.5 %collective-permute-start.37 = (bf16[96,1536]{1,0:T(8,128)(2,1)S(1)}, bf16[96,1536]{1,0:T(8,128)(2,1)S(1)}, u32[]{:S(2)}, u32[]{:S(2)}) collective-permute-start(bf16[96,1536]{1,0:T(8,128)(2,1)S(1)} %get-tuple-element.199), channel_id=1, source_target_pairs={{0,2},{2,0},{4,6},{6,4},{8,10},{10,8},{12,14},{14,12},{16,18},{18,... | collective-permute-start | bytes 884744 | tf_op jit(solution)/shard_map/up_gradient_across_1/ppermute | solution.py:140
  113.4 9.1 %collective-permute-start.38 = (bf16[96,1536]{1,0:T(8,128)(2,1)S(1)}, bf16[96,1536]{1,0:T(8,128)(2,1)S(1)}, u32[]{:S(2)}, u32[]{:S(2)}) collective-permute-start(bf16[96,1536]{1,0:T(8,128)(2,1)S(1)} %get-tuple-element.200), channel_id=1, source_target_pairs={{0,4},{2,6},{4,0},{6,2},{8,12},{10,14},{12,8},{14,10},{16,20},{18,... | collective-permute-start | bytes 884744 | tf_op jit(solution)/shard_map/up_gradient_across_2/ppermute | solution.py:140
  122.7 17.8 %collective-permute-start.39 = (bf16[192,1536]{1,0:T(8,128)(2,1)S(1)}, bf16[192,1536]{1,0:T(8,128)(2,1)S(1)}, u32[]{:S(2)}, u32[]{:S(2)}) collective-permute-start(bf16[192,1536]{1,0:T(8,128)(2,1)S(1)} %get-tuple-element.201), channel_id=1, source_target_pairs={{0,4},{2,6},{4,0},{6,2},{8,12},{10,14},{12,8},{14,10},{16,20},{18,... | collective-permute-start | bytes 1769480 | tf_op jit(solution)/shard_map/up_gradient_across_2/ppermute | solution.py:140
  123.3 18.3 %collective-permute-start.40 = (bf16[192,1536]{1,0:T(8,128)(2,1)S(1)}, bf16[192,1536]{1,0:T(8,128)(2,1)S(1)}, u32[]{:S(2)}, u32[]{:S(2)}) collective-permute-start(bf16[192,1536]{1,0:T(8,128)(2,1)S(1)} %get-tuple-element.202), channel_id=1, source_target_pairs={{0,2},{2,0},{4,6},{6,4},{8,10},{10,8},{12,14},{14,12},{16,18},{18,... | collective-permute-start | bytes 1769480 | tf_op jit(solution)/shard_map/up_gradient_across_1/ppermute | solution.py:140
  133.1 12.0 %collective-permute-start.33 = (bf16[96,1152]{1,0:T(8,128)(2,1)S(1)}, bf16[96,1152]{1,0:T(8,128)(2,1)S(1)}, u32[]{:S(2)}, u32[]{:S(2)}) collective-permute-start(bf16[96,1152]{1,0:T(8,128)(2,1)S(1)} %get-tuple-element.186), channel_id=1, source_target_pairs={{0,2},{2,0},{4,6},{6,4},{8,10},{10,8},{12,14},{14,12},{16,18},{18,... | collective-permute-start | bytes 663560 | tf_op jit(solution)/shard_map/early_gradient_across_1/ppermute | solution.py:140
  134.1 11.0 %collective-permute-start.34 = (bf16[96,1152]{1,0:T(8,128)(2,1)S(1)}, bf16[96,1152]{1,0:T(8,128)(2,1)S(1)}, u32[]{:S(2)}, u32[]{:S(2)}) collective-permute-start(bf16[96,1152]{1,0:T(8,128)(2,1)S(1)} %get-tuple-element.187), channel_id=1, source_target_pairs={{0,4},{2,6},{4,0},{6,2},{8,12},{10,14},{12,8},{14,10},{16,20},{18,... | collective-permute-start | bytes 663560 | tf_op jit(solution)/shard_map/early_gradient_across_2/ppermute | solution.py:140
  139.9 4.7 %collective-permute-start.35 = (bf16[96,512]{1,0:T(8,128)(2,1)S(1)}, bf16[96,512]{1,0:T(8,128)(2,1)S(1)}, u32[]{:S(2)}, u32[]{:S(2)}) collective-permute-start(bf16[96,512]{1,0:T(8,128)(2,1)S(1)} %get-tuple-element.192), channel_id=1, source_target_pairs={{0,2},{2,0},{4,6},{6,4},{8,10},{10,8},{12,14},{14,12},{16,18},{18,... | collective-permute-start | bytes 294920 | tf_op jit(solution)/shard_map/late_gradient_across_1/ppermute | solution.py:140
  140.5 4.6 %collective-permute-start.36 = (bf16[96,512]{1,0:T(8,128)(2,1)S(1)}, bf16[96,512]{1,0:T(8,128)(2,1)S(1)}, u32[]{:S(2)}, u32[]{:S(2)}) collective-permute-start(bf16[96,512]{1,0:T(8,128)(2,1)S(1)} %get-tuple-element.193), channel_id=1, source_target_pairs={{0,4},{2,6},{4,0},{6,2},{8,12},{10,14},{12,8},{14,10},{16,20},{18,... | collective-permute-start | bytes 294920 | tf_op jit(solution)/shard_map/late_gradient_across_2/ppermute | solution.py:140
  141.8 6.8 %collective-permute-start.43 = (bf16[96,1536]{1,0:T(8,128)(2,1)S(1)}, bf16[96,1536]{1,0:T(8,128)(2,1)S(1)}, u32[]{:S(2)}, u32[]{:S(2)}) collective-permute-start(bf16[96,1536]{1,0:T(8,128)(2,1)S(1)} %get-tuple-element.204.refs_8_), channel_id=1, source_target_pairs={{0,8},{2,10},{4,12},{6,14},{8,0},{10,2},{12,4},{14,6},{16,24},{18,... | collective-permute-start | bytes 884744 | tf_op jit(solution)/shard_map/up_gradient_across_4/ppermute | solution.py:140
  145.3 11.0 %collective-permute-start.41 = (bf16[192,1152]{1,0:T(8,128)(2,1)S(1)}, bf16[192,1152]{1,0:T(8,128)(2,1)S(1)}, u32[]{:S(2)}, u32[]{:S(2)}) collective-permute-start(bf16[192,1152]{1,0:T(8,128)(2,1)S(1)} %get-tuple-element.205.refs_2_.refs_6_), channel_id=1, source_target_pairs={{0,4},{2,6},{4,0},{6,2},{8,12},{10,14},{12,8},{14,10},{16,20},{18,... | collective-permute-start | bytes 1327112 | tf_op jit(solution)/shard_map/early_gradient_across_2/ppermute | solution.py:140
  146.5 9.9 %collective-permute-start.42 = (bf16[192,1152]{1,0:T(8,128)(2,1)S(1)}, bf16[192,1152]{1,0:T(8,128)(2,1)S(1)}, u32[]{:S(2)}, u32[]{:S(2)}) collective-permute-start(bf16[192,1152]{1,0:T(8,128)(2,1)S(1)} %get-tuple-element.206.refs_3_.refs_7_), channel_id=1, source_target_pairs={{0,2},{2,0},{4,6},{6,4},{8,10},{10,8},{12,14},{14,12},{16,18},{18,... | collective-permute-start | bytes 1327112 | tf_op jit(solution)/shard_map/early_gradient_across_1/ppermute | solution.py:140
  148.6 7.7 %collective-permute-start.44 = (bf16[48,1536]{1,0:T(8,128)(2,1)S(1)}, bf16[48,1536]{1,0:T(8,128)(2,1)S(1)}, u32[]{:S(2)}, u32[]{:S(2)}) collective-permute-start(bf16[48,1536]{1,0:T(8,128)(2,1)S(1)} %get-tuple-element.211), channel_id=1, source_target_pairs={{0,16},{2,18},{4,20},{6,22},{8,24},{10,26},{12,28},{14,30},{16,0},... | collective-permute-start | bytes 442376 | tf_op jit(solution)/shard_map/up_gradient_across_8/ppermute | solution.py:140
  156.5 14.1 %collective-permute-start.52 = (bf16[1024,768]{1,0:T(8,128)(2,1)S(1)}, bf16[1024,768]{1,0:T(8,128)(2,1)S(1)}, u32[]{:S(2)}, u32[]{:S(2)}) collective-permute-start(bf16[1024,768]{1,0:T(8,128)(2,1)S(1)} %get-tuple-element.224.refs_1_), channel_id=1, source_target_pairs={{0,1},{1,0},{2,3},{3,2},{4,5},{5,4},{6,7},{7,6},{8,9},{9,8},{10,11... | collective-permute-start | bytes 4718600 | tf_op jit(solution)/shard_map/first_gradient_other_core/ppermute | solution.py:149
  156.6 7.8 %collective-permute-start.45 = (bf16[96,1152]{1,0:T(8,128)(2,1)S(1)}, bf16[96,1152]{1,0:T(8,128)(2,1)S(1)}, u32[]{:S(2)}, u32[]{:S(2)}) collective-permute-start(bf16[96,1152]{1,0:T(8,128)(2,1)S(1)} %get-tuple-element.214), channel_id=1, source_target_pairs={{0,8},{2,10},{4,12},{6,14},{8,0},{10,2},{12,4},{14,6},{16,24},{18,... | collective-permute-start | bytes 663560 | tf_op jit(solution)/shard_map/early_gradient_across_4/ppermute | solution.py:140
  158.3 7.0 %collective-permute-start.47 = (bf16[192,512]{1,0:T(8,128)(2,1)S(1)}, bf16[192,512]{1,0:T(8,128)(2,1)S(1)}, u32[]{:S(2)}, u32[]{:S(2)}) collective-permute-start(bf16[192,512]{1,0:T(8,128)(2,1)S(1)} %get-tuple-element.208.refs_4_.refs_8_), channel_id=1, source_target_pairs={{0,4},{2,6},{4,0},{6,2},{8,12},{10,14},{12,8},{14,10},{16,20},{18,... | collective-permute-start | bytes 589832 | tf_op jit(solution)/shard_map/late_gradient_across_2/ppermute | solution.py:140
  159.4 6.7 %collective-permute-start.48 = (bf16[192,512]{1,0:T(8,128)(2,1)S(1)}, bf16[192,512]{1,0:T(8,128)(2,1)S(1)}, u32[]{:S(2)}, u32[]{:S(2)}) collective-permute-start(bf16[192,512]{1,0:T(8,128)(2,1)S(1)} %get-tuple-element.209.refs_5_.refs_9_), channel_id=1, source_target_pairs={{0,2},{2,0},{4,6},{6,4},{8,10},{10,8},{12,14},{14,12},{16,18},{18,... | collective-permute-start | bytes 589832 | tf_op jit(solution)/shard_map/late_gradient_across_1/ppermute | solution.py:140
  166.2 9.8 %collective-permute-start.49 = (bf16[48,512]{1,0:T(8,128)(2,1)S(1)}, bf16[48,512]{1,0:T(8,128)(2,1)S(1)}, u32[]{:S(2)}, u32[]{:S(2)}) collective-permute-start(bf16[48,512]{1,0:T(8,128)(2,1)S(1)} %get-tuple-element.219), channel_id=1, source_target_pairs={{0,16},{2,18},{4,20},{6,22},{8,24},{10,26},{12,28},{14,30},{16,0},... | collective-permute-start | bytes 147464 | tf_op jit(solution)/shard_map/late_gradient_across_8/ppermute | solution.py:140
  166.8 9.1 %collective-permute-start.50 = (bf16[48,512]{1,0:T(8,128)(2,1)S(1)}, bf16[48,512]{1,0:T(8,128)(2,1)S(1)}, u32[]{:S(2)}, u32[]{:S(2)}) collective-permute-start(bf16[48,512]{1,0:T(8,128)(2,1)S(1)} %get-tuple-element.220), channel_id=1, source_target_pairs={{0,8},{2,10},{4,12},{6,14},{8,0},{10,2},{12,4},{14,6},{16,24},{18,... | collective-permute-start | bytes 147464 | tf_op jit(solution)/shard_map/late_gradient_across_4/ppermute | solution.py:140
  168.5 7.5 %collective-permute-start.51 = (bf16[48,512]{1,0:T(8,128)(2,1)S(1)}, bf16[48,512]{1,0:T(8,128)(2,1)S(1)}, u32[]{:S(2)}, u32[]{:S(2)}) collective-permute-start(bf16[48,512]{1,0:T(8,128)(2,1)S(1)} %get-tuple-element.221), channel_id=1, source_target_pairs={{0,24},{2,26},{4,28},{6,30},{8,16},{10,18},{12,20},{14,22},{16,8},... | collective-permute-start | bytes 147464 | tf_op jit(solution)/shard_map/late_gradient_across_12/ppermute | solution.py:140
  170.6 7.2 %collective-permute-start.46 = (bf16[48,1152]{1,0:T(8,128)(2,1)S(1)}, bf16[48,1152]{1,0:T(8,128)(2,1)S(1)}, u32[]{:S(2)}, u32[]{:S(2)}) collective-permute-start(bf16[48,1152]{1,0:T(8,128)(2,1)S(1)} %get-tuple-element.216), channel_id=1, source_target_pairs={{0,16},{2,18},{4,20},{6,22},{8,24},{10,26},{12,28},{14,30},{16,0},... | collective-permute-start | bytes 331784 | tf_op jit(solution)/shard_map/early_gradient_across_8/ppermute | solution.py:140
  170.7 23.0 %copy-start.13 = (f32[3,48,384]{2,1,0:T(8,128)S(1)}, f32[3,48,384]{2,1,0:T(8,128)}, u32[]{:S(2)}) copy-start(f32[3,48,384]{2,1,0:T(8,128)} %get-tuple-element.236.refs_18_) | copy-start | bytes 663556
  170.7 23.0 %copy-start.14 = (f32[3,48,384]{2,1,0:T(8,128)S(1)}, f32[3,48,384]{2,1,0:T(8,128)}, u32[]{:S(2)}) copy-start(f32[3,48,384]{2,1,0:T(8,128)} %get-tuple-element.240.refs_25_) | copy-start | bytes 663556
  170.7 23.0 %copy-start.17 = (f32[48,384]{1,0:T(8,128)S(1)}, f32[48,384]{1,0:T(8,128)}, u32[]{:S(2)}) copy-start(f32[48,384]{1,0:T(8,128)} %get-tuple-element.241.refs_26_) | copy-start | bytes 221188
  170.7 23.0 %copy-start.26 = (f32[48,3]{0,1:T(4,128)S(1)}, f32[48,3]{0,1:T(4,128)}, u32[]{:S(2)}) copy-start(f32[48,3]{0,1:T(4,128)} %param.49) | copy-start | bytes 1732
  179.2 1.2 collective-permute-start.53
  180.5 5.6 %collective-permute-start.56 = (f32[1,24,128]{2,1,0:T(8,128)S(1)}, f32[1,24,128]{2,1,0:T(8,128)S(1)}, u32[]{:S(2)}, u32[]{:S(2)}) collective-permute-start(f32[1,24,128]{2,1,0:T(8,128)S(1)} %bitcast.55), channel_id=1, source_target_pairs={{0,24},{2,26},{4,28},{6,30},{8,16},{10,18},{12,20},{14,22},{16,8},... | collective-permute-start | bytes 36872 | tf_op jit(solution)/shard_map/squares_across_12/ppermute | solution.py:140
  182.5 3.8 %collective-permute-start.55 = (f32[1,24,128]{2,1,0:T(8,128)S(1)}, f32[1,24,128]{2,1,0:T(8,128)S(1)}, u32[]{:S(2)}, u32[]{:S(2)}) collective-permute-start(f32[1,24,128]{2,1,0:T(8,128)S(1)} %bitcast.56), channel_id=1, source_target_pairs={{0,8},{2,10},{4,12},{6,14},{8,0},{10,2},{12,4},{14,6},{16,24},{18,... | collective-permute-start | bytes 36872 | tf_op jit(solution)/shard_map/squares_across_4/ppermute | solution.py:140
  182.5 4.6 %collective-permute-start.54 = (f32[1,24,128]{2,1,0:T(8,128)S(1)}, f32[1,24,128]{2,1,0:T(8,128)S(1)}, u32[]{:S(2)}, u32[]{:S(2)}) collective-permute-start(f32[1,24,128]{2,1,0:T(8,128)S(1)} %bitcast.57), channel_id=1, source_target_pairs={{0,16},{2,18},{4,20},{6,22},{8,24},{10,26},{12,28},{14,30},{16,0},... | collective-permute-start | bytes 36872 | tf_op jit(solution)/shard_map/squares_across_8/ppermute | solution.py:140
  187.1 5.0 %collective-permute-start.59 = (f32[4,24,128]{2,1,0:T(8,128)S(1)}, f32[4,24,128]{2,1,0:T(8,128)S(1)}, u32[]{:S(2)}, u32[]{:S(2)}) collective-permute-start(f32[4,24,128]{2,1,0:T(8,128)S(1)} %join.17.refs_3_), channel_id=1, source_target_pairs={{0,6},{2,4},{4,2},{6,0},{8,14},{10,12},{12,10},{14,8},{16,22},{18,... | collective-permute-start | bytes 147464 | tf_op jit(solution)/shard_map/squares_across_3/ppermute | solution.py:140
  188.2 4.1 %collective-permute-start.58 = (f32[4,24,128]{2,1,0:T(8,128)S(1)}, f32[4,24,128]{2,1,0:T(8,128)S(1)}, u32[]{:S(2)}, u32[]{:S(2)}) collective-permute-start(f32[4,24,128]{2,1,0:T(8,128)S(1)} %join.17.refs_3_), channel_id=1, source_target_pairs={{0,2},{2,0},{4,6},{6,4},{8,10},{10,8},{12,14},{14,12},{16,18},{18,... | collective-permute-start | bytes 147464 | tf_op jit(solution)/shard_map/squares_across_1/ppermute | solution.py:140
  189.6 4.1 %collective-permute-start.57 = (f32[4,24,128]{2,1,0:T(8,128)S(1)}, f32[4,24,128]{2,1,0:T(8,128)S(1)}, u32[]{:S(2)}, u32[]{:S(2)}) collective-permute-start(f32[4,24,128]{2,1,0:T(8,128)S(1)} %join.17.refs_3_), channel_id=1, source_target_pairs={{0,4},{2,6},{4,0},{6,2},{8,12},{10,14},{12,8},{14,10},{16,20},{18,... | collective-permute-start | bytes 147464 | tf_op jit(solution)/shard_map/squares_across_2/ppermute | solution.py:140
  (27 other events, 337.0 us)

commit v3 on v2

--- a/solution.py
+++ b/solution.py
@@ -787,18 +787,24 @@
     )(lengths, same, positive, vectors, slope, down, up, *small_all)
 
 
-def up_grad_kernel(normed_ref, d_ref, *out_refs):
-    for n in range(normed_ref.shape[1] // ROWS):
-        columns = slice(n * ROWS, (n + 1) * ROWS)
-        spill_rows(dot_tn(normed_ref[:, columns], d_ref[...]), out_refs, n * ROWS)
-
-
-def up_grad(normed, d_hidden, rows):
+def up_grad_kernel(first, skip, normed_ref, d_ref, *out_refs):
+    end = first + skip + sum(ref.shape[0] for ref in out_refs)
+    for start in range(first, end, ROWS):
+        stop = min(start + ROWS, -(-end // LANES) * LANES)
+        grad = dot_tn(normed_ref[:, start:stop], d_ref[...])
+        if start == first:
+            spill_rows(grad[skip:], out_refs)
+        else:
+            spill_rows(grad, out_refs, start - first - skip)
+
+
+def up_grad(normed, d_hidden, rows, first=0, skip=0, deps=()):
     return call(
-        up_grad_kernel,
+        functools.partial(up_grad_kernel, first, skip),
         "hidden_in_gradient",
         [shape_of((r, d_hidden.shape[1]), low_type) for r in rows],
         cost=(1200, 15000),
+        deps=deps,
     )(normed, d_hidden)
 
 
@@ -1492,9 +1498,15 @@
         (turned_first,),
     )
     d_normed_second_came = other_core(d_normed_second, "second_gradient_other_core")
-    up_sum = Scatter(
-        up_grad(normed_second, d_hidden, piece_rows(size, width)), size, "up_gradient"
-    )
+    rows = piece_rows(size, width)
+    if size == 16:
+        start = sum(rows[:3])
+        aligned = start // ROWS * ROWS
+        corner = up_grad(normed_second, d_hidden, rows[3:], aligned, start - aligned)
+        up_rows = [*up_grad(normed_second, d_hidden, rows[:3], deps=(corner[0],)), *corner]
+    else:
+        up_rows = up_grad(normed_second, d_hidden, rows)
+    up_sum = Scatter(up_rows, size, "up_gradient")
     d_middle, d_attended, g_out = middle_back(
         lengths, rows_low, branch, branch_came, d_normed_second, d_normed_second_came, vectors,
         d_line, attended, inverse, weight_heads, slot,

time: 197 us -> 196 us (level)
  waiting for transfers between devices: 55.5 us -> 50 us
  starting transfers between devices: 63.9 us -> 66.2 us
    ppermute x55, waiting for transfers between devices: 53.1 us -> 47.6 us  [swap(): return lax.ppermute(array, 'dp', [(i, i ^ mask) for i in range(size)])]
    ppermute x55, starting transfers between devices: 63.6 us -> 66 us  [swap(): return lax.ppermute(array, 'dp', [(i, i ^ mask) for i in range(size)])]
    pallas_call x42 -> x43, Pallas kernels: 69.6 us -> 71.5 us  [apply(): pl.pallas_call(run, out_shape=[*out_shapes, *(shape_of(a.shape, a.dtype)...]
  transfers between devices with their start and end apart: 60 -> 60, of which waited for: 34 -> 35; matrix products, arithmetic and copies ran while one was open for 0% -> 0% of each run, Pallas kernels for 29% -> 30%
where the time goes in v3:
time: 196 us; the launch traced here: 195 us
  Pallas kernels  71.5 us (36%)
  starting transfers between devices  66.2 us (34%)
  waiting for transfers between devices  50 us (26%)
  local copies, waits for them, and re-layouts  5.06 us (3%)
  between operations  2.37 us (1%)
    pallas_call x43, Pallas kernels, apply(): pl.pallas_call(run, out_shape=[*out_shapes, *(shape_of(a.shape, a.dtype)...  71.5 us
    ppermute x55, starting transfers between devices, swap(): return lax.ppermute(array, 'dp', [(i, i ^ mask) for i in range(size)])  66 us
    ppermute x55, waiting for transfers between devices, swap(): return lax.ppermute(array, 'dp', [(i, i ^ mask) for i in range(size)])  47.6 us
    unnamed x62, local copies, waits for them, and re-layouts  4.37 us
  transfers between devices with their start and end apart: 60, of which 35 were waited for; matrix products, arithmetic and copies ran while one was open for 0% of the time, Pallas kernels for 30%

profile of v3, /device:TPU:0, one launch (start us, length us, event | category | flops | bytes accessed | tf_op | source)
XLA Modules:
  0.0 195.2 jit_solution(11161929646661354154)
XLA Ops:
  0.7 1.8 pack_heads.1.refs_0_
  2.5 5.0 %collective-permute-start.2 = (bf16[48,1664]{1,0:T(8,128)(2,1)}, bf16[48,1664]{1,0:T(8,128)(2,1)S(1)}, u32[]{:S(2)}, u32[]{:S(2)}) collective-permute-start(bf16[48,1664]{1,0:T(8,128)(2,1)} %pack_heads.1.refs_0_), channel_id=1, source_target_pairs={{0,24},{2,26},{4,28},{6,30},{8,16},{10,18},{12,20},{14,22},{16,8},... | collective-permute-start | bytes 479240 | tf_op jit(solution)/shard_map/heads_across_12/ppermute | solution.py:140
  10.1 1.8 collective-permute-start.4
  11.8 1.5 collective-permute-start.3
  16.3 1.4 prepare.1
  17.7 3.3 %stage.1 = (f32[3,48,384]{2,1,0:T(8,128)}, f32[48,384]{1,0:T(8,128)}, f32[48,1536]{1,0:T(8,128)}, f32[48,1536]{1,0:T(8,128)}, f32[3,48,384]{2,1,0:T(8,128)}, /*i...) custom-call(f32[3,48,384]{2,1,0:T(8,128)} %bitcast.37, ...), custom_call_target="tpu_custom_call" | custom-call | tf_op jit(solution)/shard_map/stage/pallas_call | solution.py:78
  22.3 1.6 collective-permute-start.6
  23.8 1.5 collective-permute-start.5
  25.6 1.9 order_tokens.1.refs_2_.refs_0_.refs_1_.refs_3_
  27.5 5.9 %collective-permute-done.7.refs_1_ = bf16[48,1536]{1,0:T(8,128)(2,1)S(1)} collective-permute-done((bf16[48,1536]{1,0:T(8,128)(2,1)S(1)}, bf16[48,1536]{1,0:T(8,128)(2,1)S(1)}, u32[]{:S(2)}, u32[]{:S(2)}) %collective-permute-start.7) | collective-permute-done | bytes 147488 | tf_op jit(solution)/shard_map/up_across_8/ppermute | solution.py:140
  34.1 4.7 %collective-permute-done.8.refs_3_ = bf16[48,512]{1,0:T(8,128)(2,1)S(1)} collective-permute-done((bf16[48,512]{1,0:T(8,128)(2,1)S(1)}, bf16[48,512]{1,0:T(8,128)(2,1)S(1)}, u32[]{:S(2)}, u32[]{:S(2)}) %collective-permute-start.8) | collective-permute-done | bytes 49184 | tf_op jit(solution)/shard_map/down_plane_corner_across_1/ppermute | solution.py:140
  39.0 1.6 collective-permute-start.10
  40.6 1.3 collective-permute-start.9
  43.1 4.8 %collective-permute-done.11.refs_1_ = bf16[48,1024]{1,0:T(8,128)(2,1)S(1)} collective-permute-done((bf16[48,1024]{1,0:T(8,128)(2,1)S(1)}, bf16[48,1024]{1,0:T(8,128)(2,1)S(1)}, u32[]{:S(2)}, u32[]{:S(2)}) %collective-permute-start.11) | collective-permute-done | bytes 98336 | tf_op jit(solution)/shard_map/down_across_8/ppermute | solution.py:140
  48.6 2.5 %collective-permute-done.9.refs_4_.refs_13_ = bf16[96,1664]{1,0:T(8,128)(2,1)S(1)} collective-permute-done((bf16[96,1664]{1,0:T(8,128)(2,1)S(1)}, bf16[96,1664]{1,0:T(8,128)(2,1)S(1)}, u32[]{:S(2)}, u32[]{:S(2)}) %collective-permute-start.9) | collective-permute-done | bytes 319520 | tf_op jit(solution)/shard_map/heads_corner_across_1/ppermute | solution.py:140
  51.1 3.6 %projection.1 = (bf16[3,3,1024,128]{3,2,1,0:T(8,128)(2,1)S(1)}, bf16[1024,768]{1,0:T(8,128)(2,1)S(1)}, f32[8,768]{1,0:T(8,128)S(1)}) custom-call(bf16[1024,768]{1,0:T(8,128)(2,1)S(1)} %order_tokens.1.refs_2_.refs_0_.refs_1_.refs_3_, bf16[192,1664]{1,0:T(8,128)(2,1)S(1)} %get-tuple-element.151.refs_1_.refs_10_, ...), custom_call_target="tpu_custom_call" | custom-call | tf_op jit(solution)/shard_map/projection/pallas_call | solution.py:78
  54.7 3.5 %attention_forward.2 = (bf16[1024,384]{1,0:T(8,128)(2,1)S(1)}, bf16[3,2,2,512,512]{4,3,2,1,0:T(8,128)(2,1)S(1)}, f32[1024,384]{1,0:T(8,128)S(1)}) custom-call(s32[2]{0:T(128)S(1)} %bitcast.49, f32[3,2,1024]{2,1,0:T(2,128)S(1)} %get-tuple-element.146.refs_1_, bf16[3,3,1024,128]{3,2,1,0:T(8,128)(2,1)S(1)} %get-tuple-element.156.refs_2_.refs_1_, ...), custom_call_target="tpu_custom_call" | custom-call | tf_op jit(solution)/shard_map/attention_forward/pallas_call | solution.py:78
  58.3 1.4 collective-permute-start.18
  61.5 6.6 %attention_forward.3 = (bf16[1024,384]{1,0:T(8,128)(2,1)S(1)}, bf16[3,2,2,512,512]{4,3,2,1,0:T(8,128)(2,1)S(1)}, f32[1024,384]{1,0:T(8,128)S(1)}) custom-call(s32[2]{0:T(128)S(1)} %bitcast.50, f32[3,2,1024]{2,1,0:T(2,128)S(1)} %get-tuple-element.146.refs_1_, ...), custom_call_target="tpu_custom_call", output_to_operand_aliasing={{0}: (3, {}), {1}: (4, {}), {2}: (5, {})} | custom-call | tf_op jit(solution)/shard_map/attention_forward/pallas_call | solution.py:78
  68.9 1.4 branch.1.refs_2_
  70.4 1.1 collective-permute-start.21
  72.4 1.6 collective-permute-start.24
  74.1 1.4 collective-permute-start.22
  75.5 4.3 %collective-permute-done.21.refs_9_ = bf16[96,1536]{1,0:T(8,128)(2,1)S(1)} collective-permute-done((bf16[96,1536]{1,0:T(8,128)(2,1)S(1)}, bf16[96,1536]{1,0:T(8,128)(2,1)S(1)}, u32[]{:S(2)}, u32[]{:S(2)}) %collective-permute-start.21) | collective-permute-done | bytes 294944 | tf_op jit(solution)/shard_map/up_corner_across_2/ppermute | solution.py:140
  79.8 1.0 collective-permute-start.23
  81.3 6.7 %hidden_forward.1 = (bf16[1024,768]{1,0:T(8,128)(2,1)S(1)}, bf16[1024,1536]{1,0:T(8,128)(2,1)S(1)}, f32[2,1,1536]{2,1,0:T(1,128)S(1)}, f32[2,1,768]{2,1,0:T(1,128)S(1)}, bf16[768,1536]{1,0:T(8,128)(2,1)S(1)}) custom-call(s32[2]{0:T(128)S(1)} %bitcast.51, bf16[1024,768]{1,0:T(8,128)(2,1)S(1)} %order_tokens.1.refs_2_.refs_0_.refs_1_.refs_3_, ...), custom_call_target="tpu_custom_call" | custom-call | flops 2400000000 | bytes 20000000 | tf_op jit(solution)/shard_map/hidden_forward/pallas_call | solution.py:78
  88.8 1.2 collective-permute-done.25.refs_2_
  90.7 1.9 collective-permute-start.28
  93.3 1.8 collective-permute-start.26
  95.1 1.6 collective-permute-done.28.refs_3_
  96.9 1.1 collective-permute-done.26.refs_1_
  98.0 1.8 collective-permute-start.31
  100.4 1.2 collective-permute-start.29
  101.6 2.0 %collective-permute-done.31.refs_10_.refs_3_ = f32[4,8,768]{2,1,0:T(8,128)S(1)} collective-permute-done((f32[4,8,768]{2,1,0:T(8,128)S(1)}, f32[4,8,768]{2,1,0:T(8,128)S(1)}, u32[]{:S(2)}, u32[]{:S(2)}) %collective-permute-start.31) | collective-permute-done | bytes 98336 | tf_op jit(solution)/shard_map/small_sums_across_3/ppermute | solution.py:140
  105.0 4.2 %rank_backward.1 = (f32[8,768]{1,0:T(8,128)S(1)}, f32[8,1536]{1,0:T(8,128)}, f32[2,16,128]{2,1,0:T(8,128)S(1)}, bf16[1024,1536]{1,0:T(8,128)(2,1)S(1)}, bf16[1024,768]{1,0:T(8,128)(2,1)S(1)}) custom-call(s32[2]{0:T(128)S(1)} %bitcast.53, f32[2,16,128]{2,1,0:T(8,128)S(1)} %get-tuple-element.172.refs_1_, f32[2,16,128]{2,1,0:T(8,128)S(1)} %get-tuple-element.173.refs_2_, ...), custom_call_target="tpu_custom_call" | custom-call | flops 2400000000 | bytes 20000000 | tf_op jit(solution)/shard_map/rank_backward/pallas_call | solution.py:78
  110.3 1.3 collective-permute-start.38
  112.5 2.2 %hidden_in_gradient.3 = (bf16[192,1536]{1,0:T(8,128)(2,1)S(1)}, bf16[192,1536]{1,0:T(8,128)(2,1)S(1)}, bf16[192,1536]{1,0:T(8,128)(2,1)S(1)}) custom-call(bf16[1024,768]{1,0:T(8,128)(2,1)S(1)} %get-tuple-element.194.refs_0_, bf16[1024,1536]{1,0:T(8,128)(2,1)S(1)} %get-tuple-element.195.refs_1_, bf16[96,1536]{1,0:T(8,128)(2,1)S(1)} %get-tuple-element.196.refs_2_), custom_call_target="tpu_custom_call" | custom-call | flops 2400000000 | bytes 15000000 | tf_op jit(solution)/shard_map/hidden_in_gradient/pallas_call | solution.py:78
  114.7 4.5 %middle_backward.1 = (f32[1024,768]{1,0:T(8,128)S(1)}, bf16[1024,384]{1,0:T(8,128)(2,1)S(1)}, f32[768,384]{1,0:T(8,128)S(1)}) custom-call(s32[2]{0:T(128)S(1)} %bitcast.54, bf16[1024,768]{1,0:T(8,128)(2,1)S(1)} %order_tokens.1.refs_2_.refs_0_.refs_1_.refs_3_, bf16[1024,768]{1,0:T(8,128)(2,1)S(1)} %branch.1.refs_2_, ...), custom_call_target="tpu_custom_call" | custom-call | flops 1200000000 | bytes 15000000 | tf_op jit(solution)/shard_map/middle_backward/pallas_call | solution.py:78
  121.8 1.5 collective-permute-start.40
  123.3 9.1 %attention_backward.2 = (bf16[3,3,1024,128]{3,2,1,0:T(8,128)(2,1)S(1)}, f32[2,8,128]{2,1,0:T(8,128)S(1)}, bf16[192,1152]{1,0:T(8,128)(2,1)S(1)}, bf16[192,1152]{...) custom-call(bf16[3,2,2,512,512]{4,3,2,1,0:T(8,128)(2,1)S(1)} %get-tu, ...), custom_call_target="tpu_custom_call" | custom-call | tf_op jit(solution)/shard_map/attention_backward/pallas_call | solution.py:78
  133.0 1.2 collective-permute-start.34
  134.2 4.5 %attention_backward.3 = (bf16[3,3,1024,128]{3,2,1,0:T(8,128)(2,1)S(1)}, f32[1,8,128]{2,1,0:T(8,128)S(1)}, bf16[192,512]{1,0:T(8,128)(2,1)S(1)}, bf16[192,512]{1,...) custom-call(bf16[3,2,2,512,512]{4,3,2,1,0:T(8,128)(2,1)S(1)} %get-tu, ...), custom_call_target="tpu_custom_call", output_to_operand_aliasing={{0}: (7, {})} | custom-call | tf_op jit(solution)/shard_map/attention_backward/pallas_call | solution.py:78
  139.7 1.4 collective-permute-start.36
  141.3 1.8 collective-permute-start.43
  144.5 1.5 collective-permute-start.41
  146.5 1.6 collective-permute-done.43.refs_1_
  148.1 2.1 %collective-permute-start.44 = (bf16[48,1536]{1,0:T(8,128)(2,1)S(1)}, bf16[48,1536]{1,0:T(8,128)(2,1)S(1)}, u32[]{:S(2)}, u32[]{:S(2)}) collective-permute-start(bf16[48,1536]{1,0:T(8,128)(2,1)S(1)} %get-tuple-element.211), channel_id=1, source_target_pairs={{0,16},{2,18},{4,20},{6,22},{8,24},{10,26},{12,28},{14,30},{16,0},... | collective-permute-start | bytes 442376 | tf_op jit(solution)/shard_map/up_gradient_across_8/ppermute | solution.py:140
  150.3 3.2 %normed_backward.1.refs_5_ = bf16[1024,768]{1,0:T(8,128)(2,1)S(1)} custom-call(bf16[3,3,1024,128]{3,2,1,0:T(8,128)(2,1)S(1)} %get-tuple-element.212.refs_0_, bf16[192,1664]{1,0:T(8,128)(2,1)S(1)} %get-tuple-element.151.refs_1_.refs_10_, bf16[192,1664]{1,0:T(8,128)(2,1)S(1)} %collective-permute-done.5.refs_0_.refs_2_.refs_11_, ...), custom_call_target="tpu_custom_call" | custom-call | flops 1800000000 | bytes 15000000 | tf_op jit(solution)/shard_map/normed_backward/pallas_call | solution.py:78
  155.2 1.8 collective-permute-start.45
  157.7 1.3 collective-permute-start.48
  159.0 4.0 %collective-permute-done.45.refs_1_ = bf16[96,1152]{1,0:T(8,128)(2,1)S(1)} collective-permute-done((bf16[96,1152]{1,0:T(8,128)(2,1)S(1)}, bf16[96,1152]{1,0:T(8,128)(2,1)S(1)}, u32[]{:S(2)}, u32[]{:S(2)}) %collective-permute-start.45) | collective-permute-done | bytes 221216 | tf_op jit(solution)/shard_map/early_gradient_across_4/ppermute | solution.py:140
  164.5 1.8 collective-permute-start.49
  167.0 1.9 collective-permute-start.51
  169.8 5.3 %token_gradient.1 = (f32[1024,768]{1,0:T(8,128)}, f32[8,128]{1,0:T(8,128)S(1)}) custom-call(f32[1024,768]{1,0:T(8,128)S(1)} %get-tuple-element.223.refs_0_, bf16[1024,768]{1,0:T(8,128)(2,1)S(1)} %get-tuple-element.224.refs_1_, bf16[1024,768]{1,0:T(8,128)(2,1)S(1)} %collective-permute-done.52.refs_2_, ...), custom_call_target="tpu_custom_call" | custom-call | flops 2400000000 | bytes 15000000 | tf_op jit(solution)/shard_map/token_gradient/pallas_call | solution.py:78
  175.3 1.4 collective-permute-done.46.refs_5_
  176.7 1.4 gradient_totals.1
  178.1 1.2 collective-permute-done.53.refs_1_
  179.3 1.8 collective-permute-start.56
  181.2 2.5 %collective-permute-start.54 = (f32[1,24,128]{2,1,0:T(8,128)S(1)}, f32[1,24,128]{2,1,0:T(8,128)S(1)}, u32[]{:S(2)}, u32[]{:S(2)}) collective-permute-start(f32[1,24,128]{2,1,0:T(8,128)S(1)} %bitcast.57), channel_id=1, source_target_pairs={{0,16},{2,18},{4,20},{6,22},{8,24},{10,26},{12,28},{14,30},{16,0},... | collective-permute-start | bytes 36872 | tf_op jit(solution)/shard_map/squares_across_8/ppermute | solution.py:140
  183.7 1.1 collective-permute-done.56.refs_3_
  185.8 1.7 collective-permute-start.59
  188.2 1.0 collective-permute-start.57
  189.3 1.5 collective-permute-done.59.refs_6_
  192.5 2.5 %update.1 = (f32[1,1]{1,0:T(1,128)}, f32[3,48,384]{2,1,0:T(8,128)}, f32[48,384]{1,0:T(8,128)}, f32[48,1536]{1,0:T(8,128)}, f32[48,1536]{1,0:T(8,128)}, /*index=5...) custom-call(s32[1]{0:T(128)} %bitcast.refs_0_, ...), custom_call_target="tpu_custom_call" | custom-call | bytes 6000000 | tf_op jit(solution)/shard_map/update/pallas_call | solution.py:78
  (163 shorter events, 34.3 us)
Async XLA Ops:
  2.5 18.6 %collective-permute-start.2 = (bf16[48,1664]{1,0:T(8,128)(2,1)}, bf16[48,1664]{1,0:T(8,128)(2,1)S(1)}, u32[]{:S(2)}, u32[]{:S(2)}) collective-permute-start(bf16[48,1664]{1,0:T(8,128)(2,1)} %pack_heads.1.refs_0_), channel_id=1, source_target_pairs={{0,24},{2,26},{4,28},{6,30},{8,16},{10,18},{12,20},{14,22},{16,8},... | collective-permute-start | bytes 479240 | tf_op jit(solution)/shard_map/heads_across_12/ppermute | solution.py:140
  7.5 13.5 %collective-permute-start.1 = (bf16[48,1664]{1,0:T(8,128)(2,1)}, bf16[48,1664]{1,0:T(8,128)(2,1)S(1)}, u32[]{:S(2)}, u32[]{:S(2)}) collective-permute-start(bf16[48,1664]{1,0:T(8,128)(2,1)} %pack_heads.1.refs_0_), channel_id=1, source_target_pairs={{0,8},{2,10},{4,12},{6,14},{8,0},{10,2},{12,4},{14,6},{16,24},{18,... | collective-permute-start | bytes 479240 | tf_op jit(solution)/shard_map/heads_across_4/ppermute | solution.py:140
  7.5 13.7 %collective-permute-start = (bf16[48,1664]{1,0:T(8,128)(2,1)}, bf16[48,1664]{1,0:T(8,128)(2,1)S(1)}, u32[]{:S(2)}, u32[]{:S(2)}) collective-permute-start(bf16[48,1664]{1,0:T(8,128)(2,1)} %pack_heads.1.refs_0_), channel_id=1, source_target_pairs={{0,16},{2,18},{4,20},{6,22},{8,24},{10,26},{12,28},{14,30},{16,0},... | collective-permute-start | bytes 479240 | tf_op jit(solution)/shard_map/heads_across_8/ppermute | solution.py:140
  10.1 11.0 %collective-permute-start.4 = (bf16[48,512]{1,0:T(8,128)(2,1)S(1)}, bf16[48,512]{1,0:T(8,128)(2,1)S(1)}, u32[]{:S(2)}, u32[]{:S(2)}) collective-permute-start(bf16[48,512]{1,0:T(8,128)(2,1)S(1)} %get-tuple-element.148.refs_0_), channel_id=1, source_target_pairs={{0,2},{2,0},{4,6},{6,4},{8,10},{10,8},{12,14},{14,12},{16,18},{18,... | collective-permute-start | bytes 147464 | tf_op jit(solution)/shard_map/down_plane_across_1/ppermute | solution.py:140
  11.8 9.2 %collective-permute-start.3 = (bf16[48,512]{1,0:T(8,128)(2,1)S(1)}, bf16[48,512]{1,0:T(8,128)(2,1)S(1)}, u32[]{:S(2)}, u32[]{:S(2)}) collective-permute-start(bf16[48,512]{1,0:T(8,128)(2,1)S(1)} %get-tuple-element.148.refs_0_), channel_id=1, source_target_pairs={{0,4},{2,6},{4,0},{6,2},{8,12},{10,14},{12,8},{14,10},{16,20},{18,... | collective-permute-start | bytes 147464 | tf_op jit(solution)/shard_map/down_plane_across_2/ppermute | solution.py:140
  22.3 16.6 %collective-permute-start.6 = (bf16[192,1664]{1,0:T(8,128)(2,1)S(1)}, bf16[192,1664]{1,0:T(8,128)(2,1)S(1)}, u32[]{:S(2)}, u32[]{:S(2)}) collective-permute-start(bf16[192,1664]{1,0:T(8,128)(2,1)S(1)} %get-tuple-element.151.refs_1_.refs_10_), channel_id=1, source_target_pairs={{0,2},{2,0},{4,6},{6,4},{8,10},{10,8},{12,14},{14,12},{16,18},{18,... | collective-permute-start | bytes 1916936 | tf_op jit(solution)/shard_map/heads_across_1/ppermute | solution.py:140
  23.8 15.2 %collective-permute-start.5 = (bf16[192,1664]{1,0:T(8,128)(2,1)S(1)}, bf16[192,1664]{1,0:T(8,128)(2,1)S(1)}, u32[]{:S(2)}, u32[]{:S(2)}) collective-permute-start(bf16[192,1664]{1,0:T(8,128)(2,1)S(1)} %get-tuple-element.151.refs_1_.refs_10_), channel_id=1, source_target_pairs={{0,4},{2,6},{4,0},{6,2},{8,12},{10,14},{12,8},{14,10},{16,20},{18,... | collective-permute-start | bytes 1916936 | tf_op jit(solution)/shard_map/heads_across_2/ppermute | solution.py:140
  25.3 8.0 %collective-permute-start.7 = (bf16[48,1536]{1,0:T(8,128)(2,1)S(1)}, bf16[48,1536]{1,0:T(8,128)(2,1)S(1)}, u32[]{:S(2)}, u32[]{:S(2)}) collective-permute-start(bf16[48,1536]{1,0:T(8,128)(2,1)S(1)} %get-tuple-element.152.refs_0_), channel_id=1, source_target_pairs={{0,16},{2,18},{4,20},{6,22},{8,24},{10,26},{12,28},{14,30},{16,0},... | collective-permute-start | bytes 442376 | tf_op jit(solution)/shard_map/up_across_8/ppermute | solution.py:140
  33.4 8.7 %collective-permute-start.12 = (bf16[96,1536]{1,0:T(8,128)(2,1)S(1)}, bf16[96,1536]{1,0:T(8,128)(2,1)S(1)}, u32[]{:S(2)}, u32[]{:S(2)}) collective-permute-start(bf16[96,1536]{1,0:T(8,128)(2,1)S(1)} %join.10.refs_2_.refs_0_), channel_id=1, source_target_pairs={{0,8},{2,10},{4,12},{6,14},{8,0},{10,2},{12,4},{14,6},{16,24},{18,... | collective-permute-start | bytes 884744 | tf_op jit(solution)/shard_map/up_across_4/ppermute | solution.py:140
  33.5 5.3 %collective-permute-start.8 = (bf16[48,512]{1,0:T(8,128)(2,1)S(1)}, bf16[48,512]{1,0:T(8,128)(2,1)S(1)}, u32[]{:S(2)}, u32[]{:S(2)}) collective-permute-start(bf16[48,512]{1,0:T(8,128)(2,1)S(1)} %collective-permute-done.3.refs_7_.refs_1_), channel_id=1, source_target_pairs={{0,2},{2,0},{4,6},{6,4},{8,10},{10,8},{12,14},{14,12},{16,18},{18,... | collective-permute-start | bytes 147464 | tf_op jit(solution)/shard_map/down_plane_corner_across_1/ppermute | solution.py:140
  39.0 9.6 %collective-permute-start.10 = (bf16[96,1664]{1,0:T(8,128)(2,1)S(1)}, bf16[96,1664]{1,0:T(8,128)(2,1)S(1)}, u32[]{:S(2)}, u32[]{:S(2)}) collective-permute-start(bf16[96,1664]{1,0:T(8,128)(2,1)S(1)} %get-tuple-element.155), channel_id=1, source_target_pairs={{0,4},{2,6},{4,0},{6,2},{8,12},{10,14},{12,8},{14,10},{16,20},{18,... | collective-permute-start | bytes 958472 | tf_op jit(solution)/shard_map/heads_corner_across_2/ppermute | solution.py:140
  40.6 10.5 %collective-permute-start.9 = (bf16[96,1664]{1,0:T(8,128)(2,1)S(1)}, bf16[96,1664]{1,0:T(8,128)(2,1)S(1)}, u32[]{:S(2)}, u32[]{:S(2)}) collective-permute-start(bf16[96,1664]{1,0:T(8,128)(2,1)S(1)} %get-tuple-element.154.refs_2_), channel_id=1, source_target_pairs={{0,2},{2,0},{4,6},{6,4},{8,10},{10,8},{12,14},{14,12},{16,18},{18,... | collective-permute-start | bytes 958472 | tf_op jit(solution)/shard_map/heads_corner_across_1/ppermute | solution.py:140
  42.0 6.0 %collective-permute-start.11 = (bf16[48,1024]{1,0:T(8,128)(2,1)S(1)}, bf16[48,1024]{1,0:T(8,128)(2,1)S(1)}, u32[]{:S(2)}, u32[]{:S(2)}) collective-permute-start(bf16[48,1024]{1,0:T(8,128)(2,1)S(1)} %get-tuple-element.157.refs_0_), channel_id=1, source_target_pairs={{0,16},{2,18},{4,20},{6,22},{8,24},{10,26},{12,28},{14,30},{16,0},... | collective-permute-start | bytes 294920 | tf_op jit(solution)/shard_map/down_across_8/ppermute | solution.py:140
  42.1 26.2 %collective-permute-start.14 = (bf16[192,1536]{1,0:T(8,128)(2,1)S(1)}, bf16[192,1536]{1,0:T(8,128)(2,1)S(1)}, u32[]{:S(2)}, u32[]{:S(2)}) collective-permute-start(bf16[192,1536]{1,0:T(8,128)(2,1)S(1)} %join.11.refs_2_.refs_5_), channel_id=1, source_target_pairs={{0,2},{2,0},{4,6},{6,4},{8,10},{10,8},{12,14},{14,12},{16,18},{18,... | collective-permute-start | bytes 1769480 | tf_op jit(solution)/shard_map/up_across_1/ppermute | solution.py:140
  48.0 10.2 %collective-permute-start.15 = (bf16[96,1024]{1,0:T(8,128)(2,1)S(1)}, bf16[96,1024]{1,0:T(8,128)(2,1)S(1)}, u32[]{:S(2)}, u32[]{:S(2)}) collective-permute-start(bf16[96,1024]{1,0:T(8,128)(2,1)S(1)} %join.12.refs_3_.refs_0_), channel_id=1, source_target_pairs={{0,8},{2,10},{4,12},{6,14},{8,0},{10,2},{12,4},{14,6},{16,24},{18,... | collective-permute-start | bytes 589832 | tf_op jit(solution)/shard_map/down_across_4/ppermute | solution.py:140
  48.1 20.3 %collective-permute-start.13 = (bf16[192,1536]{1,0:T(8,128)(2,1)S(1)}, bf16[192,1536]{1,0:T(8,128)(2,1)S(1)}, u32[]{:S(2)}, u32[]{:S(2)}) collective-permute-start(bf16[192,1536]{1,0:T(8,128)(2,1)S(1)} %join.11.refs_2_.refs_5_), channel_id=1, source_target_pairs={{0,4},{2,6},{4,0},{6,2},{8,12},{10,14},{12,8},{14,10},{16,20},{18,... | collective-permute-start | bytes 1769480 | tf_op jit(solution)/shard_map/up_across_2/ppermute | solution.py:140
  58.3 10.7 %collective-permute-start.18 = (bf16[192,1024]{1,0:T(8,128)(2,1)S(1)}, bf16[192,1024]{1,0:T(8,128)(2,1)S(1)}, u32[]{:S(2)}, u32[]{:S(2)}) collective-permute-start(bf16[192,1024]{1,0:T(8,128)(2,1)S(1)} %join.13.refs_4_.refs_1_), channel_id=1, source_target_pairs={{0,2},{2,0},{4,6},{6,4},{8,10},{10,8},{12,14},{14,12},{16,18},{18,... | collective-permute-start | bytes 1179656 | tf_op jit(solution)/shard_map/down_across_1/ppermute | solution.py:140
  59.7 9.3 %collective-permute-start.17 = (bf16[192,1024]{1,0:T(8,128)(2,1)S(1)}, bf16[192,1024]{1,0:T(8,128)(2,1)S(1)}, u32[]{:S(2)}, u32[]{:S(2)}) collective-permute-start(bf16[192,1024]{1,0:T(8,128)(2,1)S(1)} %join.13.refs_4_.refs_1_), channel_id=1, source_target_pairs={{0,4},{2,6},{4,0},{6,2},{8,12},{10,14},{12,8},{14,10},{16,20},{18,... | collective-permute-start | bytes 1179656 | tf_op jit(solution)/shard_map/down_across_2/ppermute | solution.py:140
  60.2 8.1 %collective-permute-start.16 = (bf16[192,512]{1,0:T(8,128)(2,1)S(1)}, bf16[192,512]{1,0:T(8,128)(2,1)S(1)}, u32[]{:S(2)}, u32[]{:S(2)}) collective-permute-start(bf16[192,512]{1,0:T(8,128)(2,1)S(1)} %join.14.refs_0_), channel_id=1, source_target_pairs={{0,16},{2,18},{4,20},{6,22},{8,24},{10,26},{12,28},{14,30},{16,0},... | collective-permute-start | bytes 589832 | tf_op jit(solution)/shard_map/down_plane_across_8/ppermute | solution.py:140
  70.3 11.0 %collective-permute-start.19 = (bf16[1024,768]{1,0:T(8,128)(2,1)S(1)}, bf16[1024,768]{1,0:T(8,128)(2,1)S(1)}, u32[]{:S(2)}, u32[]{:S(2)}) collective-permute-start(bf16[1024,768]{1,0:T(8,128)(2,1)S(1)} %branch.1.refs_2_), channel_id=1, source_target_pairs={{0,1},{1,0},{2,3},{3,2},{4,5},{5,4},{6,7},{7,6},{8,9},{9,8},{10,11... | collective-permute-start | bytes 4718600 | tf_op jit(solution)/shard_map/branch_other_core/ppermute | solution.py:149
  70.4 9.4 %collective-permute-start.21 = (bf16[96,1536]{1,0:T(8,128)(2,1)S(1)}, bf16[96,1536]{1,0:T(8,128)(2,1)S(1)}, u32[]{:S(2)}, u32[]{:S(2)}) collective-permute-start(bf16[96,1536]{1,0:T(8,128)(2,1)S(1)} %get-tuple-element.165), channel_id=1, source_target_pairs={{0,4},{2,6},{4,0},{6,2},{8,12},{10,14},{12,8},{14,10},{16,20},{18,... | collective-permute-start | bytes 884744 | tf_op jit(solution)/shard_map/up_corner_across_2/ppermute | solution.py:140
  71.5 9.9 %collective-permute-start.20 = (bf16[96,1536]{1,0:T(8,128)(2,1)S(1)}, bf16[96,1536]{1,0:T(8,128)(2,1)S(1)}, u32[]{:S(2)}, u32[]{:S(2)}) collective-permute-start(bf16[96,1536]{1,0:T(8,128)(2,1)S(1)} %get-tuple-element.162.refs_6_), channel_id=1, source_target_pairs={{0,2},{2,0},{4,6},{6,4},{8,10},{10,8},{12,14},{14,12},{16,18},{18,... | collective-permute-start | bytes 884744 | tf_op jit(solution)/shard_map/up_corner_across_1/ppermute | solution.py:140
  72.4 15.6 %collective-permute-start.24 = (bf16[384,512]{1,0:T(8,128)(2,1)S(1)}, bf16[384,512]{1,0:T(8,128)(2,1)S(1)}, u32[]{:S(2)}, u32[]{:S(2)}) collective-permute-start(bf16[384,512]{1,0:T(8,128)(2,1)S(1)} %join.15.refs_7_.refs_6_), channel_id=1, source_target_pairs={{0,8},{2,10},{4,12},{6,14},{8,0},{10,2},{12,4},{14,6},{16,24},{18,... | collective-permute-start | bytes 1179656 | tf_op jit(solution)/shard_map/down_plane_across_4/ppermute | solution.py:140
  74.1 13.9 %collective-permute-start.22 = (bf16[96,1024]{1,0:T(8,128)(2,1)S(1)}, bf16[96,1024]{1,0:T(8,128)(2,1)S(1)}, u32[]{:S(2)}, u32[]{:S(2)}) collective-permute-start(bf16[96,1024]{1,0:T(8,128)(2,1)S(1)} %get-tuple-element.167), channel_id=1, source_target_pairs={{0,2},{2,0},{4,6},{6,4},{8,10},{10,8},{12,14},{14,12},{16,18},{18,... | collective-permute-start | bytes 589832 | tf_op jit(solution)/shard_map/down_corner_across_1/ppermute | solution.py:140
  79.8 8.2 %collective-permute-start.23 = (bf16[96,1024]{1,0:T(8,128)(2,1)S(1)}, bf16[96,1024]{1,0:T(8,128)(2,1)S(1)}, u32[]{:S(2)}, u32[]{:S(2)}) collective-permute-start(bf16[96,1024]{1,0:T(8,128)(2,1)S(1)} %get-tuple-element.168), channel_id=1, source_target_pairs={{0,4},{2,6},{4,0},{6,2},{8,12},{10,14},{12,8},{14,10},{16,20},{18,... | collective-permute-start | bytes 589832 | tf_op jit(solution)/shard_map/down_corner_across_2/ppermute | solution.py:140
  88.8 1.2 collective-permute-start.25
  90.7 6.0 %collective-permute-start.28 = (f32[1,8,768]{2,1,0:T(8,128)S(1)}, f32[1,8,768]{2,1,0:T(8,128)S(1)}, u32[]{:S(2)}, u32[]{:S(2)}) collective-permute-start(f32[1,8,768]{2,1,0:T(8,128)S(1)} %bitcast.39), channel_id=1, source_target_pairs={{0,24},{2,26},{4,28},{6,30},{8,16},{10,18},{12,20},{14,22},{16,8},... | collective-permute-start | bytes 73736 | tf_op jit(solution)/shard_map/small_sums_across_12/ppermute | solution.py:140
  92.6 4.3 %collective-permute-start.27 = (f32[1,8,768]{2,1,0:T(8,128)S(1)}, f32[1,8,768]{2,1,0:T(8,128)S(1)}, u32[]{:S(2)}, u32[]{:S(2)}) collective-permute-start(f32[1,8,768]{2,1,0:T(8,128)S(1)} %bitcast.40), channel_id=1, source_target_pairs={{0,8},{2,10},{4,12},{6,14},{8,0},{10,2},{12,4},{14,6},{16,24},{18,... | collective-permute-start | bytes 73736 | tf_op jit(solution)/shard_map/small_sums_across_4/ppermute | solution.py:140
  93.3 4.7 %collective-permute-start.26 = (f32[1,8,768]{2,1,0:T(8,128)S(1)}, f32[1,8,768]{2,1,0:T(8,128)S(1)}, u32[]{:S(2)}, u32[]{:S(2)}) collective-permute-start(f32[1,8,768]{2,1,0:T(8,128)S(1)} %bitcast.41), channel_id=1, source_target_pairs={{0,16},{2,18},{4,20},{6,22},{8,24},{10,26},{12,28},{14,30},{16,0},... | collective-permute-start | bytes 73736 | tf_op jit(solution)/shard_map/small_sums_across_8/ppermute | solution.py:140
  98.0 5.6 %collective-permute-start.31 = (f32[4,8,768]{2,1,0:T(8,128)S(1)}, f32[4,8,768]{2,1,0:T(8,128)S(1)}, u32[]{:S(2)}, u32[]{:S(2)}) collective-permute-start(f32[4,8,768]{2,1,0:T(8,128)S(1)} %join.16.refs_7_.refs_0_), channel_id=1, source_target_pairs={{0,6},{2,4},{4,2},{6,0},{8,14},{10,12},{12,10},{14,8},{16,22},{18,... | collective-permute-start | bytes 294920 | tf_op jit(solution)/shard_map/small_sums_across_3/ppermute | solution.py:140
  99.8 4.6 %collective-permute-start.30 = (f32[4,8,768]{2,1,0:T(8,128)S(1)}, f32[4,8,768]{2,1,0:T(8,128)S(1)}, u32[]{:S(2)}, u32[]{:S(2)}) collective-permute-start(f32[4,8,768]{2,1,0:T(8,128)S(1)} %join.16.refs_7_.refs_0_), channel_id=1, source_target_pairs={{0,2},{2,0},{4,6},{6,4},{8,10},{10,8},{12,14},{14,12},{16,18},{18,... | collective-permute-start | bytes 294920 | tf_op jit(solution)/shard_map/small_sums_across_1/ppermute | solution.py:140
  100.4 4.6 %collective-permute-start.29 = (f32[4,8,768]{2,1,0:T(8,128)S(1)}, f32[4,8,768]{2,1,0:T(8,128)S(1)}, u32[]{:S(2)}, u32[]{:S(2)}) collective-permute-start(f32[4,8,768]{2,1,0:T(8,128)S(1)} %join.16.refs_7_.refs_0_), channel_id=1, source_target_pairs={{0,4},{2,6},{4,0},{6,2},{8,12},{10,14},{12,8},{14,10},{16,20},{18,... | collective-permute-start | bytes 294920 | tf_op jit(solution)/shard_map/small_sums_across_2/ppermute | solution.py:140
  109.2 5.5 %collective-permute-start.32 = (bf16[1024,768]{1,0:T(8,128)(2,1)S(1)}, bf16[1024,768]{1,0:T(8,128)(2,1)S(1)}, u32[]{:S(2)}, u32[]{:S(2)}) collective-permute-start(bf16[1024,768]{1,0:T(8,128)(2,1)S(1)} %get-tuple-element.177.refs_4_), channel_id=1, source_target_pairs={{0,1},{1,0},{2,3},{3,2},{4,5},{5,4},{6,7},{7,6},{8,9},{9,8},{10,11... | collective-permute-start | bytes 4718600 | tf_op jit(solution)/shard_map/second_gradient_other_core/ppermute | solution.py:149
  110.3 9.5 %collective-permute-start.38 = (bf16[96,1536]{1,0:T(8,128)(2,1)S(1)}, bf16[96,1536]{1,0:T(8,128)(2,1)S(1)}, u32[]{:S(2)}, u32[]{:S(2)}) collective-permute-start(bf16[96,1536]{1,0:T(8,128)(2,1)S(1)} %get-tuple-element.200), channel_id=1, source_target_pairs={{0,4},{2,6},{4,0},{6,2},{8,12},{10,14},{12,8},{14,10},{16,20},{18,... | collective-permute-start | bytes 884744 | tf_op jit(solution)/shard_map/up_gradient_across_2/ppermute | solution.py:140
  111.6 9.1 %collective-permute-start.37 = (bf16[96,1536]{1,0:T(8,128)(2,1)S(1)}, bf16[96,1536]{1,0:T(8,128)(2,1)S(1)}, u32[]{:S(2)}, u32[]{:S(2)}) collective-permute-start(bf16[96,1536]{1,0:T(8,128)(2,1)S(1)} %get-tuple-element.196.refs_2_), channel_id=1, source_target_pairs={{0,2},{2,0},{4,6},{6,4},{8,10},{10,8},{12,14},{14,12},{16,18},{18,... | collective-permute-start | bytes 884744 | tf_op jit(solution)/shard_map/up_gradient_across_1/ppermute | solution.py:140
  120.9 18.8 %collective-permute-start.39 = (bf16[192,1536]{1,0:T(8,128)(2,1)S(1)}, bf16[192,1536]{1,0:T(8,128)(2,1)S(1)}, u32[]{:S(2)}, u32[]{:S(2)}) collective-permute-start(bf16[192,1536]{1,0:T(8,128)(2,1)S(1)} %get-tuple-element.201), channel_id=1, source_target_pairs={{0,4},{2,6},{4,0},{6,2},{8,12},{10,14},{12,8},{14,10},{16,20},{18,... | collective-permute-start | bytes 1769480 | tf_op jit(solution)/shard_map/up_gradient_across_2/ppermute | solution.py:140
  121.8 19.3 %collective-permute-start.40 = (bf16[192,1536]{1,0:T(8,128)(2,1)S(1)}, bf16[192,1536]{1,0:T(8,128)(2,1)S(1)}, u32[]{:S(2)}, u32[]{:S(2)}) collective-permute-start(bf16[192,1536]{1,0:T(8,128)(2,1)S(1)} %get-tuple-element.202), channel_id=1, source_target_pairs={{0,2},{2,0},{4,6},{6,4},{8,10},{10,8},{12,14},{14,12},{16,18},{18,... | collective-permute-start | bytes 1769480 | tf_op jit(solution)/shard_map/up_gradient_across_1/ppermute | solution.py:140
  132.4 11.9 %collective-permute-start.33 = (bf16[96,1152]{1,0:T(8,128)(2,1)S(1)}, bf16[96,1152]{1,0:T(8,128)(2,1)S(1)}, u32[]{:S(2)}, u32[]{:S(2)}) collective-permute-start(bf16[96,1152]{1,0:T(8,128)(2,1)S(1)} %get-tuple-element.186), channel_id=1, source_target_pairs={{0,2},{2,0},{4,6},{6,4},{8,10},{10,8},{12,14},{14,12},{16,18},{18,... | collective-permute-start | bytes 663560 | tf_op jit(solution)/shard_map/early_gradient_across_1/ppermute | solution.py:140
  133.0 11.3 %collective-permute-start.34 = (bf16[96,1152]{1,0:T(8,128)(2,1)S(1)}, bf16[96,1152]{1,0:T(8,128)(2,1)S(1)}, u32[]{:S(2)}, u32[]{:S(2)}) collective-permute-start(bf16[96,1152]{1,0:T(8,128)(2,1)S(1)} %get-tuple-element.187), channel_id=1, source_target_pairs={{0,4},{2,6},{4,0},{6,2},{8,12},{10,14},{12,8},{14,10},{16,20},{18,... | collective-permute-start | bytes 663560 | tf_op jit(solution)/shard_map/early_gradient_across_2/ppermute | solution.py:140
  138.7 4.7 %collective-permute-start.35 = (bf16[96,512]{1,0:T(8,128)(2,1)S(1)}, bf16[96,512]{1,0:T(8,128)(2,1)S(1)}, u32[]{:S(2)}, u32[]{:S(2)}) collective-permute-start(bf16[96,512]{1,0:T(8,128)(2,1)S(1)} %get-tuple-element.192), channel_id=1, source_target_pairs={{0,2},{2,0},{4,6},{6,4},{8,10},{10,8},{12,14},{14,12},{16,18},{18,... | collective-permute-start | bytes 294920 | tf_op jit(solution)/shard_map/late_gradient_across_1/ppermute | solution.py:140
  139.7 4.6 %collective-permute-start.36 = (bf16[96,512]{1,0:T(8,128)(2,1)S(1)}, bf16[96,512]{1,0:T(8,128)(2,1)S(1)}, u32[]{:S(2)}, u32[]{:S(2)}) collective-permute-start(bf16[96,512]{1,0:T(8,128)(2,1)S(1)} %get-tuple-element.193), channel_id=1, source_target_pairs={{0,4},{2,6},{4,0},{6,2},{8,12},{10,14},{12,8},{14,10},{16,20},{18,... | collective-permute-start | bytes 294920 | tf_op jit(solution)/shard_map/late_gradient_across_2/ppermute | solution.py:140
  141.3 6.8 %collective-permute-start.43 = (bf16[96,1536]{1,0:T(8,128)(2,1)S(1)}, bf16[96,1536]{1,0:T(8,128)(2,1)S(1)}, u32[]{:S(2)}, u32[]{:S(2)}) collective-permute-start(bf16[96,1536]{1,0:T(8,128)(2,1)S(1)} %get-tuple-element.204.refs_8_), channel_id=1, source_target_pairs={{0,8},{2,10},{4,12},{6,14},{8,0},{10,2},{12,4},{14,6},{16,24},{18,... | collective-permute-start | bytes 884744 | tf_op jit(solution)/shard_map/up_gradient_across_4/ppermute | solution.py:140
  144.5 9.8 %collective-permute-start.41 = (bf16[192,1152]{1,0:T(8,128)(2,1)S(1)}, bf16[192,1152]{1,0:T(8,128)(2,1)S(1)}, u32[]{:S(2)}, u32[]{:S(2)}) collective-permute-start(bf16[192,1152]{1,0:T(8,128)(2,1)S(1)} %get-tuple-element.205.refs_2_.refs_6_), channel_id=1, source_target_pairs={{0,4},{2,6},{4,0},{6,2},{8,12},{10,14},{12,8},{14,10},{16,20},{18,... | collective-permute-start | bytes 1327112 | tf_op jit(solution)/shard_map/early_gradient_across_2/ppermute | solution.py:140
  146.0 8.9 %collective-permute-start.42 = (bf16[192,1152]{1,0:T(8,128)(2,1)S(1)}, bf16[192,1152]{1,0:T(8,128)(2,1)S(1)}, u32[]{:S(2)}, u32[]{:S(2)}) collective-permute-start(bf16[192,1152]{1,0:T(8,128)(2,1)S(1)} %get-tuple-element.206.refs_3_.refs_7_), channel_id=1, source_target_pairs={{0,2},{2,0},{4,6},{6,4},{8,10},{10,8},{12,14},{14,12},{16,18},{18,... | collective-permute-start | bytes 1327112 | tf_op jit(solution)/shard_map/early_gradient_across_1/ppermute | solution.py:140
  148.1 6.1 %collective-permute-start.44 = (bf16[48,1536]{1,0:T(8,128)(2,1)S(1)}, bf16[48,1536]{1,0:T(8,128)(2,1)S(1)}, u32[]{:S(2)}, u32[]{:S(2)}) collective-permute-start(bf16[48,1536]{1,0:T(8,128)(2,1)S(1)} %get-tuple-element.211), channel_id=1, source_target_pairs={{0,16},{2,18},{4,20},{6,22},{8,24},{10,26},{12,28},{14,30},{16,0},... | collective-permute-start | bytes 442376 | tf_op jit(solution)/shard_map/up_gradient_across_8/ppermute | solution.py:140
  155.1 14.7 %collective-permute-start.52 = (bf16[1024,768]{1,0:T(8,128)(2,1)S(1)}, bf16[1024,768]{1,0:T(8,128)(2,1)S(1)}, u32[]{:S(2)}, u32[]{:S(2)}) collective-permute-start(bf16[1024,768]{1,0:T(8,128)(2,1)S(1)} %get-tuple-element.224.refs_1_), channel_id=1, source_target_pairs={{0,1},{1,0},{2,3},{3,2},{4,5},{5,4},{6,7},{7,6},{8,9},{9,8},{10,11... | collective-permute-start | bytes 4718600 | tf_op jit(solution)/shard_map/first_gradient_other_core/ppermute | solution.py:149
  155.2 7.8 %collective-permute-start.45 = (bf16[96,1152]{1,0:T(8,128)(2,1)S(1)}, bf16[96,1152]{1,0:T(8,128)(2,1)S(1)}, u32[]{:S(2)}, u32[]{:S(2)}) collective-permute-start(bf16[96,1152]{1,0:T(8,128)(2,1)S(1)} %get-tuple-element.214), channel_id=1, source_target_pairs={{0,8},{2,10},{4,12},{6,14},{8,0},{10,2},{12,4},{14,6},{16,24},{18,... | collective-permute-start | bytes 663560 | tf_op jit(solution)/shard_map/early_gradient_across_4/ppermute | solution.py:140
  157.0 7.0 %collective-permute-start.47 = (bf16[192,512]{1,0:T(8,128)(2,1)S(1)}, bf16[192,512]{1,0:T(8,128)(2,1)S(1)}, u32[]{:S(2)}, u32[]{:S(2)}) collective-permute-start(bf16[192,512]{1,0:T(8,128)(2,1)S(1)} %get-tuple-element.208.refs_4_.refs_8_), channel_id=1, source_target_pairs={{0,4},{2,6},{4,0},{6,2},{8,12},{10,14},{12,8},{14,10},{16,20},{18,... | collective-permute-start | bytes 589832 | tf_op jit(solution)/shard_map/late_gradient_across_2/ppermute | solution.py:140
  157.7 6.7 %collective-permute-start.48 = (bf16[192,512]{1,0:T(8,128)(2,1)S(1)}, bf16[192,512]{1,0:T(8,128)(2,1)S(1)}, u32[]{:S(2)}, u32[]{:S(2)}) collective-permute-start(bf16[192,512]{1,0:T(8,128)(2,1)S(1)} %get-tuple-element.209.refs_5_.refs_9_), channel_id=1, source_target_pairs={{0,2},{2,0},{4,6},{6,4},{8,10},{10,8},{12,14},{14,12},{16,18},{18,... | collective-permute-start | bytes 589832 | tf_op jit(solution)/shard_map/late_gradient_across_1/ppermute | solution.py:140
  164.5 10.8 %collective-permute-start.49 = (bf16[48,512]{1,0:T(8,128)(2,1)S(1)}, bf16[48,512]{1,0:T(8,128)(2,1)S(1)}, u32[]{:S(2)}, u32[]{:S(2)}) collective-permute-start(bf16[48,512]{1,0:T(8,128)(2,1)S(1)} %get-tuple-element.219), channel_id=1, source_target_pairs={{0,16},{2,18},{4,20},{6,22},{8,24},{10,26},{12,28},{14,30},{16,0},... | collective-permute-start | bytes 147464 | tf_op jit(solution)/shard_map/late_gradient_across_8/ppermute | solution.py:140
  166.2 9.0 %collective-permute-start.50 = (bf16[48,512]{1,0:T(8,128)(2,1)S(1)}, bf16[48,512]{1,0:T(8,128)(2,1)S(1)}, u32[]{:S(2)}, u32[]{:S(2)}) collective-permute-start(bf16[48,512]{1,0:T(8,128)(2,1)S(1)} %get-tuple-element.220), channel_id=1, source_target_pairs={{0,8},{2,10},{4,12},{6,14},{8,0},{10,2},{12,4},{14,6},{16,24},{18,... | collective-permute-start | bytes 147464 | tf_op jit(solution)/shard_map/late_gradient_across_4/ppermute | solution.py:140
  167.0 8.2 %collective-permute-start.51 = (bf16[48,512]{1,0:T(8,128)(2,1)S(1)}, bf16[48,512]{1,0:T(8,128)(2,1)S(1)}, u32[]{:S(2)}, u32[]{:S(2)}) collective-permute-start(bf16[48,512]{1,0:T(8,128)(2,1)S(1)} %get-tuple-element.221), channel_id=1, source_target_pairs={{0,24},{2,26},{4,28},{6,30},{8,16},{10,18},{12,20},{14,22},{16,8},... | collective-permute-start | bytes 147464 | tf_op jit(solution)/shard_map/late_gradient_across_12/ppermute | solution.py:140
  168.9 7.7 %collective-permute-start.46 = (bf16[48,1152]{1,0:T(8,128)(2,1)S(1)}, bf16[48,1152]{1,0:T(8,128)(2,1)S(1)}, u32[]{:S(2)}, u32[]{:S(2)}) collective-permute-start(bf16[48,1152]{1,0:T(8,128)(2,1)S(1)} %get-tuple-element.216), channel_id=1, source_target_pairs={{0,16},{2,18},{4,20},{6,22},{8,24},{10,26},{12,28},{14,30},{16,0},... | collective-permute-start | bytes 331784 | tf_op jit(solution)/shard_map/early_gradient_across_8/ppermute | solution.py:140
  169.8 22.6 %copy-start.13 = (f32[3,48,384]{2,1,0:T(8,128)S(1)}, f32[3,48,384]{2,1,0:T(8,128)}, u32[]{:S(2)}) copy-start(f32[3,48,384]{2,1,0:T(8,128)} %get-tuple-element.236.refs_18_) | copy-start | bytes 663556
  169.8 22.6 %copy-start.14 = (f32[3,48,384]{2,1,0:T(8,128)S(1)}, f32[3,48,384]{2,1,0:T(8,128)}, u32[]{:S(2)}) copy-start(f32[3,48,384]{2,1,0:T(8,128)} %get-tuple-element.240.refs_25_) | copy-start | bytes 663556
  169.8 22.6 %copy-start.17 = (f32[48,384]{1,0:T(8,128)S(1)}, f32[48,384]{1,0:T(8,128)}, u32[]{:S(2)}) copy-start(f32[48,384]{1,0:T(8,128)} %get-tuple-element.241.refs_26_) | copy-start | bytes 221188
  169.8 22.6 %copy-start.26 = (f32[48,3]{0,1:T(4,128)S(1)}, f32[48,3]{0,1:T(4,128)}, u32[]{:S(2)}) copy-start(f32[48,3]{0,1:T(4,128)} %param.49) | copy-start | bytes 1732
  178.0 1.2 collective-permute-start.53
  179.3 5.5 %collective-permute-start.56 = (f32[1,24,128]{2,1,0:T(8,128)S(1)}, f32[1,24,128]{2,1,0:T(8,128)S(1)}, u32[]{:S(2)}, u32[]{:S(2)}) collective-permute-start(f32[1,24,128]{2,1,0:T(8,128)S(1)} %bitcast.55), channel_id=1, source_target_pairs={{0,24},{2,26},{4,28},{6,30},{8,16},{10,18},{12,20},{14,22},{16,8},... | collective-permute-start | bytes 36872 | tf_op jit(solution)/shard_map/squares_across_12/ppermute | solution.py:140
  181.2 3.8 %collective-permute-start.55 = (f32[1,24,128]{2,1,0:T(8,128)S(1)}, f32[1,24,128]{2,1,0:T(8,128)S(1)}, u32[]{:S(2)}, u32[]{:S(2)}) collective-permute-start(f32[1,24,128]{2,1,0:T(8,128)S(1)} %bitcast.56), channel_id=1, source_target_pairs={{0,8},{2,10},{4,12},{6,14},{8,0},{10,2},{12,4},{14,6},{16,24},{18,... | collective-permute-start | bytes 36872 | tf_op jit(solution)/shard_map/squares_across_4/ppermute | solution.py:140
  181.2 4.6 %collective-permute-start.54 = (f32[1,24,128]{2,1,0:T(8,128)S(1)}, f32[1,24,128]{2,1,0:T(8,128)S(1)}, u32[]{:S(2)}, u32[]{:S(2)}) collective-permute-start(f32[1,24,128]{2,1,0:T(8,128)S(1)} %bitcast.57), channel_id=1, source_target_pairs={{0,16},{2,18},{4,20},{6,22},{8,24},{10,26},{12,28},{14,30},{16,0},... | collective-permute-start | bytes 36872 | tf_op jit(solution)/shard_map/squares_across_8/ppermute | solution.py:140
  185.8 5.0 %collective-permute-start.59 = (f32[4,24,128]{2,1,0:T(8,128)S(1)}, f32[4,24,128]{2,1,0:T(8,128)S(1)}, u32[]{:S(2)}, u32[]{:S(2)}) collective-permute-start(f32[4,24,128]{2,1,0:T(8,128)S(1)} %join.17.refs_3_), channel_id=1, source_target_pairs={{0,6},{2,4},{4,2},{6,0},{8,14},{10,12},{12,10},{14,8},{16,22},{18,... | collective-permute-start | bytes 147464 | tf_op jit(solution)/shard_map/squares_across_3/ppermute | solution.py:140
  187.4 4.1 %collective-permute-start.58 = (f32[4,24,128]{2,1,0:T(8,128)S(1)}, f32[4,24,128]{2,1,0:T(8,128)S(1)}, u32[]{:S(2)}, u32[]{:S(2)}) collective-permute-start(f32[4,24,128]{2,1,0:T(8,128)S(1)} %join.17.refs_3_), channel_id=1, source_target_pairs={{0,2},{2,0},{4,6},{6,4},{8,10},{10,8},{12,14},{14,12},{16,18},{18,... | collective-permute-start | bytes 147464 | tf_op jit(solution)/shard_map/squares_across_1/ppermute | solution.py:140
  188.2 4.1 %collective-permute-start.57 = (f32[4,24,128]{2,1,0:T(8,128)S(1)}, f32[4,24,128]{2,1,0:T(8,128)S(1)}, u32[]{:S(2)}, u32[]{:S(2)}) collective-permute-start(f32[4,24,128]{2,1,0:T(8,128)S(1)} %join.17.refs_3_), channel_id=1, source_target_pairs={{0,4},{2,6},{4,0},{6,2},{8,12},{10,14},{12,8},{14,10},{16,20},{18,... | collective-permute-start | bytes 147464 | tf_op jit(solution)/shard_map/squares_across_2/ppermute | solution.py:140
  (27 other events, 327.6 us)
